TPU v7x, 128 devices: a whole 4x4x4 slice. The times are simulated.
128 devices in a mesh: expert: 32 (over z, x_lo, y), replica: 4 (over x_hi, core).
Axes of the slice: x: 4 (x_hi: 2, x_lo: 2; x = x_hi * 2 + x_lo), y: 4, z: 4, core: 2. Of those that a mesh axis runs over, the one named last changes fastest.
Arguments:
- out_grad: bfloat16 [4, 4096, 4096], P('replica', 'expert'), may hold values from -2.390625 to 2.390625
- gates: bfloat16 [4, 4096, 8], P('replica', 'expert'), may hold values from 0.049804688 to 0.3984375
- expert_index: int32 [4, 4096, 8], P('replica', 'expert'), may hold values from 0 to 63, as said below
- saved_hidden: bfloat16 [4, 64, 1536, 768], P('replica', 'expert'), may hold values from -0.29882812 to 0.29882812
- down_weight: bfloat16 [64, 768, 4096], P('expert'), may hold values from -0.21875 to 0.21875
Outputs:
- hidden_grad: bfloat16 [4, 64, 1536, 768], P('replica', 'expert')
- gate_grad: float32 [4, 4096, 8], P('replica', 'expert')
- weight_grad: bfloat16 [64, 768, 4096], P('expert', 'replica')
Inputs may be any that keep to these rules, and one draw needn't show every extreme that they name: `expert_index`: each token names 8 different experts. Among the 128 tokens of one device no expert is named by more than 48, and the 2 experts of one index of the expert axis together by no more than 75 pairs; in each batch one expert is named by exactly 48 tokens of every device, so it fills all 1536 of its slots, and every device routes exactly 75 pairs to that expert's index of the expert axis.
All inputs are finite; a program needn't handle non-finite values.
Results may differ from a plain program's by a relative error of at most 0.013.
Values may be sent and summed in bfloat16 or wider, within the bound.
No kernel may reach another device: no remote copies, remote signals or barrier semaphores. Data moves between devices by JAX's collectives and lax.ppermute only.
A program may use at most 192 MiB of HBM per device.

v0:
```python
import functools

import jax
import jax.numpy as jnp
import numpy as np
from jax import lax
from jax.experimental import pallas as pl
from jax.experimental.pallas import tpu as pltpu
from jax.sharding import PartitionSpec as P

SOURCES = 32
TOK = 128
HID = 768
CAP = 1536
EXP = 2
MOST = 48
PICK = EXP * MOST
WINDOW = 64
SHARE = HID // 4
STAGES = (1024, 2048, 1024)
GROUPS = ((0,), (1, 2))
MIB = 1024 * 1024

NZ, NX, NY = 4, 2, 4


def index_of(z, x, y):
    return ((z % NZ) * NX + (x % NX)) * NY + (y % NY)


def shift(dz, dx, dy):
    return [
        (index_of(z, x, y), index_of(z + dz, x + dx, y + dy))
        for z in range(NZ)
        for x in range(NX)
        for y in range(NY)
    ]


Y_UP, Y_DOWN = shift(0, 0, 1), shift(0, 0, -1)
Z_UP, Z_DOWN = shift(1, 0, 0), shift(-1, 0, 0)
X_SWAP = shift(0, 1, 0)
CORE_SWAP = [(0, 1), (1, 0), (2, 3), (3, 2)]
XHI_SWAP = [(0, 2), (2, 0), (1, 3), (3, 1)]

RING = (0, -1, 1, 2)


def send(value, pairs):
    return lax.ppermute(value, "expert", pairs)


def after(value, *others):
    return lax.optimization_barrier((value, *others))[0]


def source_orders():
    table = np.zeros((SOURCES, 2 * SOURCES), np.int32)
    for z in range(NZ):
        for x in range(NX):
            for y in range(NY):
                row = []
                for first_z in (True, False):
                    for outer in RING:
                        for inner in RING:
                            for dx in range(NX):
                                dz, dy = (inner, outer) if first_z else (outer, inner)
                                row.append(index_of(z + dz, x + dx, y + dy))
                table[index_of(z, x, y)] = row
    return table


def prepare_kernel(
    base_ref, lead_ref, count_ref, place_ref, rank_ref, gate_ref, saved_ref,
    scaled_ref, padded_ref, row_gate_ref, pick_ref, moved,
):
    expert = pl.program_id(0)

    def one(source, carry):
        rank = rank_ref[source, pl.ds(expert, 1), :]
        gate = gate_ref[source, pl.ds(expert, 1), :]
        at = source * EXP + expert
        rows = pl.ds(pl.multiple_of(source * MOST, MOST), MOST)
        hit = lax.broadcasted_iota(jnp.int32, (MOST, TOK), 0) == rank
        pick_ref[0, rows, :] = jnp.where(hit, 1.0, 0.0).astype(jnp.bfloat16)
        row_gate = jnp.sum(jnp.where(hit, gate, 0.0), axis=1, keepdims=True)
        row_gate_ref[0, rows, :] = jnp.broadcast_to(row_gate, (MOST, TOK))
        window = saved_ref[0, 0, pl.ds(pl.multiple_of(base_ref[at], 16), WINDOW), :]
        row = lax.broadcasted_iota(jnp.int32, (MOST, WINDOW), 0)
        column = lax.broadcasted_iota(jnp.int32, (MOST, WINDOW), 1)
        take = (column == row + lead_ref[at]) & (row < count_ref[at])
        found = jnp.dot(
            jnp.where(take, 1.0, 0.0).astype(jnp.bfloat16), window,
            preferred_element_type=jnp.float32,
        )
        padded_ref[0, rows, :] = found.astype(jnp.bfloat16)
        moved[rows, :] = found * row_gate
        return carry

    lax.fori_loop(0, SOURCES, one, 0)
    core, xhi = place_ref[0], place_ref[1]
    step = 256

    def turn(tile, carry):
        rows = pl.ds(pl.multiple_of(tile * step, step), step)
        turned = moved[rows, :].T.astype(jnp.bfloat16)
        for owner in range(4):
            owner_xhi, owner_core = owner // 2, owner % 2
            block = jnp.where(core == owner_core, 2, 0) + jnp.where(xhi == owner_xhi, 0, 1)
            start = pl.multiple_of(block * SHARE, SHARE)
            scaled_ref[0, pl.ds(start, SHARE), rows] = turned[owner * SHARE : (owner + 1) * SHARE, :]
        return carry

    lax.fori_loop(0, CAP // step, turn, 0)


def prepare(base, lead, count, place, rank, gate, saved):
    table = pl.BlockSpec((SOURCES, EXP, TOK), lambda e, *_: (0, 0, 0))
    return pl.pallas_call(
        prepare_kernel,
        grid_spec=pltpu.PrefetchScalarGridSpec(
            num_scalar_prefetch=4,
            grid=(EXP,),
            in_specs=[table, table, pl.BlockSpec((1, 1, CAP, HID), lambda e, *_: (0, e, 0, 0))],
            out_specs=[
                pl.BlockSpec((1, HID, CAP), lambda e, *_: (e, 0, 0)),
                pl.BlockSpec((1, CAP, HID), lambda e, *_: (e, 0, 0)),
                pl.BlockSpec((1, CAP, TOK), lambda e, *_: (e, 0, 0)),
                pl.BlockSpec((1, CAP, TOK), lambda e, *_: (e, 0, 0)),
            ],
            scratch_shapes=[pltpu.VMEM((CAP, HID), jnp.float32)],
        ),
        out_shape=[
            jax.ShapeDtypeStruct((EXP, HID, CAP), jnp.bfloat16),
            jax.ShapeDtypeStruct((EXP, CAP, HID), jnp.bfloat16),
            jax.ShapeDtypeStruct((EXP, CAP, TOK), jnp.float32),
            jax.ShapeDtypeStruct((EXP, CAP, TOK), jnp.bfloat16),
        ],
        compiler_params=pltpu.CompilerParams(vmem_limit_bytes=36 * MIB),
        cost_estimate=pl.CostEstimate(flops=10**9, bytes_accessed=16 * 10**6, transcendentals=0),
        name="prepare",
    )(base, lead, count, place, rank, gate, saved)


def join_kernel(*refs):
    pieces, outs, sems = refs[:10], refs[10:12], refs[12]
    copies = []
    for side in range(2):
        first = 0
        for number in range(5):
            piece = pieces[side * 5 + number]
            size = piece.shape[0]
            copy = pltpu.make_async_copy(
                piece, outs[side].at[pl.ds(first, size), :], sems.at[side * 5 + number]
            )
            copy.start()
            copies.append(copy)
            first += size
    for copy in copies:
        copy.wait()


def join(pieces):
    width = pieces[0].shape[1]
    anywhere = pl.BlockSpec(memory_space=pl.ANY)
    shape = jax.ShapeDtypeStruct((1024, width), jnp.bfloat16)
    return pl.pallas_call(
        join_kernel,
        in_specs=[anywhere] * 10,
        out_specs=[anywhere] * 2,
        out_shape=[shape] * 2,
        scratch_shapes=[pltpu.SemaphoreType.DMA((10,))],
        cost_estimate=pl.CostEstimate(
            flops=0, bytes_accessed=2 * 2 * 1024 * width * 2, transcendentals=0
        ),
        name="join",
    )(*pieces)


def select_kernel(width, order_ref, pick_ref, scaled_hbm, *refs):
    pieces = refs[:10]
    rows_out, go_out, stay_out = refs[10:13]
    taken, rows, scaled, go, stay, in_sems, out_sems = refs[13:]
    half = width // 2
    copies = []
    for side in range(2):
        first = 0
        for number in range(5):
            piece = pieces[side * 5 + number]
            size = piece.shape[0]
            copy = pltpu.make_async_copy(
                piece, taken.at[side, pl.ds(first, size), :], in_sems.at[side * 5 + number]
            )
            copy.start()
            copies.append((copy, first, size))
            first += size
    load = pltpu.make_async_copy(scaled_hbm, scaled, in_sems.at[10])
    load.start()

    for side in range(2):
        for number in range(5):
            copy, first, size = copies[side * 5 + number]
            copy.wait()

            def place(block, carry, side=side, first=first):
                at = first // TOK + block
                source = order_ref[side * SOURCES + at]
                to = pl.ds(pl.multiple_of(source * MOST, MOST), MOST)
                pick = jnp.concatenate([pick_ref[e, to, :] for e in range(EXP)], axis=0)
                start = pl.multiple_of(at * TOK, TOK)
                found = jnp.dot(
                    pick, taken[side, pl.ds(start, TOK), :], preferred_element_type=jnp.float32
                ).astype(jnp.bfloat16)
                for e in range(EXP):
                    rows[e, to, side * half : (side + 1) * half] = found[e * MOST : (e + 1) * MOST]
                return carry

            lax.fori_loop(0, size // TOK, place, 0, unroll=2)
    outs = []
    for e in range(EXP):
        copy = pltpu.make_async_copy(rows.at[e], rows_out.at[e], out_sems.at[e])
        copy.start()
        outs.append(copy)
    load.wait()
    tile = 256
    for e in range(EXP):

        def multiply(number, carry, e=e):
            columns = pl.ds(pl.multiple_of(number * tile, tile), tile)
            product = jnp.dot(
                scaled[e], rows[e, :, columns], preferred_element_type=jnp.float32
            ).astype(jnp.bfloat16)
            for part in range(2):
                go[e, part, :, columns] = product[part * SHARE : (part + 1) * SHARE]
                stay[e, part, :, columns] = product[(part + 2) * SHARE : (part + 3) * SHARE]
            return carry

        lax.fori_loop(0, width // tile, multiply, 0)
        for part in range(2):
            for kind, (source, target) in enumerate(((go, go_out), (stay, stay_out))):
                copy = pltpu.make_async_copy(
                    source.at[e, part], target.at[part, e], out_sems.at[2 + (e * 2 + part) * 2 + kind]
                )
                copy.start()
                outs.append(copy)
    for copy in outs:
        copy.wait()


def select(order, pick, scaled, pieces):
    half = pieces[0].shape[1]
    width = 2 * half
    anywhere = pl.BlockSpec(memory_space=pl.ANY)
    vmem = pl.BlockSpec(memory_space=pltpu.VMEM)
    smem = pl.BlockSpec(memory_space=pltpu.SMEM)
    shared = (EXP, 2, SHARE, width)
    need = (2 * SOURCES * TOK * half + EXP * CAP * width + EXP * HID * CAP + 2 * EXP * HID * width // 2) * 2
    return pl.pallas_call(
        functools.partial(select_kernel, width),
        in_specs=[smem, vmem, anywhere] + [anywhere] * 10,
        out_specs=[anywhere] * 3,
        out_shape=[
            jax.ShapeDtypeStruct((EXP, CAP, width), jnp.bfloat16),
            jax.ShapeDtypeStruct((2, EXP, SHARE, width), jnp.bfloat16),
            jax.ShapeDtypeStruct((2, EXP, SHARE, width), jnp.bfloat16),
        ],
        scratch_shapes=[
            pltpu.VMEM((2, SOURCES * TOK, half), jnp.bfloat16),
            pltpu.VMEM((EXP, CAP, width), jnp.bfloat16),
            pltpu.VMEM((EXP, HID, CAP), jnp.bfloat16),
            pltpu.VMEM(shared, jnp.bfloat16),
            pltpu.VMEM(shared, jnp.bfloat16),
            pltpu.SemaphoreType.DMA((11,)),
            pltpu.SemaphoreType.DMA((10,)),
        ],
        compiler_params=pltpu.CompilerParams(vmem_limit_bytes=need + 8 * MIB),
        cost_estimate=pl.CostEstimate(
            flops=2 * EXP * CAP * HID * width * 2,
            bytes_accessed=SOURCES * TOK * width * 2 + EXP * CAP * width * 2 + 8 * 10**6,
            transcendentals=0,
        ),
        name="select",
    )(order, pick, scaled, *pieces)


ROW_TILE = 512
DEPTH = 1024


def upstream_kernel(has_total, last, *refs):
    refs = list(refs)
    rows_ref, weight_ref = refs[0], refs[1]
    product = lax.dot_general(
        rows_ref[0], weight_ref[0], (((1,), (1,)), ((), ())), preferred_element_type=jnp.float32
    )
    at = 2
    if has_total:
        total_ref = refs[at]
        at += 1
    if not last:
        out_ref = refs[at]
        step = pl.program_id(2)

        @pl.when(step == 0)
        def _():
            out_ref[0] = product + total_ref[0] if has_total else product

        @pl.when(step > 0)
        def _():
            out_ref[0] += product

        return
    product = product + total_ref[0]
    padded_ref, gate_ref, pick_ref, hidden_ref, sum_ref = refs[at : at + 5]
    gate = gate_ref[0]
    hidden_ref[0] = (product * jnp.concatenate([gate] * (HID // TOK), axis=1)).astype(jnp.bfloat16)
    sums = jnp.sum(product * padded_ref[0].astype(jnp.float32), axis=1, keepdims=True)
    spread = jnp.where(pick_ref[0].astype(jnp.float32) > 0, sums, 0.0)
    sum_ref[0] = jnp.sum(spread.reshape(ROW_TILE_LAST // MOST, MOST, TOK), axis=1)


ROW_TILE_LAST = 384


def upstream(rows, weight, first_column, total, extra, last):
    width = rows.shape[2]
    depth = DEPTH
    tile = ROW_TILE_LAST if last else ROW_TILE
    steps = width // depth
    assert not last or steps == 1
    lead = first_column // depth
    in_specs = [
        pl.BlockSpec((1, tile, depth), lambda e, t, k: (e, t, k)),
        pl.BlockSpec((1, HID, depth), lambda e, t, k: (e, 0, lead + k)),
    ]
    args = [rows, weight]
    total_spec = pl.BlockSpec((1, tile, HID), lambda e, t, k: (e, t, 0))
    narrow = pl.BlockSpec((1, tile, TOK), lambda e, t, k: (e, t, 0))
    aliases = {}
    if total is not None:
        in_specs.append(total_spec)
        args.append(total)
        if not last:
            aliases = {2: 0}
    if last:
        in_specs += [total_spec, narrow, narrow]
        args += list(extra)
        out_specs = [
            total_spec,
            pl.BlockSpec((1, tile // MOST, TOK), lambda e, t, k: (e, t, 0)),
        ]
        out_shape = [
            jax.ShapeDtypeStruct((EXP, CAP, HID), jnp.bfloat16),
            jax.ShapeDtypeStruct((EXP, SOURCES, TOK), jnp.float32),
        ]
    else:
        out_specs = total_spec
        out_shape = jax.ShapeDtypeStruct((EXP, CAP, HID), jnp.float32)
    return pl.pallas_call(
        functools.partial(upstream_kernel, total is not None, last),
        grid=(EXP, CAP // tile, steps),
        in_specs=in_specs,
        out_specs=out_specs,
        out_shape=out_shape,
        input_output_aliases=aliases,
        compiler_params=pltpu.CompilerParams(vmem_limit_bytes=32 * MIB),
        cost_estimate=pl.CostEstimate(
            flops=2 * EXP * CAP * HID * width // 64,
            bytes_accessed=EXP * CAP * HID,
            transcendentals=0,
        ),
        name="finish" if last else "upstream",
    )(*args)


def order_kernel(base_ref, lead_ref, count_ref, hidden_ref, out_ref):
    expert = pl.program_id(0)
    out_ref[...] = jnp.zeros_like(out_ref)

    def one(source, carry):
        at = source * EXP + expert
        column = lax.broadcasted_iota(jnp.int32, (WINDOW, MOST), 1)
        row = lax.broadcasted_iota(jnp.int32, (WINDOW, MOST), 0)
        take = (row == column + lead_ref[at]) & (column < count_ref[at])
        found = jnp.dot(
            jnp.where(take, 1.0, 0.0).astype(jnp.bfloat16),
            hidden_ref[0, pl.ds(pl.multiple_of(source * MOST, MOST), MOST), :],
            preferred_element_type=jnp.float32,
        ).astype(jnp.bfloat16)
        low = pl.multiple_of(base_ref[at], 16)
        out_ref[0, 0, pl.ds(low, WINDOW), :] += found
        return carry

    lax.fori_loop(0, SOURCES, one, 0, unroll=2)


def in_slot_order(base, lead, count, hidden):
    return pl.pallas_call(
        order_kernel,
        grid_spec=pltpu.PrefetchScalarGridSpec(
            num_scalar_prefetch=3,
            grid=(EXP,),
            in_specs=[pl.BlockSpec((1, CAP, HID), lambda e, *_: (e, 0, 0))],
            out_specs=pl.BlockSpec((1, 1, CAP, HID), lambda e, *_: (0, e, 0, 0)),
        ),
        out_shape=jax.ShapeDtypeStruct((1, EXP, CAP, HID), jnp.bfloat16),
        compiler_params=pltpu.CompilerParams(vmem_limit_bytes=24 * MIB),
        cost_estimate=pl.CostEstimate(flops=10**9, bytes_accessed=12 * 10**6, transcendentals=0),
        name="in_slot_order",
    )(base, lead, count, hidden)


def ring_first(block, up, down):
    return send(block, up), send(block, down)


def ring_second(from_up, from_down, up, down):
    half = from_up.shape[0] // 2
    return send(from_up[:half], up), send(from_down[half:], down)


def gate_tables(gates, index):
    index_t = index[0].T
    gates_t = gates[0].T
    experts = jnp.arange(SOURCES * EXP, dtype=jnp.int32)[None, :, None]
    dense = jnp.sum(
        jnp.where(index_t[:, None, :] == experts, gates_t[:, None, :].astype(jnp.float32), 0.0), axis=0
    )
    dense = dense.astype(jnp.bfloat16).reshape(SOURCES, EXP, TOK)
    gate = lax.all_to_all(dense, "expert", split_axis=0, concat_axis=0, tiled=True)
    present = gate > 0
    ones = present.astype(jnp.float32)
    earlier_token = jnp.triu(jnp.ones((TOK, TOK), jnp.float32), 1)
    rank = jnp.einsum("set,tu->seu", ones, earlier_token, preferred_element_type=jnp.float32)
    counts = jnp.sum(ones, axis=2)
    earlier_source = jnp.tril(jnp.ones((SOURCES, SOURCES), jnp.float32), -1)
    offset = jnp.einsum("rs,se->re", earlier_source, counts, preferred_element_type=jnp.float32)
    offset = offset.astype(jnp.int32)
    base = jnp.minimum(offset // 16 * 16, CAP - WINDOW)
    rank = jnp.where(present, rank.astype(jnp.int32), -1)
    flat = (SOURCES * EXP,)
    return (
        gate.astype(jnp.float32),
        rank,
        base.reshape(flat),
        (offset - base).reshape(flat),
        counts.astype(jnp.int32).reshape(flat),
    )


def body(out_grad, gates, expert_index, saved_hidden, down_weight):
    tokens = out_grad[0]
    order = lax.dynamic_index_in_dim(
        jnp.asarray(source_orders()), lax.axis_index("expert"), 0, keepdims=False
    )
    replica = lax.axis_index("replica")
    place = jnp.stack([replica % 2, replica // 2]).astype(jnp.int32)

    count = len(STAGES)
    starts = [sum(STAGES[:s]) for s in range(count)]

    def first_rings(group, hold, ready):
        lefts, rights, spans = [], [], []
        at = 0
        for s in group:
            half = STAGES[s] // 2
            lefts.append(tokens[:, starts[s] : starts[s] + half])
            rights.append(tokens[:, starts[s] + half : starts[s] + 2 * half])
            spans.append((at, at + half))
            at += half
        mine = jnp.concatenate(lefts + rights, axis=1)
        if hold is not None:
            mine = after(mine, *hold)
        both = jnp.concatenate([mine, send(mine, X_SWAP)], axis=0)
        if ready is not None:
            both = after(both, ready)
        a, b = both[:, :at], both[:, at:]
        a_up, a_down = ring_first(a, Z_UP, Z_DOWN)
        b_up, b_down = ring_first(b, Y_UP, Y_DOWN)
        a_far = ring_second(a_up, a_down, Z_UP, Z_DOWN)
        b_far = ring_second(b_up, b_down, Y_UP, Y_DOWN)
        pieces = (a, a_up, a_down, *a_far, b, b_up, b_down, *b_far)
        if len(group) == 1:
            return {group[0]: join(pieces)}
        return {
            s: join(tuple(piece[:, low:high] for piece in pieces))
            for s, (low, high) in zip(group, spans)
        }

    gate, rank, base, lead, counts = gate_tables(gates, expert_index)
    scaled, padded, row_gate, pick = prepare(base, lead, counts, place, rank, gate, saved_hidden)

    wide = first_rings(GROUPS[0], None, None)
    later = list(GROUPS[1:])
    total = None
    shares = []
    near = pair = None
    selected, crossed = [], []
    hidden = sums = None

    def second_ring_first(s):
        a, b = wide[s]
        hold = list(near or ())
        if s >= 2:
            hold.append(selected[s - 2])
        if hold:
            a, b = after(a, *hold), after(b, *hold)
        return (a, b), (*ring_first(a, Y_UP, Y_DOWN), *ring_first(b, Z_UP, Z_DOWN))

    def second_ring_second(near, hold):
        ends = [after(value, *hold) if hold else value for value in near]
        return (
            ring_second(ends[0], ends[1], Y_UP, Y_DOWN),
            ring_second(ends[2], ends[3], Z_UP, Z_DOWN),
        )

    (a, b), near = second_ring_first(0)
    wide.update(first_rings(later.pop(0), (a, b), scaled))
    far_a, far_b = second_ring_second(near, ())
    for s in range(count):
        pieces = (a, near[0], near[1], *far_a, b, near[2], near[3], *far_b)
        last = s + 1 == count
        if not last:
            (a, b), near = second_ring_first(s + 1)
        hold = []
        if s > 0:
            hold += [total, pair]
        if s > 1:
            hold.append(crossed[s - 2])
        if s + 1 < count:
            hold += [a, b]
        if hold:
            pieces = tuple(after(piece, *hold) for piece in pieces)
        rows, go, stay = select(order, pick, scaled, pieces)
        selected.append(go)
        leaving = after(go, *near) if 0 < s < count - 1 else go
        met = lax.ppermute(leaving, "replica", CORE_SWAP)
        pair = (met.astype(jnp.float32) + stay.astype(jnp.float32)).astype(jnp.bfloat16)
        across = lax.ppermute(pair[1], "replica", XHI_SWAP)
        shares.append(
            (pair[0].astype(jnp.float32) + across.astype(jnp.float32)).astype(jnp.bfloat16)
        )
        if not last:
            far_a, far_b = second_ring_second(near, (go,))
        if last:
            rows = after(rows, pair, *crossed[s - 1 :])
        crossed.append(across)
        result = upstream(rows, down_weight, starts[s], total, (padded, row_gate, pick), last)
        if last:
            hidden, sums = result
        else:
            total = result

    weight_grad = jnp.concatenate(shares, axis=2)
    back = lax.all_to_all(
        jnp.swapaxes(sums, 0, 1), "expert", split_axis=0, concat_axis=0, tiled=True
    ).reshape(SOURCES * EXP, TOK)
    hidden_grad = in_slot_order(base, lead, counts, hidden)
    index_t = expert_index[0].T
    experts = jnp.arange(SOURCES * EXP, dtype=jnp.int32)[None, :, None]
    picked = jnp.sum(jnp.where(index_t[:, None, :] == experts, back[None], 0.0), axis=1)
    gate_grad = picked.T[None]
    return (hidden_grad, gate_grad, weight_grad)


def solution(mesh):
    in_specs = (
        P("replica", "expert", None),
        P("replica", "expert", None),
        P("replica", "expert", None),
        P("replica", "expert", None, None),
        P("expert", None, None),
    )
    out_specs = (
        P("replica", "expert", None, None),
        P("replica", "expert", None),
        P("expert", "replica", None),
    )
    return jax.shard_map(body, mesh=mesh, in_specs=in_specs, out_specs=out_specs, check_vma=False)
```

profile of v0, /device:TPU:1, one launch (start us, length us, event | category | flops | bytes accessed | tf_op | source)
XLA Modules:
  0.0 652.2 jit_solution(11127433812533684155)
XLA Ops:
  2.6 9.8 %all-to-all-start = ((bf16[32,2,128]{2,1,0:T(2,128)(2,1)}), bf16[32,2,128]{2,1,0:T(2,128)(2,1)S(1)}, u32[]{:S(2)}, u32[]{:S(2)}) async-start(bf16[32,2,128]{2,1,0:T(2,128)(2,1)} %bitcast.4), calls=%async_computation | async-start | bytes 32768 | tf_op jit(solution)/shard_map/all_to_all | solution.py:430
  15.9 4.7 collective-permute-done
  28.1 2.7 collective-permute-start.4
  33.9 2.3 collective-permute-done.7.refs_8_
  37.5 64.7 %join.3 = (bf16[1024,512]{1,0:T(8,128)(2,1)}, bf16[1024,512]{1,0:T(8,128)(2,1)}) custom-call(bf16[256,512]{1,0:T(8,128)(2,1)} %copy-done.43, bf16[256,512]{1,0:T(8,128)(2,1)} %copy-done.44, bf16[256,512]{1,0:T(8,128)(2,1)} %copy-done.45, bf16[128,512]{1,0:T(8,128)(2,1)} %copy-done.52, bf16[128,512]{1,0:T(8,128)(2,1)} %copy-done.53, ...), custom_call_target="tpu_custom_call" | custom-call | bytes 4194304 | tf_op jit(solution)/shard_map/join/pallas_call | solution.py:167
  103.8 2.3 copy-done.8
  106.1 12.5 %prepare.1 = (bf16[2,768,1536]{2,1,0:T(8,128)(2,1)S(1)}, bf16[2,1536,768]{2,1,0:T(8,128)(2,1)S(1)}, f32[2,1536,128]{2,1,0:T(8,128)S(1)}, bf16[2,1536,128]{2,1,0:T(8,128)(2,1)S(1)}) custom-call(s32[64]{0:T(128)S(1)} %reshape.30.base_ref, s32[64]{0:T(128)S(1)} %reshape.31.lead_ref, s32[64]{0:T(128)S(1)} %convert_element_type.107.count_ref, ...), custom_call_target="tpu_custom_call" | custom-call | flops 1000000000 | bytes 16000000 | tf_op jit(solution)/shard_map/prepare/pallas_call | solution.py:119
  126.8 2.7 collective-permute-start.11
  129.5 12.4 %collective-permute-done.18.refs_1_ = bf16[1024,512]{1,0:T(8,128)(2,1)S(1)} collective-permute-done((bf16[1024,512]{1,0:T(8,128)(2,1)S(1)}, bf16[1024,512]{1,0:T(8,128)(2,1)S(1)}, u32[]{:S(2)}, u32[]{:S(2)}) %collective-permute-start.18) | collective-permute-done | bytes 1048608 | tf_op jit(solution)/shard_map/ppermute | solution.py:50
  142.5 2.6 collective-permute-start.15
  146.3 11.7 %collective-permute-done.14 = bf16[256,1536]{1,0:T(8,128)(2,1)S(1)} collective-permute-done((bf16[256,1536]{1,0:T(8,128)(2,1)S(1)}, bf16[256,1536]{1,0:T(8,128)(2,1)S(1)}, u32[]{:S(2)}, u32[]{:S(2)}) %collective-permute-start.14) | collective-permute-done | bytes 786464 | tf_op jit(solution)/shard_map/ppermute | solution.py:50
  158.4 4.2 collective-permute-done.20.refs_6_
  166.1 2.7 collective-permute-start.27
  171.1 2.6 collective-permute-done.13
  174.6 3.9 collective-permute-start.29
  186.8 128.2 %join.5 = (bf16[1024,1024]{1,0:T(8,128)(2,1)}, bf16[1024,1024]{1,0:T(8,128)(2,1)}) custom-call(bf16[256,1024]{1,0:T(8,128)(2,1)} %get-tuple-element.140.refs_0_, bf16[256,1024]{1,0:T(8,128)(2,1)} %slice.245.refs_1_, bf16[256,1024]{1,0:T(8,128)(2,1)} %slice.246.refs_2_, bf16[128,1024]{1,0:T(8,128)(2,1)} %slice.247.refs_3_, bf16[128,1024]{1,0:T(8,128)(2,1)} %slice.248.refs_4_, ...), custom_call_target="tpu_custom_call" | custom-call | bytes 8388608 | tf_op jit(solution)/shard_map/join/pallas_call | solution.py:167
  317.8 2.7 collective-permute-start.25
  326.1 2.3 copy-done.22
  329.6 15.9 %select.13 = (bf16[2,1536,1024]{2,1,0:T(8,128)(2,1)S(1)}, bf16[2,2,192,1024]{3,2,1,0:T(8,128)(2,1)}, bf16[2,2,192,1024]{3,2,1,0:T(8,128)(2,1)S(1)}) custom-call(s32[64]{0:T(128)S(1)} %dynamic-slice_bitcast_fusion.order_ref, bf16[2,1536,128]{2,1,0:T(8,128)(2,1)S(1)} %get-tuple-element.70.pick_ref.refs_5_, bf16[2,768,1536]{2,1,0:T(8,128)(2,1)S(1)} %copy-done.22, ...), custom_call_target="tpu_custom_call" | custom-call | flops 9663676416 | bytes 22680064 | tf_op jit(solution)/shard_map/select/pallas_call | solution.py:258
  345.6 2.6 copy-done.2
  348.1 8.3 %collective-permute-start.30 = (bf16[2,2,192,1024]{3,2,1,0:T(8,128)(2,1)}, bf16[2,2,192,1024]{3,2,1,0:T(8,128)(2,1)}, u32[]{:S(2)}, u32[]{:S(2)}) collective-permute-start(bf16[2,2,192,1024]{3,2,1,0:T(8,128)(2,1)} %get-tuple-element.91), channel_id=1, source_target_pairs={{0,1},{1,0},{2,3},{3,2},{4,5},{5,4},{6,7},{7,6},{8,9},{9,8},{10,11... | collective-permute-start | bytes 4718600 | tf_op jit(solution)/shard_map/ppermute | solution.py:537
  356.5 2.3 slice.209
  363.7 2.3 slice.211
  366.1 2.3 slice.212
  368.3 2.7 collective-permute-start.34
  385.8 64.7 %join.4 = (bf16[1024,512]{1,0:T(8,128)(2,1)}, bf16[1024,512]{1,0:T(8,128)(2,1)}) custom-call(bf16[256,512]{1,0:T(8,128)(2,1)} %get-tuple-element.144.refs_0_, bf16[256,512]{1,0:T(8,128)(2,1)} %slice.233.refs_1_, bf16[256,512]{1,0:T(8,128)(2,1)} %slice.234.refs_2_, bf16[128,512]{1,0:T(8,128)(2,1)} %slice.236.refs_3_, bf16[128,512]{1,0:T(8,128)(2,1)} %slice.238.refs_4_, ...), custom_call_target="tpu_custom_call" | custom-call | bytes 4194304 | tf_op jit(solution)/shard_map/join/pallas_call | solution.py:167
  450.5 2.8 copy-done.3
  453.3 8.1 %upstream.2.refs_2_ = f32[2,1536,768]{2,1,0:T(8,128)S(1)} custom-call(bf16[2,1536,1024]{2,1,0:T(8,128)(2,1)S(1)} %copy-done.3, bf16[2,768,4096]{2,1,0:T(8,128)(2,1)} %refs_1_.5), custom_call_target="tpu_custom_call" | custom-call | flops 75497472 | bytes 2359296 | tf_op jit(solution)/shard_map/upstream/pallas_call | solution.py:359
  461.4 3.5 add_convert_fusion.2
  466.2 2.4 collective-permute-start.36
  468.5 2.8 collective-permute-start.38
  472.6 24.0 %select.14 = (bf16[2,1536,2048]{2,1,0:T(8,128)(2,1)}, bf16[2,2,192,2048]{3,2,1,0:T(8,128)(2,1)}, bf16[2,2,192,2048]{3,2,1,0:T(8,128)(2,1)}) custom-call(s32[64]{0:T(128)S(1)} %dynamic-slice_bitcast_fusion.order_ref, bf16[2,1536,128]{2,1,0:T(8,128)(2,1)S(1)} %copy-done.12, bf16[2,768,1536]{2,1,0:T(8,128)(2,1)} %copy-done.21, ...), custom_call_target="tpu_custom_call" | custom-call | flops 19327352832 | bytes 37360128 | tf_op jit(solution)/shard_map/select/pallas_call | solution.py:258
  496.6 11.7 %collective-permute-start.39 = (bf16[2,2,192,2048]{3,2,1,0:T(8,128)(2,1)}, bf16[2,2,192,2048]{3,2,1,0:T(8,128)(2,1)S(1)}, u32[]{:S(2)}, u32[]{:S(2)}) collective-permute-start(bf16[2,2,192,2048]{3,2,1,0:T(8,128)(2,1)} %get-tuple-element.113), channel_id=1, source_target_pairs={{0,1},{1,0},{2,3},{3,2},{4,5},{5,4},{6,7},{7,6},{8,9},{9,8},{10,11... | collective-permute-start | bytes 9437192 | tf_op jit(solution)/shard_map/ppermute | solution.py:537
  509.5 2.5 collective-permute-start.40
  514.2 2.7 collective-permute-start.42
  519.2 4.6 copy-done.1
  523.8 18.3 %upstream.3.refs_2_ = f32[2,1536,768]{2,1,0:T(8,128)S(1)} custom-call(bf16[2,1536,2048]{2,1,0:T(8,128)(2,1)S(1)} %copy-done.1, bf16[2,768,4096]{2,1,0:T(8,128)(2,1)} %refs_1_.5, f32[2,1536,768]{2,1,0:T(8,128)S(1)} %upstream.2.refs_2_), custom_call_target="tpu_custom_call", output_to_operand_aliasing={{}: (2, {})} | custom-call | flops 150994944 | bytes 2359296 | tf_op jit(solution)/shard_map/upstream/pallas_call | solution.py:359
  542.1 2.7 collective-permute-start.44
  544.8 5.8 add_convert_fusion
  550.7 4.2 collective-permute-done.44.refs_9_
  554.9 2.3 copy-done.23
  557.2 16.6 %select.15 = (bf16[2,1536,1024]{2,1,0:T(8,128)(2,1)S(1)}, bf16[2,2,192,1024]{3,2,1,0:T(8,128)(2,1)S(1)}, bf16[2,2,192,1024]{3,2,1,0:T(8,128)(2,1)S(1)}) custom-call(s32[64]{0:T(128)S(1)} %dynamic-slice_bitcast_fusion.order_ref, bf16[2,1536,128]{2,1,0:T(8,128)(2,1)S(1)} %copy-done.12, bf16[2,768,1536]{2,1,0:T(8,128)(2,1)S(1)} %copy-done.23, ...), custom_call_target="tpu_custom_call" | custom-call | flops 9663676416 | bytes 22680064 | tf_op jit(solution)/shard_map/select/pallas_call | solution.py:258
  580.7 33.0 %collective-permute-done.46 = bf16[2,192,2048]{2,1,0:T(8,128)(2,1)S(1)} collective-permute-done((bf16[2,192,2048]{2,1,0:T(8,128)(2,1)S(1)}, bf16[2,192,2048]{2,1,0:T(8,128)(2,1)S(1)}, u32[]{:S(2)}, u32[]{:S(2)}) %collective-permute-start.46) | collective-permute-done | bytes 1572896 | tf_op jit(solution)/shard_map/ppermute | solution.py:539
  614.5 2.3 copy-done.5
  616.8 11.1 %finish.1 = (bf16[2,1536,768]{2,1,0:T(8,128)(2,1)S(1)}, f32[2,32,128]{2,1,0:T(8,128)S(1)}) custom-call(bf16[2,1536,1024]{2,1,0:T(8,128)(2,1)S(1)} %get-tuple-element.132.refs_0_, bf16[2,768,4096]{2,1,0:T(8,128)(2,1)} %refs_1_.5, f32[2,1536,768]{2,1,0:T(8,128)} %copy-done, bf16[2,1536,768]{2,1,0:T(8,128)(2,1)S(1)} %copy-done.5, ...), custom_call_target="tpu_custom_call" | custom-call | flops 75497472 | bytes 2359296 | tf_op jit(solution)/shard_map/finish/pallas_call | solution.py:359
  630.7 5.7 all-to-all-start.1
  636.5 2.7 fusion
  639.8 8.3 %in_slot_order.1 = bf16[1,2,1536,768]{3,2,1,0:T(8,128)(2,1)} custom-call(s32[64]{0:T(128)S(1)} %reshape.30.base_ref, s32[64]{0:T(128)S(1)} %reshape.31.lead_ref, s32[64]{0:T(128)S(1)} %convert_element_type.107.count_ref, bf16[2,1536,768]{2,1,0:T(8,128)(2,1)S(1)} %copy-done.7), custom_call_target="tpu_custom_call" | custom-call | flops 1000000000 | bytes 12000000 | tf_op jit(solution)/shard_map/in_slot_order/pallas_call | solution.py:398
  (250 shorter events, 96.1 us)
Async XLA Ops:
  2.6 31.1 %all-to-all-start = ((bf16[32,2,128]{2,1,0:T(2,128)(2,1)}), bf16[32,2,128]{2,1,0:T(2,128)(2,1)S(1)}, u32[]{:S(2)}, u32[]{:S(2)}) async-start(bf16[32,2,128]{2,1,0:T(2,128)(2,1)} %bitcast.4), calls=%async_computation | async-start | bytes 32768 | tf_op jit(solution)/shard_map/all_to_all | solution.py:430
  13.6 7.0 %collective-permute-start = (bf16[128,1024]{1,0:T(8,128)(2,1)S(1)}, bf16[128,1024]{1,0:T(8,128)(2,1)S(1)}, u32[]{:S(2)}, u32[]{:S(2)}) collective-permute-start(bf16[128,1024]{1,0:T(8,128)(2,1)S(1)} %get-tuple-element.145), channel_id=1, source_target_pairs={{0,16},{4,20},{8,24},{12,28},{16,0},{20,4},{24,8},{28,12},{32,48},... | collective-permute-start | bytes 786440 | tf_op jit(solution)/shard_map/ppermute | solution.py:50
  20.7 7.3 %collective-permute-start.1 = (bf16[256,512]{1,0:T(8,128)(2,1)S(1)}, bf16[256,512]{1,0:T(8,128)(2,1)S(1)}, u32[]{:S(2)}, u32[]{:S(2)}) collective-permute-start(bf16[256,512]{1,0:T(8,128)(2,1)S(1)} %get-tuple-element.151.refs_0_), channel_id=1, source_target_pairs={{0,32},{4,36},{8,40},{12,44},{16,48},{20,52},{24,56},{28,60},{32,6... | collective-permute-start | bytes 786440 | tf_op jit(solution)/shard_map/ppermute | solution.py:50
  21.6 6.4 collective-permute-start.2
  23.5 7.4 %collective-permute-start.5 = (bf16[256,512]{1,0:T(8,128)(2,1)S(1)}, bf16[256,512]{1,0:T(8,128)(2,1)S(1)}, u32[]{:S(2)}, u32[]{:S(2)}) collective-permute-start(bf16[256,512]{1,0:T(8,128)(2,1)S(1)} %get-tuple-element.150.refs_5_), channel_id=1, source_target_pairs={{0,4},{4,8},{8,12},{12,0},{16,20},{20,24},{24,28},{28,16},{32,36},... | collective-permute-start | bytes 786440 | tf_op jit(solution)/shard_map/ppermute | solution.py:50
  24.3 7.1 %collective-permute-start.6 = (bf16[256,512]{1,0:T(8,128)(2,1)S(1)}, bf16[256,512]{1,0:T(8,128)(2,1)S(1)}, u32[]{:S(2)}, u32[]{:S(2)}) collective-permute-start(bf16[256,512]{1,0:T(8,128)(2,1)S(1)} %get-tuple-element.150.refs_5_), channel_id=1, source_target_pairs={{0,12},{4,0},{8,4},{12,8},{16,28},{20,16},{24,20},{28,24},{32,44},... | collective-permute-start | bytes 786440 | tf_op jit(solution)/shard_map/ppermute | solution.py:50
  28.0 5.9 collective-permute-start.3
  28.1 5.8 collective-permute-start.4
  30.8 5.4 collective-permute-start.7
  102.2 21.3 %collective-permute-start.9 = (bf16[128,3072]{1,0:T(8,128)(2,1)}, bf16[128,3072]{1,0:T(8,128)(2,1)}, u32[]{:S(2)}, u32[]{:S(2)}) collective-permute-start(bf16[128,3072]{1,0:T(8,128)(2,1)} %pad_maximum_fusion.2), channel_id=1, source_target_pairs={{0,16},{4,20},{8,24},{12,28},{16,0},{20,4},{24,8},{28,12},{32,48},... | collective-permute-start | bytes 2359304 | tf_op jit(solution)/shard_map/ppermute | solution.py:50
  120.9 21.1 %collective-permute-start.18 = (bf16[1024,512]{1,0:T(8,128)(2,1)S(1)}, bf16[1024,512]{1,0:T(8,128)(2,1)S(1)}, u32[]{:S(2)}, u32[]{:S(2)}) collective-permute-start(bf16[1024,512]{1,0:T(8,128)(2,1)S(1)} %copy-done.25), channel_id=1, source_target_pairs={{0,4},{4,8},{8,12},{12,0},{16,20},{20,24},{24,28},{28,16},{32,36},... | collective-permute-start | bytes 3145736 | tf_op jit(solution)/shard_map/ppermute | solution.py:50
  121.5 20.4 %collective-permute-start.19 = (bf16[1024,512]{1,0:T(8,128)(2,1)S(1)}, bf16[1024,512]{1,0:T(8,128)(2,1)S(1)}, u32[]{:S(2)}, u32[]{:S(2)}) collective-permute-start(bf16[1024,512]{1,0:T(8,128)(2,1)S(1)} %copy-done.25), channel_id=1, source_target_pairs={{0,12},{4,0},{8,4},{12,8},{16,28},{20,16},{24,20},{28,24},{32,44},... | collective-permute-start | bytes 3145736 | tf_op jit(solution)/shard_map/ppermute | solution.py:50
  125.2 17.3 %collective-permute-start.10 = (bf16[256,1536]{1,0:T(8,128)(2,1)S(1)}, bf16[256,1536]{1,0:T(8,128)(2,1)S(1)}, u32[]{:S(2)}, u32[]{:S(2)}) collective-permute-start(bf16[256,1536]{1,0:T(8,128)(2,1)S(1)} %get-tuple-element.142), channel_id=1, source_target_pairs={{0,32},{4,36},{8,40},{12,44},{16,48},{20,52},{24,56},{28,60},{32,6... | collective-permute-start | bytes 2359304 | tf_op jit(solution)/shard_map/ppermute | solution.py:50
  126.8 35.8 %collective-permute-start.20 = (bf16[1024,512]{1,0:T(8,128)(2,1)S(1)}, bf16[1024,512]{1,0:T(8,128)(2,1)S(1)}, u32[]{:S(2)}, u32[]{:S(2)}) collective-permute-start(bf16[1024,512]{1,0:T(8,128)(2,1)S(1)} %copy-done.26), channel_id=1, source_target_pairs={{0,32},{4,36},{8,40},{12,44},{16,48},{20,52},{24,56},{28,60},{32,6... | collective-permute-start | bytes 3145736 | tf_op jit(solution)/shard_map/ppermute | solution.py:50
  126.8 18.3 %collective-permute-start.11 = (bf16[256,1536]{1,0:T(8,128)(2,1)S(1)}, bf16[256,1536]{1,0:T(8,128)(2,1)S(1)}, u32[]{:S(2)}, u32[]{:S(2)}) collective-permute-start(bf16[256,1536]{1,0:T(8,128)(2,1)S(1)} %get-tuple-element.142), channel_id=1, source_target_pairs={{0,96},{4,100},{8,104},{12,108},{16,112},{20,116},{24,120},{28,124... | collective-permute-start | bytes 2359304 | tf_op jit(solution)/shard_map/ppermute | solution.py:50
  141.9 16.0 %collective-permute-start.14 = (bf16[256,1536]{1,0:T(8,128)(2,1)S(1)}, bf16[256,1536]{1,0:T(8,128)(2,1)S(1)}, u32[]{:S(2)}, u32[]{:S(2)}) collective-permute-start(bf16[256,1536]{1,0:T(8,128)(2,1)S(1)} %get-tuple-element.141), channel_id=1, source_target_pairs={{0,4},{4,8},{8,12},{12,0},{16,20},{20,24},{24,28},{28,16},{32,36},... | collective-permute-start | bytes 2359304 | tf_op jit(solution)/shard_map/ppermute | solution.py:50
  142.0 23.2 %collective-permute-start.21 = (bf16[1024,512]{1,0:T(8,128)(2,1)S(1)}, bf16[1024,512]{1,0:T(8,128)(2,1)S(1)}, u32[]{:S(2)}, u32[]{:S(2)}) collective-permute-start(bf16[1024,512]{1,0:T(8,128)(2,1)S(1)} %copy-done.26), channel_id=1, source_target_pairs={{0,96},{4,100},{8,104},{12,108},{16,112},{20,116},{24,120},{28,124... | collective-permute-start | bytes 3145736 | tf_op jit(solution)/shard_map/ppermute | solution.py:50
  142.5 23.6 %collective-permute-start.15 = (bf16[256,1536]{1,0:T(8,128)(2,1)S(1)}, bf16[256,1536]{1,0:T(8,128)(2,1)S(1)}, u32[]{:S(2)}, u32[]{:S(2)}) collective-permute-start(bf16[256,1536]{1,0:T(8,128)(2,1)S(1)} %get-tuple-element.141), channel_id=1, source_target_pairs={{0,12},{4,0},{8,4},{12,8},{16,28},{20,16},{24,20},{28,24},{32,44},... | collective-permute-start | bytes 2359304 | tf_op jit(solution)/shard_map/ppermute | solution.py:50
  145.1 25.9 %collective-permute-start.12 = (bf16[128,1536]{1,0:T(8,128)(2,1)S(1)}, bf16[128,1536]{1,0:T(8,128)(2,1)S(1)}, u32[]{:S(2)}, u32[]{:S(2)}) collective-permute-start(bf16[128,1536]{1,0:T(8,128)(2,1)S(1)} %slice.235), channel_id=1, source_target_pairs={{0,32},{4,36},{8,40},{12,44},{16,48},{20,52},{24,56},{28,60},{32,6... | collective-permute-start | bytes 1179656 | tf_op jit(solution)/shard_map/ppermute | solution.py:50
  157.9 15.7 %collective-permute-start.13 = (bf16[128,1536]{1,0:T(8,128)(2,1)S(1)}, bf16[128,1536]{1,0:T(8,128)(2,1)S(1)}, u32[]{:S(2)}, u32[]{:S(2)}) collective-permute-start(bf16[128,1536]{1,0:T(8,128)(2,1)S(1)} %slice.237), channel_id=1, source_target_pairs={{0,96},{4,100},{8,104},{12,108},{16,112},{20,116},{24,120},{28,124... | collective-permute-start | bytes 1179656 | tf_op jit(solution)/shard_map/ppermute | solution.py:50
  162.6 11.9 %collective-permute-start.16 = (bf16[128,1536]{1,0:T(8,128)(2,1)S(1)}, bf16[128,1536]{1,0:T(8,128)(2,1)S(1)}, u32[]{:S(2)}, u32[]{:S(2)}) collective-permute-start(bf16[128,1536]{1,0:T(8,128)(2,1)S(1)} %slice.241), channel_id=1, source_target_pairs={{0,4},{4,8},{8,12},{12,0},{16,20},{20,24},{24,28},{28,16},{32,36},... | collective-permute-start | bytes 1179656 | tf_op jit(solution)/shard_map/ppermute | solution.py:50
  165.2 151.3 %collective-permute-start.26 = (bf16[512,512]{1,0:T(8,128)(2,1)}, bf16[512,512]{1,0:T(8,128)(2,1)}, u32[]{:S(2)}, u32[]{:S(2)}) collective-permute-start(bf16[512,512]{1,0:T(8,128)(2,1)} %slice.253), channel_id=1, source_target_pairs={{0,4},{4,8},{8,12},{12,0},{16,20},{20,24},{24,28},{28,16},{32,36},... | collective-permute-start | bytes 1572872 | tf_op jit(solution)/shard_map/ppermute | solution.py:50
  166.1 151.6 %collective-permute-start.27 = (bf16[512,512]{1,0:T(8,128)(2,1)}, bf16[512,512]{1,0:T(8,128)(2,1)}, u32[]{:S(2)}, u32[]{:S(2)}) collective-permute-start(bf16[512,512]{1,0:T(8,128)(2,1)} %slice.254), channel_id=1, source_target_pairs={{0,12},{4,0},{8,4},{12,8},{16,28},{20,16},{24,20},{28,24},{32,44},... | collective-permute-start | bytes 1572872 | tf_op jit(solution)/shard_map/ppermute | solution.py:50
  171.0 146.7 %collective-permute-start.28 = (bf16[512,512]{1,0:T(8,128)(2,1)}, bf16[512,512]{1,0:T(8,128)(2,1)}, u32[]{:S(2)}, u32[]{:S(2)}) collective-permute-start(bf16[512,512]{1,0:T(8,128)(2,1)} %slice.255), channel_id=1, source_target_pairs={{0,32},{4,36},{8,40},{12,44},{16,48},{20,52},{24,56},{28,60},{32,6... | collective-permute-start | bytes 1572872 | tf_op jit(solution)/shard_map/ppermute | solution.py:50
  173.6 11.7 %collective-permute-start.17 = (bf16[128,1536]{1,0:T(8,128)(2,1)S(1)}, bf16[128,1536]{1,0:T(8,128)(2,1)S(1)}, u32[]{:S(2)}, u32[]{:S(2)}) collective-permute-start(bf16[128,1536]{1,0:T(8,128)(2,1)S(1)} %slice.243), channel_id=1, source_target_pairs={{0,12},{4,0},{8,4},{12,8},{16,28},{20,16},{24,20},{28,24},{32,44},... | collective-permute-start | bytes 1179656 | tf_op jit(solution)/shard_map/ppermute | solution.py:50
  174.6 146.6 %collective-permute-start.29 = (bf16[512,512]{1,0:T(8,128)(2,1)}, bf16[512,512]{1,0:T(8,128)(2,1)}, u32[]{:S(2)}, u32[]{:S(2)}) collective-permute-start(bf16[512,512]{1,0:T(8,128)(2,1)} %slice.256), channel_id=1, source_target_pairs={{0,96},{4,100},{8,104},{12,108},{16,112},{20,116},{24,120},{28,124... | collective-permute-start | bytes 1572872 | tf_op jit(solution)/shard_map/ppermute | solution.py:50
  315.0 41.5 %collective-permute-start.22 = (bf16[1024,1024]{1,0:T(8,128)(2,1)}, bf16[1024,1024]{1,0:T(8,128)(2,1)}, u32[]{:S(2)}, u32[]{:S(2)}) collective-permute-start(bf16[1024,1024]{1,0:T(8,128)(2,1)} %get-tuple-element.97.refs_0_), channel_id=1, source_target_pairs={{0,4},{4,8},{8,12},{12,0},{16,20},{20,24},{24,28},{28,16},{32,36},... | collective-permute-start | bytes 6291464 | tf_op jit(solution)/shard_map/ppermute | solution.py:50
  316.5 43.8 %collective-permute-start.23 = (bf16[1024,1024]{1,0:T(8,128)(2,1)}, bf16[1024,1024]{1,0:T(8,128)(2,1)}, u32[]{:S(2)}, u32[]{:S(2)}) collective-permute-start(bf16[1024,1024]{1,0:T(8,128)(2,1)} %get-tuple-element.97.refs_0_), channel_id=1, source_target_pairs={{0,12},{4,0},{8,4},{12,8},{16,28},{20,16},{24,20},{28,24},{32,44},... | collective-permute-start | bytes 6291464 | tf_op jit(solution)/shard_map/ppermute | solution.py:50
  317.8 45.9 %collective-permute-start.24 = (bf16[1024,1024]{1,0:T(8,128)(2,1)}, bf16[1024,1024]{1,0:T(8,128)(2,1)}, u32[]{:S(2)}, u32[]{:S(2)}) collective-permute-start(bf16[1024,1024]{1,0:T(8,128)(2,1)} %get-tuple-element.104.refs_5_), channel_id=1, source_target_pairs={{0,32},{4,36},{8,40},{12,44},{16,48},{20,52},{24,56},{28,60},{32,6... | collective-permute-start | bytes 6291464 | tf_op jit(solution)/shard_map/ppermute | solution.py:50
  317.8 48.3 %collective-permute-start.25 = (bf16[1024,1024]{1,0:T(8,128)(2,1)}, bf16[1024,1024]{1,0:T(8,128)(2,1)}, u32[]{:S(2)}, u32[]{:S(2)}) collective-permute-start(bf16[1024,1024]{1,0:T(8,128)(2,1)} %get-tuple-element.104.refs_5_), channel_id=1, source_target_pairs={{0,96},{4,100},{8,104},{12,108},{16,112},{20,116},{24,120},{28,124... | collective-permute-start | bytes 6291464 | tf_op jit(solution)/shard_map/ppermute | solution.py:50
  348.1 113.2 %collective-permute-start.30 = (bf16[2,2,192,1024]{3,2,1,0:T(8,128)(2,1)}, bf16[2,2,192,1024]{3,2,1,0:T(8,128)(2,1)}, u32[]{:S(2)}, u32[]{:S(2)}) collective-permute-start(bf16[2,2,192,1024]{3,2,1,0:T(8,128)(2,1)} %get-tuple-element.91), channel_id=1, source_target_pairs={{0,1},{1,0},{2,3},{3,2},{4,5},{5,4},{6,7},{7,6},{8,9},{9,8},{10,11... | collective-permute-start | bytes 4718600 | tf_op jit(solution)/shard_map/ppermute | solution.py:537
  358.8 106.4 %collective-permute-start.31 = (bf16[512,1024]{1,0:T(8,128)(2,1)}, bf16[512,1024]{1,0:T(8,128)(2,1)S(1)}, u32[]{:S(2)}, u32[]{:S(2)}) collective-permute-start(bf16[512,1024]{1,0:T(8,128)(2,1)} %slice.209), channel_id=1, source_target_pairs={{0,4},{4,8},{8,12},{12,0},{16,20},{20,24},{24,28},{28,16},{32,36},... | collective-permute-start | bytes 3145736 | tf_op jit(solution)/shard_map/ppermute | solution.py:50
  362.5 106.0 %collective-permute-start.32 = (bf16[512,1024]{1,0:T(8,128)(2,1)}, bf16[512,1024]{1,0:T(8,128)(2,1)}, u32[]{:S(2)}, u32[]{:S(2)}) collective-permute-start(bf16[512,1024]{1,0:T(8,128)(2,1)} %slice.210), channel_id=1, source_target_pairs={{0,12},{4,0},{8,4},{12,8},{16,28},{20,16},{24,20},{28,24},{32,44},... | collective-permute-start | bytes 3145736 | tf_op jit(solution)/shard_map/ppermute | solution.py:50
  366.1 102.5 %collective-permute-start.33 = (bf16[512,1024]{1,0:T(8,128)(2,1)}, bf16[512,1024]{1,0:T(8,128)(2,1)}, u32[]{:S(2)}, u32[]{:S(2)}) collective-permute-start(bf16[512,1024]{1,0:T(8,128)(2,1)} %slice.211), channel_id=1, source_target_pairs={{0,32},{4,36},{8,40},{12,44},{16,48},{20,52},{24,56},{28,60},{32,6... | collective-permute-start | bytes 3145736 | tf_op jit(solution)/shard_map/ppermute | solution.py:50
  368.3 103.0 %collective-permute-start.34 = (bf16[512,1024]{1,0:T(8,128)(2,1)}, bf16[512,1024]{1,0:T(8,128)(2,1)}, u32[]{:S(2)}, u32[]{:S(2)}) collective-permute-start(bf16[512,1024]{1,0:T(8,128)(2,1)} %slice.212), channel_id=1, source_target_pairs={{0,96},{4,100},{8,104},{12,108},{16,112},{20,116},{24,120},{28,124... | collective-permute-start | bytes 3145736 | tf_op jit(solution)/shard_map/ppermute | solution.py:50
  464.9 31.7 %collective-permute-start.35 = (bf16[1024,512]{1,0:T(8,128)(2,1)}, bf16[1024,512]{1,0:T(8,128)(2,1)}, u32[]{:S(2)}, u32[]{:S(2)}) collective-permute-start(bf16[1024,512]{1,0:T(8,128)(2,1)} %get-tuple-element.115.refs_0_), channel_id=1, source_target_pairs={{0,4},{4,8},{8,12},{12,0},{16,20},{20,24},{24,28},{28,16},{32,36},... | collective-permute-start | bytes 3145736 | tf_op jit(solution)/shard_map/ppermute | solution.py:50
  466.2 30.4 %collective-permute-start.36 = (bf16[1024,512]{1,0:T(8,128)(2,1)}, bf16[1024,512]{1,0:T(8,128)(2,1)}, u32[]{:S(2)}, u32[]{:S(2)}) collective-permute-start(bf16[1024,512]{1,0:T(8,128)(2,1)} %get-tuple-element.115.refs_0_), channel_id=1, source_target_pairs={{0,12},{4,0},{8,4},{12,8},{16,28},{20,16},{24,20},{28,24},{32,44},... | collective-permute-start | bytes 3145736 | tf_op jit(solution)/shard_map/ppermute | solution.py:50
  468.5 28.1 %collective-permute-start.37 = (bf16[1024,512]{1,0:T(8,128)(2,1)}, bf16[1024,512]{1,0:T(8,128)(2,1)}, u32[]{:S(2)}, u32[]{:S(2)}) collective-permute-start(bf16[1024,512]{1,0:T(8,128)(2,1)} %get-tuple-element.122.refs_5_), channel_id=1, source_target_pairs={{0,32},{4,36},{8,40},{12,44},{16,48},{20,52},{24,56},{28,60},{32,6... | collective-permute-start | bytes 3145736 | tf_op jit(solution)/shard_map/ppermute | solution.py:50
  468.5 28.1 %collective-permute-start.38 = (bf16[1024,512]{1,0:T(8,128)(2,1)}, bf16[1024,512]{1,0:T(8,128)(2,1)}, u32[]{:S(2)}, u32[]{:S(2)}) collective-permute-start(bf16[1024,512]{1,0:T(8,128)(2,1)} %get-tuple-element.122.refs_5_), channel_id=1, source_target_pairs={{0,96},{4,100},{8,104},{12,108},{16,112},{20,116},{24,120},{28,124... | collective-permute-start | bytes 3145736 | tf_op jit(solution)/shard_map/ppermute | solution.py:50
  496.6 45.4 %collective-permute-start.39 = (bf16[2,2,192,2048]{3,2,1,0:T(8,128)(2,1)}, bf16[2,2,192,2048]{3,2,1,0:T(8,128)(2,1)S(1)}, u32[]{:S(2)}, u32[]{:S(2)}) collective-permute-start(bf16[2,2,192,2048]{3,2,1,0:T(8,128)(2,1)} %get-tuple-element.113), channel_id=1, source_target_pairs={{0,1},{1,0},{2,3},{3,2},{4,5},{5,4},{6,7},{7,6},{8,9},{9,8},{10,11... | collective-permute-start | bytes 9437192 | tf_op jit(solution)/shard_map/ppermute | solution.py:537
  509.5 41.2 %collective-permute-start.40 = (bf16[2,192,1024]{2,1,0:T(8,128)(2,1)S(1)}, bf16[2,192,1024]{2,1,0:T(8,128)(2,1)S(1)}, u32[]{:S(2)}, u32[]{:S(2)}) collective-permute-start(bf16[2,192,1024]{2,1,0:T(8,128)(2,1)S(1)} %slice_bitcast_fusion.5), channel_id=1, source_target_pairs={{0,2},{2,0},{1,3},{3,1},{4,6},{6,4},{5,7},{7,5},{8,10},{10,8},{9,1... | collective-permute-start | bytes 2359304 | tf_op jit(solution)/shard_map/ppermute | solution.py:539
  513.1 37.6 %collective-permute-start.41 = (bf16[512,512]{1,0:T(8,128)(2,1)S(1)}, bf16[512,512]{1,0:T(8,128)(2,1)S(1)}, u32[]{:S(2)}, u32[]{:S(2)}) collective-permute-start(bf16[512,512]{1,0:T(8,128)(2,1)S(1)} %slice.214), channel_id=1, source_target_pairs={{0,4},{4,8},{8,12},{12,0},{16,20},{20,24},{24,28},{28,16},{32,36},... | collective-permute-start | bytes 1572872 | tf_op jit(solution)/shard_map/ppermute | solution.py:50
  514.2 36.5 %collective-permute-start.42 = (bf16[512,512]{1,0:T(8,128)(2,1)S(1)}, bf16[512,512]{1,0:T(8,128)(2,1)S(1)}, u32[]{:S(2)}, u32[]{:S(2)}) collective-permute-start(bf16[512,512]{1,0:T(8,128)(2,1)S(1)} %slice.215), channel_id=1, source_target_pairs={{0,12},{4,0},{8,4},{12,8},{16,28},{20,16},{24,20},{28,24},{32,44},... | collective-permute-start | bytes 1572872 | tf_op jit(solution)/shard_map/ppermute | solution.py:50
  518.0 32.7 %collective-permute-start.43 = (bf16[512,512]{1,0:T(8,128)(2,1)S(1)}, bf16[512,512]{1,0:T(8,128)(2,1)S(1)}, u32[]{:S(2)}, u32[]{:S(2)}) collective-permute-start(bf16[512,512]{1,0:T(8,128)(2,1)S(1)} %slice.216), channel_id=1, source_target_pairs={{0,32},{4,36},{8,40},{12,44},{16,48},{20,52},{24,56},{28,60},{32,6... | collective-permute-start | bytes 1572872 | tf_op jit(solution)/shard_map/ppermute | solution.py:50
  542.1 12.8 %collective-permute-start.44 = (bf16[512,512]{1,0:T(8,128)(2,1)S(1)}, bf16[512,512]{1,0:T(8,128)(2,1)S(1)}, u32[]{:S(2)}, u32[]{:S(2)}) collective-permute-start(bf16[512,512]{1,0:T(8,128)(2,1)S(1)} %slice.217), channel_id=1, source_target_pairs={{0,96},{4,100},{8,104},{12,108},{16,112},{20,116},{24,120},{28,124... | collective-permute-start | bytes 1572872 | tf_op jit(solution)/shard_map/ppermute | solution.py:50
  576.2 37.6 %collective-permute-start.46 = (bf16[2,192,2048]{2,1,0:T(8,128)(2,1)S(1)}, bf16[2,192,2048]{2,1,0:T(8,128)(2,1)S(1)}, u32[]{:S(2)}, u32[]{:S(2)}) collective-permute-start(bf16[2,192,2048]{2,1,0:T(8,128)(2,1)S(1)} %slice_bitcast_fusion.1), channel_id=1, source_target_pairs={{0,2},{2,0},{1,3},{3,1},{4,6},{6,4},{5,7},{7,5},{8,10},{10,8},{9,1... | collective-permute-start | bytes 4718600 | tf_op jit(solution)/shard_map/ppermute | solution.py:539
  613.8 35.0 %collective-permute-start.47 = (bf16[2,192,1024]{2,1,0:T(8,128)(2,1)}, bf16[2,192,1024]{2,1,0:T(8,128)(2,1)}, u32[]{:S(2)}, u32[]{:S(2)}) collective-permute-start(bf16[2,192,1024]{2,1,0:T(8,128)(2,1)} %slice_bitcast_fusion.2), channel_id=1, source_target_pairs={{0,2},{2,0},{1,3},{3,1},{4,6},{6,4},{5,7},{7,5},{8,10},{10,8},{9,1... | collective-permute-start | bytes 2359304 | tf_op jit(solution)/shard_map/ppermute | solution.py:539
  630.7 17.3 %all-to-all-start.1 = ((f32[32,2,128]{2,1,0:T(2,128)}), f32[32,2,128]{2,1,0:T(2,128)S(1)}, u32[]{:S(2)}, u32[]{:S(2)}) async-start(f32[32,2,128]{2,1,0:T(2,128)} %copy.28), calls=%async_computation.1 | async-start | bytes 65536 | tf_op jit(solution)/shard_map/all_to_all | solution.py:555
  (59 other events, 767.1 us)
where the time goes:
time: 663 us; the launch traced here: 652 us
  Pallas kernels  372 us (56%)
  starting transfers between devices  93 us (14%)
  local copies, waits for them, and re-layouts  82 us (12%)
  waiting for transfers between devices  80.2 us (12%)
  other arithmetic  22.5 us (3%)
    pallas_call x3, Pallas kernels, join(): pl.pallas_call(join_kernel, in_specs=[anywhere] * 10, out_specs=[anywhere...  258 us
    pallas_call x3, Pallas kernels, select(): pl.pallas_call(functools.partial(select_kernel, width), in_specs=[smem, v...  56.5 us
    ppermute x42, starting transfers between devices, send(): return lax.ppermute(value, 'expert', pairs)  51.5 us
    ppermute x42, waiting for transfers between devices, send(): return lax.ppermute(value, 'expert', pairs)  46.1 us
    pallas_call x3, Pallas kernels, upstream(): pl.pallas_call(functools.partial(upstream_kernel, total is not None, last...  37.4 us
    unnamed x114, local copies, waits for them, and re-layouts  36.2 us
    ppermute x3, waiting for transfers between devices, body(): across = lax.ppermute(pair[1], 'replica', XHI_SWAP)  33 us
    slice x18, local copies, waits for them, and re-layouts, first_rings(): piece[:, low:high]  22.3 us
  transfers between devices with their start and end apart: 50, of which 12 were waited for; matrix products, arithmetic and copies ran while one was open for 10% of the time, Pallas kernels for 45%

commit v1 on v0

--- a/solution.py
+++ b/solution.py
@@ -17,9 +17,10 @@
 PICK = EXP * MOST
 WINDOW = 64
 SHARE = HID // 4
-STAGES = (1024, 2048, 1024)
+STAGES = (1280, 1536, 1280)
 GROUPS = ((0,), (1, 2))
 MIB = 1024 * 1024
+CROSSED_LAG = 1
 
 NZ, NX, NY = 4, 2, 4
 
@@ -142,37 +143,39 @@
     )(base, lead, count, place, rank, gate, saved)
 
 
-def join_kernel(*refs):
-    pieces, outs, sems = refs[:10], refs[10:12], refs[12]
+def join_kernel(spans, *refs):
+    pieces, outs, sems = refs[:10], refs[10:-1], refs[-1]
     copies = []
-    for side in range(2):
-        first = 0
-        for number in range(5):
-            piece = pieces[side * 5 + number]
-            size = piece.shape[0]
-            copy = pltpu.make_async_copy(
-                piece, outs[side].at[pl.ds(first, size), :], sems.at[side * 5 + number]
-            )
-            copy.start()
-            copies.append(copy)
-            first += size
+    for number, (low, high) in enumerate(spans):
+        for side in range(2):
+            first = 0
+            for part in range(5):
+                piece = pieces[side * 5 + part]
+                size = piece.shape[0]
+                copy = pltpu.make_async_copy(
+                    piece.at[:, pl.ds(low, high - low)],
+                    outs[number * 2 + side].at[pl.ds(first, size), :],
+                    sems.at[len(copies)],
+                )
+                copy.start()
+                copies.append(copy)
+                first += size
     for copy in copies:
         copy.wait()
 
 
-def join(pieces):
-    width = pieces[0].shape[1]
-    anywhere = pl.BlockSpec(memory_space=pl.ANY)
-    shape = jax.ShapeDtypeStruct((1024, width), jnp.bfloat16)
+def join(pieces, spans):
+    shapes = []
+    for low, high in spans:
+        shapes += [jax.ShapeDtypeStruct((1024, high - low), jnp.bfloat16)] * 2
     return pl.pallas_call(
-        join_kernel,
-        in_specs=[anywhere] * 10,
-        out_specs=[anywhere] * 2,
-        out_shape=[shape] * 2,
-        scratch_shapes=[pltpu.SemaphoreType.DMA((10,))],
-        cost_estimate=pl.CostEstimate(
-            flops=0, bytes_accessed=2 * 2 * 1024 * width * 2, transcendentals=0
-        ),
+        functools.partial(join_kernel, spans),
+        in_specs=[pl.BlockSpec(memory_space=pl.ANY)] * 10,
+        out_specs=[pl.BlockSpec(memory_space=pltpu.VMEM)] * len(shapes),
+        out_shape=shapes,
+        scratch_shapes=[pltpu.SemaphoreType.DMA((10 * len(spans),))],
+        compiler_params=pltpu.CompilerParams(vmem_limit_bytes=16 * MIB),
+        cost_estimate=pl.CostEstimate(flops=0, bytes_accessed=2 * MIB, transcendentals=0),
         name="join",
     )(*pieces)
 
@@ -284,14 +287,32 @@
 
 
 ROW_TILE = 512
-DEPTH = 1024
-
-
-def upstream_kernel(has_total, last, *refs):
+
+
+def upstream_kernel(has_total, last, first_column, *refs):
     refs = list(refs)
-    rows_ref, weight_ref = refs[0], refs[1]
+    rows_ref, weight_hbm = refs[0], refs[1]
+    weight, sems = refs[-2:]
+    expert = pl.program_id(0)
+    columns = pl.ds(first_column, weight.shape[2])
+
+    def load(e):
+        return pltpu.make_async_copy(weight_hbm.at[e, :, columns], weight.at[e], sems.at[e])
+
+    for e in range(EXP):
+
+        @pl.when((expert == 0) & (pl.program_id(1) == 0))
+        def _(e=e):
+            load(e).start()
+
+    for e in range(EXP):
+
+        @pl.when((expert == e) & (pl.program_id(1) == 0))
+        def _(e=e):
+            load(e).wait()
+
     product = lax.dot_general(
-        rows_ref[0], weight_ref[0], (((1,), (1,)), ((), ())), preferred_element_type=jnp.float32
+        rows_ref[0], weight[expert], (((1,), (1,)), ((), ())), preferred_element_type=jnp.float32
     )
     at = 2
     if has_total:
@@ -299,16 +320,7 @@
         at += 1
     if not last:
         out_ref = refs[at]
-        step = pl.program_id(2)
-
-        @pl.when(step == 0)
-        def _():
-            out_ref[0] = product + total_ref[0] if has_total else product
-
-        @pl.when(step > 0)
-        def _():
-            out_ref[0] += product
-
+        out_ref[0] = product + total_ref[0] if has_total else product
         return
     product = product + total_ref[0]
     padded_ref, gate_ref, pick_ref, hidden_ref, sum_ref = refs[at : at + 5]
@@ -324,18 +336,14 @@
 
 def upstream(rows, weight, first_column, total, extra, last):
     width = rows.shape[2]
-    depth = DEPTH
     tile = ROW_TILE_LAST if last else ROW_TILE
-    steps = width // depth
-    assert not last or steps == 1
-    lead = first_column // depth
     in_specs = [
-        pl.BlockSpec((1, tile, depth), lambda e, t, k: (e, t, k)),
-        pl.BlockSpec((1, HID, depth), lambda e, t, k: (e, 0, lead + k)),
+        pl.BlockSpec((1, tile, width), lambda e, t: (e, t, 0)),
+        pl.BlockSpec(memory_space=pl.ANY),
     ]
     args = [rows, weight]
-    total_spec = pl.BlockSpec((1, tile, HID), lambda e, t, k: (e, t, 0))
-    narrow = pl.BlockSpec((1, tile, TOK), lambda e, t, k: (e, t, 0))
+    total_spec = pl.BlockSpec((1, tile, HID), lambda e, t: (e, t, 0))
+    narrow = pl.BlockSpec((1, tile, TOK), lambda e, t: (e, t, 0))
     aliases = {}
     if total is not None:
         in_specs.append(total_spec)
@@ -347,7 +355,7 @@
         args += list(extra)
         out_specs = [
             total_spec,
-            pl.BlockSpec((1, tile // MOST, TOK), lambda e, t, k: (e, t, 0)),
+            pl.BlockSpec((1, tile // MOST, TOK), lambda e, t: (e, t, 0)),
         ]
         out_shape = [
             jax.ShapeDtypeStruct((EXP, CAP, HID), jnp.bfloat16),
@@ -357,11 +365,15 @@
         out_specs = total_spec
         out_shape = jax.ShapeDtypeStruct((EXP, CAP, HID), jnp.float32)
     return pl.pallas_call(
-        functools.partial(upstream_kernel, total is not None, last),
-        grid=(EXP, CAP // tile, steps),
+        functools.partial(upstream_kernel, total is not None, last, first_column),
+        grid=(EXP, CAP // tile),
         in_specs=in_specs,
         out_specs=out_specs,
         out_shape=out_shape,
+        scratch_shapes=[
+            pltpu.VMEM((EXP, HID, width), jnp.bfloat16),
+            pltpu.SemaphoreType.DMA((EXP,)),
+        ],
         input_output_aliases=aliases,
         compiler_params=pltpu.CompilerParams(vmem_limit_bytes=32 * MIB),
         cost_estimate=pl.CostEstimate(
@@ -459,7 +471,7 @@
     count = len(STAGES)
     starts = [sum(STAGES[:s]) for s in range(count)]
 
-    def first_rings(group, hold, ready):
+    def first_swap(group, hold):
         lefts, rights, spans = [], [], []
         at = 0
         for s in group:
@@ -471,7 +483,11 @@
         mine = jnp.concatenate(lefts + rights, axis=1)
         if hold is not None:
             mine = after(mine, *hold)
-        both = jnp.concatenate([mine, send(mine, X_SWAP)], axis=0)
+        met = send(mine, X_SWAP)
+        return jnp.concatenate([mine, met], axis=0), at, spans, group, met
+
+    def first_rings(swapped, ready):
+        both, at, spans, group, _ = swapped
         if ready is not None:
             both = after(both, ready)
         a, b = both[:, :at], both[:, at:]
@@ -480,18 +496,16 @@
         a_far = ring_second(a_up, a_down, Z_UP, Z_DOWN)
         b_far = ring_second(b_up, b_down, Y_UP, Y_DOWN)
         pieces = (a, a_up, a_down, *a_far, b, b_up, b_down, *b_far)
-        if len(group) == 1:
-            return {group[0]: join(pieces)}
-        return {
-            s: join(tuple(piece[:, low:high] for piece in pieces))
-            for s, (low, high) in zip(group, spans)
-        }
-
-    gate, rank, base, lead, counts = gate_tables(gates, expert_index)
-    scaled, padded, row_gate, pick = prepare(base, lead, counts, place, rank, gate, saved_hidden)
-
-    wide = first_rings(GROUPS[0], None, None)
-    later = list(GROUPS[1:])
+        joined = join(pieces, tuple(spans))
+        return {s: joined[2 * i : 2 * i + 2] for i, s in enumerate(group)}
+
+    swapped = first_swap(GROUPS[0], None)
+    gate, rank, base, lead, counts = gate_tables(after(gates, swapped[4]), expert_index)
+    wide = first_rings(swapped, None)
+    swapped = first_swap(GROUPS[1], (wide[0][0],))
+    scaled, padded, row_gate, pick = prepare(
+        base, lead, counts, place, after(rank, wide[0][0]), gate, saved_hidden
+    )
     total = None
     shares = []
     near = pair = None
@@ -515,7 +529,7 @@
         )
 
     (a, b), near = second_ring_first(0)
-    wide.update(first_rings(later.pop(0), (a, b), scaled))
+    wide.update(first_rings(swapped, scaled))
     far_a, far_b = second_ring_second(near, ())
     for s in range(count):
         pieces = (a, near[0], near[1], *far_a, b, near[2], near[3], *far_b)
@@ -525,15 +539,16 @@
         hold = []
         if s > 0:
             hold += [total, pair]
-        if s > 1:
-            hold.append(crossed[s - 2])
+        lag = CROSSED_LAG if last else 1
+        if s >= lag:
+            hold.append(crossed[s - lag])
         if s + 1 < count:
             hold += [a, b]
         if hold:
             pieces = tuple(after(piece, *hold) for piece in pieces)
         rows, go, stay = select(order, pick, scaled, pieces)
         selected.append(go)
-        leaving = after(go, *near) if 0 < s < count - 1 else go
+        leaving = after(go, *near) if not last else go
         met = lax.ppermute(leaving, "replica", CORE_SWAP)
         pair = (met.astype(jnp.float32) + stay.astype(jnp.float32)).astype(jnp.bfloat16)
         across = lax.ppermute(pair[1], "replica", XHI_SWAP)
@@ -543,7 +558,7 @@
         if not last:
             far_a, far_b = second_ring_second(near, (go,))
         if last:
-            rows = after(rows, pair, *crossed[s - 1 :])
+            rows = after(rows, pair)
         crossed.append(across)
         result = upstream(rows, down_weight, starts[s], total, (padded, row_gate, pick), last)
         if last:

time: 663 us -> 374 us (0.56); the launches traced: 652 us -> 372 us
  Pallas kernels: 372 us -> 118 us
  local copies, waits for them, and re-layouts: 82 us -> 64.9 us
  other arithmetic: 22.5 us -> 13.6 us
    pallas_call x3 -> x2, Pallas kernels: 258 us -> 4.93 us  [join(): pl.pallas_call(functools.partial(join_kernel, spans), in_specs=[pl.BlockS...]
    ppermute x3, waiting for transfers between devices: 33 us -> 6.94 us  [body(): across = lax.ppermute(pair[1], 'replica', XHI_SWAP)]
    slice x19 -> x2, local copies, waits for them, and re-layouts: 23.2 us -> 2.1 us  [first_swap(): lefts.append(tokens[:, starts[s]:starts[s] + half])]
    unnamed x114 -> x122, local copies, waits for them, and re-layouts: 36.2 us -> 48.1 us
    ppermute x3, waiting for transfers between devices: 1.06 us -> 11.4 us  [body(): met = lax.ppermute(leaving, 'replica', CORE_SWAP)]
    all_to_all x1, waiting for transfers between devices: 0.01 us -> 6.98 us  [gate_tables(): lax.all_to_all(dense, 'expert', split_axis=0, concat_axis=0, tiled=True)]
  transfers between devices with their start and end apart: 50 -> 50, of which waited for: 12 -> 13; matrix products, arithmetic and copies ran while one was open for 10% -> 6% of each run, Pallas kernels for 45% -> 26%
where the time goes in v1:
time: 374 us; the launch traced here: 372 us
  Pallas kernels  118 us (32%)
  starting transfers between devices  99.1 us (26%)
  waiting for transfers between devices  75.5 us (20%)
  local copies, waits for them, and re-layouts  64.9 us (17%)
  other arithmetic  13.6 us (4%)
    pallas_call x3, Pallas kernels, select(): pl.pallas_call(functools.partial(select_kernel, width), in_specs=[smem, v...  59.5 us
    ppermute x42, starting transfers between devices, send(): return lax.ppermute(value, 'expert', pairs)  54.6 us
    ppermute x42, waiting for transfers between devices, send(): return lax.ppermute(value, 'expert', pairs)  50.2 us
    unnamed x122, local copies, waits for them, and re-layouts  48.1 us
    pallas_call x3, Pallas kernels, upstream(): pl.pallas_call(functools.partial(upstream_kernel, total is not None, last...  32.4 us
    ppermute x3, starting transfers between devices, body(): met = lax.ppermute(leaving, 'replica', CORE_SWAP)  26 us
    pallas_call x1, Pallas kernels, prepare(): pl.pallas_call(prepare_kernel, grid_spec=pltpu.PrefetchScalarGridSpec(num...  12.5 us
    ppermute x3, waiting for transfers between devices, body(): met = lax.ppermute(leaving, 'replica', CORE_SWAP)  11.4 us
  transfers between devices with their start and end apart: 50, of which 13 were waited for; matrix products, arithmetic and copies ran while one was open for 6% of the time, Pallas kernels for 26%

profile of v1, /device:TPU:1, one launch (start us, length us, event | category | flops | bytes accessed | tf_op | source)
XLA Modules:
  0.0 372.4 jit_solution(7065519173207304837)
XLA Ops:
  6.9 3.8 %collective-permute-done = bf16[128,1280]{1,0:T(8,128)(2,1)S(1)} collective-permute-done((bf16[128,1280]{1,0:T(8,128)(2,1)S(1)}, bf16[128,1280]{1,0:T(8,128)(2,1)S(1)}, u32[]{:S(2)}, u32[]{:S(2)}) %collective-permute-start) | collective-permute-done | bytes 327712 | tf_op jit(solution)/shard_map/ppermute | solution.py:51
  12.9 2.2 collective-permute-start.2
  18.5 5.3 %all-to-all-start = ((bf16[32,2,128]{2,1,0:T(2,128)(2,1)}), bf16[32,2,128]{2,1,0:T(2,128)(2,1)S(1)}, u32[]{:S(2)}, u32[]{:S(2)}) async-start(bf16[32,2,128]{2,1,0:T(2,128)(2,1)} %bitcast.5), calls=%async_computation | async-start | bytes 32768 | tf_op jit(solution)/shard_map/all_to_all | solution.py:442
  23.9 7.0 %all-to-all-done = bf16[32,2,128]{2,1,0:T(2,128)(2,1)S(1)} async-done(((bf16[32,2,128]{2,1,0:T(2,128)(2,1)}), bf16[32,2,128]{2,1,0:T(2,128)(2,1)S(1)}, u32[]{:S(2)}, u32[]{:S(2)}) %all-to-all-start) | async-done | bytes 16416 | tf_op jit(solution)/shard_map/all_to_all | solution.py:442
  31.5 2.4 collective-permute-start.4
  34.3 2.4 collective-permute-start.8
  41.9 2.7 collective-permute-start.19
  44.6 2.3 copy-done.6
  46.9 12.5 %prepare.1 = (bf16[2,768,1536]{2,1,0:T(8,128)(2,1)S(1)}, bf16[2,1536,768]{2,1,0:T(8,128)(2,1)S(1)}, f32[2,1536,128]{2,1,0:T(8,128)S(1)}, bf16[2,1536,128]{2,1,0:T(8,128)(2,1)S(1)}) custom-call(s32[64]{0:T(128)S(1)} %reshape.30.base_ref, s32[64]{0:T(128)S(1)} %reshape.31.lead_ref, s32[64]{0:T(128)S(1)} %convert_element_type.107.count_ref, ...), custom_call_target="tpu_custom_call" | custom-call | flops 1000000000 | bytes 16000000 | tf_op jit(solution)/shard_map/prepare/pallas_call | solution.py:120
  63.9 2.7 collective-permute-start.21
  68.0 8.1 %collective-permute-done.10.refs_1_ = bf16[256,1408]{1,0:T(8,128)(2,1)S(1)} collective-permute-done((bf16[256,1408]{1,0:T(8,128)(2,1)S(1)}, bf16[256,1408]{1,0:T(8,128)(2,1)S(1)}, u32[]{:S(2)}, u32[]{:S(2)}) %collective-permute-start.10) | collective-permute-done | bytes 720928 | tf_op jit(solution)/shard_map/ppermute | solution.py:51
  77.2 26.0 %collective-permute-done.11.refs_2_ = bf16[256,1408]{1,0:T(8,128)(2,1)S(1)} collective-permute-done((bf16[256,1408]{1,0:T(8,128)(2,1)S(1)}, bf16[256,1408]{1,0:T(8,128)(2,1)S(1)}, u32[]{:S(2)}, u32[]{:S(2)}) %collective-permute-start.11) | collective-permute-done | bytes 720928 | tf_op jit(solution)/shard_map/ppermute | solution.py:51
  107.1 2.7 collective-permute-start.27
  109.9 4.9 %collective-permute-done.12.refs_3_ = bf16[128,1408]{1,0:T(8,128)(2,1)S(1)} collective-permute-done((bf16[128,1408]{1,0:T(8,128)(2,1)S(1)}, bf16[128,1408]{1,0:T(8,128)(2,1)S(1)}, u32[]{:S(2)}, u32[]{:S(2)}) %collective-permute-start.12) | collective-permute-done | bytes 360480 | tf_op jit(solution)/shard_map/ppermute | solution.py:51
  114.9 2.7 collective-permute-start.17
  118.6 4.1 %collective-permute-done.16.refs_8_ = bf16[128,1408]{1,0:T(8,128)(2,1)S(1)} collective-permute-done((bf16[128,1408]{1,0:T(8,128)(2,1)S(1)}, bf16[128,1408]{1,0:T(8,128)(2,1)S(1)}, u32[]{:S(2)}, u32[]{:S(2)}) %collective-permute-start.16) | collective-permute-done | bytes 360480 | tf_op jit(solution)/shard_map/ppermute | solution.py:51
  123.3 3.4 join.3
  126.8 2.7 collective-permute-start.23
  139.9 2.3 copy-done.20
  147.0 19.7 %select.13 = (bf16[2,1536,1280]{2,1,0:T(8,128)(2,1)}, bf16[2,2,192,1280]{3,2,1,0:T(8,128)(2,1)S(1)}, bf16[2,2,192,1280]{3,2,1,0:T(8,128)(2,1)S(1)}) custom-call(s32[64]{0:T(128)S(1)} %dynamic-slice_bitcast_fusion.order_ref, bf16[2,1536,128]{2,1,0:T(8,128)(2,1)S(1)} %get-tuple-element.76.pick_ref.refs_5_, bf16[2,768,1536]{2,1,0:T(8,128)(2,1)S(1)} %copy-done.20, ...), custom_call_target="tpu_custom_call" | custom-call | flops 12079595520 | bytes 26350080 | tf_op jit(solution)/shard_map/select/pallas_call | solution.py:261
  166.7 22.4 %collective-permute-start.30 = (bf16[2,2,192,1280]{3,2,1,0:T(8,128)(2,1)S(1)}, bf16[2,2,192,1280]{3,2,1,0:T(8,128)(2,1)S(1)}, u32[]{:S(2)}, u32[]{:S(2)}) collective-permute-start(bf16[2,2,192,1280]{3,2,1,0:T(8,128)(2,1)S(1)} %get-tuple-element.99), channel_id=1, source_target_pairs={{0,1},{1,0},{2,3},{3,2},{4,5},{5,4},{6,7},{7,6},{8,9},{9,8},{10,11... | collective-permute-start | bytes 5898248 | tf_op jit(solution)/shard_map/ppermute | solution.py:552
  189.1 3.6 collective-permute-done.30
  193.3 2.5 collective-permute-start.31
  198.3 2.7 collective-permute-start.33
  203.5 2.7 collective-permute-start.35
  206.2 9.0 %upstream.2.refs_2_ = f32[2,1536,768]{2,1,0:T(8,128)S(1)} custom-call(bf16[2,1536,1280]{2,1,0:T(8,128)(2,1)S(1)} %bitcast.45, bf16[2,768,4096]{2,1,0:T(8,128)(2,1)} %refs_1_.5), custom_call_target="tpu_custom_call" | custom-call | flops 94371840 | bytes 2359296 | tf_op jit(solution)/shard_map/upstream/pallas_call | solution.py:367
  215.2 2.7 collective-permute-done.31
  218.8 2.6 collective-permute-start.37
  223.2 2.7 collective-permute-start.39
  232.4 20.3 %select.14 = (bf16[2,1536,1536]{2,1,0:T(8,128)(2,1)}, bf16[2,2,192,1536]{3,2,1,0:T(8,128)(2,1)S(1)}, bf16[2,2,192,1536]{3,2,1,0:T(8,128)(2,1)}) custom-call(s32[64]{0:T(128)S(1)} %dynamic-slice_bitcast_fusion.order_ref, bf16[2,1536,128]{2,1,0:T(8,128)(2,1)S(1)} %copy-done.8, bf16[2,768,1536]{2,1,0:T(8,128)(2,1)} %copy-done.19, ...), custom_call_target="tpu_custom_call" | custom-call | flops 14495514624 | bytes 30020096 | tf_op jit(solution)/shard_map/select/pallas_call | solution.py:261
  252.8 2.4 collective-permute-start.40
  255.2 4.2 %collective-permute-done.40 = bf16[2,2,192,1536]{3,2,1,0:T(8,128)(2,1)S(1)} collective-permute-done((bf16[2,2,192,1536]{3,2,1,0:T(8,128)(2,1)S(1)}, bf16[2,2,192,1536]{3,2,1,0:T(8,128)(2,1)S(1)}, u32[]{:S(2)}, u32[]{:S(2)}) %collective-permute-start.40) | collective-permute-done | bytes 2359328 | tf_op jit(solution)/shard_map/ppermute | solution.py:552
  259.4 2.6 add_convert_fusion
  262.1 2.5 collective-permute-start.41
  267.0 2.7 collective-permute-start.43
  272.1 3.5 collective-permute-start.45
  275.5 11.0 %upstream.3.refs_2_ = f32[2,1536,768]{2,1,0:T(8,128)S(1)} custom-call(bf16[2,1536,1536]{2,1,0:T(8,128)(2,1)S(1)} %copy-done.1, bf16[2,768,4096]{2,1,0:T(8,128)(2,1)} %refs_1_.5, f32[2,1536,768]{2,1,0:T(8,128)S(1)} %upstream.2.refs_2_), custom_call_target="tpu_custom_call", output_to_operand_aliasing={{}: (2, {})} | custom-call | flops 113246208 | bytes 2359296 | tf_op jit(solution)/shard_map/upstream/pallas_call | solution.py:367
  286.5 4.3 %collective-permute-done.41 = bf16[2,192,1536]{2,1,0:T(8,128)(2,1)S(1)} collective-permute-done((bf16[2,192,1536]{2,1,0:T(8,128)(2,1)S(1)}, bf16[2,192,1536]{2,1,0:T(8,128)(2,1)S(1)}, u32[]{:S(2)}, u32[]{:S(2)}) %collective-permute-start.41) | collective-permute-done | bytes 1179680 | tf_op jit(solution)/shard_map/ppermute | solution.py:554
  295.4 2.3 copy-done.21
  302.1 19.5 %select.15 = (bf16[2,1536,1280]{2,1,0:T(8,128)(2,1)}, bf16[2,2,192,1280]{3,2,1,0:T(8,128)(2,1)S(1)}, bf16[2,2,192,1280]{3,2,1,0:T(8,128)(2,1)S(1)}) custom-call(s32[64]{0:T(128)S(1)} %dynamic-slice_bitcast_fusion.order_ref, bf16[2,1536,128]{2,1,0:T(8,128)(2,1)S(1)} %copy-done.9, bf16[2,768,1536]{2,1,0:T(8,128)(2,1)S(1)} %copy-done.21, ...), custom_call_target="tpu_custom_call" | custom-call | flops 12079595520 | bytes 26350080 | tf_op jit(solution)/shard_map/select/pallas_call | solution.py:261
  322.9 3.6 collective-permute-done.46
  328.1 2.4 collective-permute-start.47
  330.5 2.7 fusion.2
  334.5 2.3 copy-done.3
  336.9 12.4 %finish.1 = (bf16[2,1536,768]{2,1,0:T(8,128)(2,1)S(1)}, f32[2,32,128]{2,1,0:T(8,128)S(1)}) custom-call(bf16[2,1536,1280]{2,1,0:T(8,128)(2,1)S(1)} %bitcast.47, bf16[2,768,4096]{2,1,0:T(8,128)(2,1)} %refs_1_.5, f32[2,1536,768]{2,1,0:T(8,128)} %copy-done, bf16[2,1536,768]{2,1,0:T(8,128)(2,1)S(1)} %copy-done.3, f32[2,1536,128]{2,1,0:T(8,128)S(1)} %get-tuple-element.140.refs_4_, ...), custom_call_target="tpu_custom_call" | custom-call | flops 94371840 | bytes 2359296 | tf_op jit(solution)/shard_map/finish/pallas_call | solution.py:367
  352.1 5.6 %all-to-all-start.1 = ((f32[32,2,128]{2,1,0:T(2,128)}), f32[32,2,128]{2,1,0:T(2,128)S(1)}, u32[]{:S(2)}, u32[]{:S(2)}) async-start(f32[32,2,128]{2,1,0:T(2,128)} %copy.28), calls=%async_computation.1 | async-start | bytes 65536 | tf_op jit(solution)/shard_map/all_to_all | solution.py:570
  357.7 2.3 copy-done.5
  360.1 8.3 %in_slot_order.1 = bf16[1,2,1536,768]{3,2,1,0:T(8,128)(2,1)} custom-call(s32[64]{0:T(128)S(1)} %reshape.30.base_ref, s32[64]{0:T(128)S(1)} %reshape.31.lead_ref, s32[64]{0:T(128)S(1)} %convert_element_type.107.count_ref, bf16[2,1536,768]{2,1,0:T(8,128)(2,1)S(1)} %copy-done.5), custom_call_target="tpu_custom_call" | custom-call | flops 1000000000 | bytes 12000000 | tf_op jit(solution)/shard_map/in_slot_order/pallas_call | solution.py:410
  (242 shorter events, 85.1 us)
Async XLA Ops:
  1.6 9.0 %collective-permute-start = (bf16[128,1280]{1,0:T(8,128)(2,1)S(1)}, bf16[128,1280]{1,0:T(8,128)(2,1)S(1)}, u32[]{:S(2)}, u32[]{:S(2)}) collective-permute-start(bf16[128,1280]{1,0:T(8,128)(2,1)S(1)} %concatenate.20), channel_id=1, source_target_pairs={{0,16},{4,20},{8,24},{12,28},{16,0},{20,4},{24,8},{28,12},{32,48},... | collective-permute-start | bytes 983048 | tf_op jit(solution)/shard_map/ppermute | solution.py:51
  10.7 20.3 %collective-permute-start.1 = (bf16[256,640]{1,0:T(8,128)(2,1)S(1)}, bf16[256,640]{1,0:T(8,128)(2,1)S(1)}, u32[]{:S(2)}, u32[]{:S(2)}) collective-permute-start(bf16[256,640]{1,0:T(8,128)(2,1)S(1)} %get-tuple-element.152.refs_0_), channel_id=1, source_target_pairs={{0,32},{4,36},{8,40},{12,44},{16,48},{20,52},{24,56},{28,60},{32,6... | collective-permute-start | bytes 983048 | tf_op jit(solution)/shard_map/ppermute | solution.py:51
  12.9 18.6 %collective-permute-start.2 = (bf16[256,640]{1,0:T(8,128)(2,1)S(1)}, bf16[256,640]{1,0:T(8,128)(2,1)S(1)}, u32[]{:S(2)}, u32[]{:S(2)}) collective-permute-start(bf16[256,640]{1,0:T(8,128)(2,1)S(1)} %get-tuple-element.152.refs_0_), channel_id=1, source_target_pairs={{0,96},{4,100},{8,104},{12,108},{16,112},{20,116},{24,120},{28,124... | collective-permute-start | bytes 983048 | tf_op jit(solution)/shard_map/ppermute | solution.py:51
  15.1 18.8 %collective-permute-start.5 = (bf16[256,640]{1,0:T(8,128)(2,1)S(1)}, bf16[256,640]{1,0:T(8,128)(2,1)S(1)}, u32[]{:S(2)}, u32[]{:S(2)}) collective-permute-start(bf16[256,640]{1,0:T(8,128)(2,1)S(1)} %get-tuple-element.151.refs_5_), channel_id=1, source_target_pairs={{0,4},{4,8},{8,12},{12,0},{16,20},{20,24},{24,28},{28,16},{32,36},... | collective-permute-start | bytes 983048 | tf_op jit(solution)/shard_map/ppermute | solution.py:51
  16.4 17.9 %collective-permute-start.6 = (bf16[256,640]{1,0:T(8,128)(2,1)S(1)}, bf16[256,640]{1,0:T(8,128)(2,1)S(1)}, u32[]{:S(2)}, u32[]{:S(2)}) collective-permute-start(bf16[256,640]{1,0:T(8,128)(2,1)S(1)} %get-tuple-element.151.refs_5_), channel_id=1, source_target_pairs={{0,12},{4,0},{8,4},{12,8},{16,28},{20,16},{24,20},{28,24},{32,44},... | collective-permute-start | bytes 983048 | tf_op jit(solution)/shard_map/ppermute | solution.py:51
  18.5 12.4 %all-to-all-start = ((bf16[32,2,128]{2,1,0:T(2,128)(2,1)}), bf16[32,2,128]{2,1,0:T(2,128)(2,1)S(1)}, u32[]{:S(2)}, u32[]{:S(2)}) async-start(bf16[32,2,128]{2,1,0:T(2,128)(2,1)} %bitcast.5), calls=%async_computation | async-start | bytes 32768 | tf_op jit(solution)/shard_map/all_to_all | solution.py:442
  31.0 6.4 %collective-permute-start.3 = (bf16[128,640]{1,0:T(8,128)(2,1)S(1)}, bf16[128,640]{1,0:T(8,128)(2,1)S(1)}, u32[]{:S(2)}, u32[]{:S(2)}) collective-permute-start(bf16[128,640]{1,0:T(8,128)(2,1)S(1)} %slice.141), channel_id=1, source_target_pairs={{0,32},{4,36},{8,40},{12,44},{16,48},{20,52},{24,56},{28,60},{32,6... | collective-permute-start | bytes 491528 | tf_op jit(solution)/shard_map/ppermute | solution.py:51
  31.5 6.0 %collective-permute-start.4 = (bf16[128,640]{1,0:T(8,128)(2,1)S(1)}, bf16[128,640]{1,0:T(8,128)(2,1)S(1)}, u32[]{:S(2)}, u32[]{:S(2)}) collective-permute-start(bf16[128,640]{1,0:T(8,128)(2,1)S(1)} %slice.142), channel_id=1, source_target_pairs={{0,96},{4,100},{8,104},{12,108},{16,112},{20,116},{24,120},{28,124... | collective-permute-start | bytes 491528 | tf_op jit(solution)/shard_map/ppermute | solution.py:51
  33.9 5.7 %collective-permute-start.7 = (bf16[128,640]{1,0:T(8,128)(2,1)S(1)}, bf16[128,640]{1,0:T(8,128)(2,1)S(1)}, u32[]{:S(2)}, u32[]{:S(2)}) collective-permute-start(bf16[128,640]{1,0:T(8,128)(2,1)S(1)} %slice.143), channel_id=1, source_target_pairs={{0,4},{4,8},{8,12},{12,0},{16,20},{20,24},{24,28},{28,16},{32,36},... | collective-permute-start | bytes 491528 | tf_op jit(solution)/shard_map/ppermute | solution.py:51
  41.2 20.4 %collective-permute-start.9 = (bf16[128,2816]{1,0:T(8,128)(2,1)}, bf16[128,2816]{1,0:T(8,128)(2,1)S(1)}, u32[]{:S(2)}, u32[]{:S(2)}) collective-permute-start(bf16[128,2816]{1,0:T(8,128)(2,1)} %pad_maximum_fusion.2), channel_id=1, source_target_pairs={{0,16},{4,20},{8,24},{12,28},{16,0},{20,4},{24,8},{28,12},{32,48},... | collective-permute-start | bytes 2162696 | tf_op jit(solution)/shard_map/ppermute | solution.py:51
  41.8 25.7 %collective-permute-start.18 = (bf16[1024,640]{1,0:T(8,128)(2,1)S(1)}, bf16[1024,640]{1,0:T(8,128)(2,1)S(1)}, u32[]{:S(2)}, u32[]{:S(2)}) collective-permute-start(bf16[1024,640]{1,0:T(8,128)(2,1)S(1)} %get-tuple-element.86.refs_0_), channel_id=1, source_target_pairs={{0,4},{4,8},{8,12},{12,0},{16,20},{20,24},{24,28},{28,16},{32,36},... | collective-permute-start | bytes 3932168 | tf_op jit(solution)/shard_map/ppermute | solution.py:51
  41.9 26.1 %collective-permute-start.19 = (bf16[1024,640]{1,0:T(8,128)(2,1)S(1)}, bf16[1024,640]{1,0:T(8,128)(2,1)S(1)}, u32[]{:S(2)}, u32[]{:S(2)}) collective-permute-start(bf16[1024,640]{1,0:T(8,128)(2,1)S(1)} %get-tuple-element.86.refs_0_), channel_id=1, source_target_pairs={{0,12},{4,0},{8,4},{12,8},{16,28},{20,16},{24,20},{28,24},{32,44},... | collective-permute-start | bytes 3932168 | tf_op jit(solution)/shard_map/ppermute | solution.py:51
  63.9 12.3 %collective-permute-start.10 = (bf16[256,1408]{1,0:T(8,128)(2,1)S(1)}, bf16[256,1408]{1,0:T(8,128)(2,1)S(1)}, u32[]{:S(2)}, u32[]{:S(2)}) collective-permute-start(bf16[256,1408]{1,0:T(8,128)(2,1)S(1)} %get-tuple-element.146.refs_0_), channel_id=1, source_target_pairs={{0,32},{4,36},{8,40},{12,44},{16,48},{20,52},{24,56},{28,60},{32,6... | collective-permute-start | bytes 2162696 | tf_op jit(solution)/shard_map/ppermute | solution.py:51
  63.9 41.0 %collective-permute-start.20 = (bf16[1024,640]{1,0:T(8,128)(2,1)S(1)}, bf16[1024,640]{1,0:T(8,128)(2,1)S(1)}, u32[]{:S(2)}, u32[]{:S(2)}) collective-permute-start(bf16[1024,640]{1,0:T(8,128)(2,1)S(1)} %get-tuple-element.91.refs_5_), channel_id=1, source_target_pairs={{0,32},{4,36},{8,40},{12,44},{16,48},{20,52},{24,56},{28,60},{32,6... | collective-permute-start | bytes 3932168 | tf_op jit(solution)/shard_map/ppermute | solution.py:51
  63.9 43.1 %collective-permute-start.21 = (bf16[1024,640]{1,0:T(8,128)(2,1)S(1)}, bf16[1024,640]{1,0:T(8,128)(2,1)S(1)}, u32[]{:S(2)}, u32[]{:S(2)}) collective-permute-start(bf16[1024,640]{1,0:T(8,128)(2,1)S(1)} %get-tuple-element.91.refs_5_), channel_id=1, source_target_pairs={{0,96},{4,100},{8,104},{12,108},{16,112},{20,116},{24,120},{28,124... | collective-permute-start | bytes 3932168 | tf_op jit(solution)/shard_map/ppermute | solution.py:51
  67.5 35.8 %collective-permute-start.11 = (bf16[256,1408]{1,0:T(8,128)(2,1)S(1)}, bf16[256,1408]{1,0:T(8,128)(2,1)S(1)}, u32[]{:S(2)}, u32[]{:S(2)}) collective-permute-start(bf16[256,1408]{1,0:T(8,128)(2,1)S(1)} %get-tuple-element.146.refs_0_), channel_id=1, source_target_pairs={{0,96},{4,100},{8,104},{12,108},{16,112},{20,116},{24,120},{28,124... | collective-permute-start | bytes 2162696 | tf_op jit(solution)/shard_map/ppermute | solution.py:51
  68.0 39.1 %collective-permute-start.14 = (bf16[256,1408]{1,0:T(8,128)(2,1)S(1)}, bf16[256,1408]{1,0:T(8,128)(2,1)S(1)}, u32[]{:S(2)}, u32[]{:S(2)}) collective-permute-start(bf16[256,1408]{1,0:T(8,128)(2,1)S(1)} %get-tuple-element.145.refs_5_), channel_id=1, source_target_pairs={{0,4},{4,8},{8,12},{12,0},{16,20},{20,24},{24,28},{28,16},{32,36},... | collective-permute-start | bytes 2162696 | tf_op jit(solution)/shard_map/ppermute | solution.py:51
  76.2 33.6 %collective-permute-start.15 = (bf16[256,1408]{1,0:T(8,128)(2,1)S(1)}, bf16[256,1408]{1,0:T(8,128)(2,1)S(1)}, u32[]{:S(2)}, u32[]{:S(2)}) collective-permute-start(bf16[256,1408]{1,0:T(8,128)(2,1)S(1)} %get-tuple-element.145.refs_5_), channel_id=1, source_target_pairs={{0,12},{4,0},{8,4},{12,8},{16,28},{20,16},{24,20},{28,24},{32,44},... | collective-permute-start | bytes 2162696 | tf_op jit(solution)/shard_map/ppermute | solution.py:51
  103.3 11.6 %collective-permute-start.12 = (bf16[128,1408]{1,0:T(8,128)(2,1)S(1)}, bf16[128,1408]{1,0:T(8,128)(2,1)S(1)}, u32[]{:S(2)}, u32[]{:S(2)}) collective-permute-start(bf16[128,1408]{1,0:T(8,128)(2,1)S(1)} %slice.149), channel_id=1, source_target_pairs={{0,32},{4,36},{8,40},{12,44},{16,48},{20,52},{24,56},{28,60},{32,6... | collective-permute-start | bytes 1081352 | tf_op jit(solution)/shard_map/ppermute | solution.py:51
  104.9 10.0 %collective-permute-start.13 = (bf16[128,1408]{1,0:T(8,128)(2,1)S(1)}, bf16[128,1408]{1,0:T(8,128)(2,1)S(1)}, u32[]{:S(2)}, u32[]{:S(2)}) collective-permute-start(bf16[128,1408]{1,0:T(8,128)(2,1)S(1)} %slice.150), channel_id=1, source_target_pairs={{0,96},{4,100},{8,104},{12,108},{16,112},{20,116},{24,120},{28,124... | collective-permute-start | bytes 1081352 | tf_op jit(solution)/shard_map/ppermute | solution.py:51
  107.0 19.8 %collective-permute-start.26 = (bf16[512,640]{1,0:T(8,128)(2,1)S(1)}, bf16[512,640]{1,0:T(8,128)(2,1)S(1)}, u32[]{:S(2)}, u32[]{:S(2)}) collective-permute-start(bf16[512,640]{1,0:T(8,128)(2,1)S(1)} %slice.153), channel_id=1, source_target_pairs={{0,4},{4,8},{8,12},{12,0},{16,20},{20,24},{24,28},{28,16},{32,36},... | collective-permute-start | bytes 1966088 | tf_op jit(solution)/shard_map/ppermute | solution.py:51
  107.1 22.4 %collective-permute-start.27 = (bf16[512,640]{1,0:T(8,128)(2,1)S(1)}, bf16[512,640]{1,0:T(8,128)(2,1)S(1)}, u32[]{:S(2)}, u32[]{:S(2)}) collective-permute-start(bf16[512,640]{1,0:T(8,128)(2,1)S(1)} %slice.154), channel_id=1, source_target_pairs={{0,12},{4,0},{8,4},{12,8},{16,28},{20,16},{24,20},{28,24},{32,44},... | collective-permute-start | bytes 1966088 | tf_op jit(solution)/shard_map/ppermute | solution.py:51
  109.8 21.3 %collective-permute-start.28 = (bf16[512,640]{1,0:T(8,128)(2,1)S(1)}, bf16[512,640]{1,0:T(8,128)(2,1)S(1)}, u32[]{:S(2)}, u32[]{:S(2)}) collective-permute-start(bf16[512,640]{1,0:T(8,128)(2,1)S(1)} %slice.155), channel_id=1, source_target_pairs={{0,32},{4,36},{8,40},{12,44},{16,48},{20,52},{24,56},{28,60},{32,6... | collective-permute-start | bytes 1966088 | tf_op jit(solution)/shard_map/ppermute | solution.py:51
  114.9 7.8 %collective-permute-start.16 = (bf16[128,1408]{1,0:T(8,128)(2,1)S(1)}, bf16[128,1408]{1,0:T(8,128)(2,1)S(1)}, u32[]{:S(2)}, u32[]{:S(2)}) collective-permute-start(bf16[128,1408]{1,0:T(8,128)(2,1)S(1)} %slice.151), channel_id=1, source_target_pairs={{0,4},{4,8},{8,12},{12,0},{16,20},{20,24},{24,28},{28,16},{32,36},... | collective-permute-start | bytes 1081352 | tf_op jit(solution)/shard_map/ppermute | solution.py:51
  114.9 8.4 %collective-permute-start.17 = (bf16[128,1408]{1,0:T(8,128)(2,1)S(1)}, bf16[128,1408]{1,0:T(8,128)(2,1)S(1)}, u32[]{:S(2)}, u32[]{:S(2)}) collective-permute-start(bf16[128,1408]{1,0:T(8,128)(2,1)S(1)} %slice.152), channel_id=1, source_target_pairs={{0,12},{4,0},{8,4},{12,8},{16,28},{20,16},{24,20},{28,24},{32,44},... | collective-permute-start | bytes 1081352 | tf_op jit(solution)/shard_map/ppermute | solution.py:51
  122.7 11.9 %collective-permute-start.29 = (bf16[512,640]{1,0:T(8,128)(2,1)}, bf16[512,640]{1,0:T(8,128)(2,1)}, u32[]{:S(2)}, u32[]{:S(2)}) collective-permute-start(bf16[512,640]{1,0:T(8,128)(2,1)} %slice.156), channel_id=1, source_target_pairs={{0,96},{4,100},{8,104},{12,108},{16,112},{20,116},{24,120},{28,124... | collective-permute-start | bytes 1966088 | tf_op jit(solution)/shard_map/ppermute | solution.py:51
  126.7 40.0 %collective-permute-start.22 = (bf16[1024,768]{1,0:T(8,128)(2,1)}, bf16[1024,768]{1,0:T(8,128)(2,1)}, u32[]{:S(2)}, u32[]{:S(2)}) collective-permute-start(bf16[1024,768]{1,0:T(8,128)(2,1)} %get-tuple-element.103.refs_0_), channel_id=1, source_target_pairs={{0,4},{4,8},{8,12},{12,0},{16,20},{20,24},{24,28},{28,16},{32,36},... | collective-permute-start | bytes 4718600 | tf_op jit(solution)/shard_map/ppermute | solution.py:51
  126.8 39.9 %collective-permute-start.23 = (bf16[1024,768]{1,0:T(8,128)(2,1)}, bf16[1024,768]{1,0:T(8,128)(2,1)}, u32[]{:S(2)}, u32[]{:S(2)}) collective-permute-start(bf16[1024,768]{1,0:T(8,128)(2,1)} %get-tuple-element.103.refs_0_), channel_id=1, source_target_pairs={{0,12},{4,0},{8,4},{12,8},{16,28},{20,16},{24,20},{28,24},{32,44},... | collective-permute-start | bytes 4718600 | tf_op jit(solution)/shard_map/ppermute | solution.py:51
  130.3 36.4 %collective-permute-start.24 = (bf16[1024,768]{1,0:T(8,128)(2,1)}, bf16[1024,768]{1,0:T(8,128)(2,1)}, u32[]{:S(2)}, u32[]{:S(2)}) collective-permute-start(bf16[1024,768]{1,0:T(8,128)(2,1)} %get-tuple-element.110.refs_5_), channel_id=1, source_target_pairs={{0,32},{4,36},{8,40},{12,44},{16,48},{20,52},{24,56},{28,60},{32,6... | collective-permute-start | bytes 4718600 | tf_op jit(solution)/shard_map/ppermute | solution.py:51
  132.0 34.7 %collective-permute-start.25 = (bf16[1024,768]{1,0:T(8,128)(2,1)}, bf16[1024,768]{1,0:T(8,128)(2,1)}, u32[]{:S(2)}, u32[]{:S(2)}) collective-permute-start(bf16[1024,768]{1,0:T(8,128)(2,1)} %get-tuple-element.110.refs_5_), channel_id=1, source_target_pairs={{0,96},{4,100},{8,104},{12,108},{16,112},{20,116},{24,120},{28,124... | collective-permute-start | bytes 4718600 | tf_op jit(solution)/shard_map/ppermute | solution.py:51
  166.7 26.0 %collective-permute-start.30 = (bf16[2,2,192,1280]{3,2,1,0:T(8,128)(2,1)S(1)}, bf16[2,2,192,1280]{3,2,1,0:T(8,128)(2,1)S(1)}, u32[]{:S(2)}, u32[]{:S(2)}) collective-permute-start(bf16[2,2,192,1280]{3,2,1,0:T(8,128)(2,1)S(1)} %get-tuple-element.99), channel_id=1, source_target_pairs={{0,1},{1,0},{2,3},{3,2},{4,5},{5,4},{6,7},{7,6},{8,9},{9,8},{10,11... | collective-permute-start | bytes 5898248 | tf_op jit(solution)/shard_map/ppermute | solution.py:552
  193.3 24.6 %collective-permute-start.31 = (bf16[2,192,1280]{2,1,0:T(8,128)(2,1)S(1)}, bf16[2,192,1280]{2,1,0:T(8,128)(2,1)S(1)}, u32[]{:S(2)}, u32[]{:S(2)}) collective-permute-start(bf16[2,192,1280]{2,1,0:T(8,128)(2,1)S(1)} %slice_bitcast_fusion.5), channel_id=1, source_target_pairs={{0,2},{2,0},{1,3},{3,1},{4,6},{6,4},{5,7},{7,5},{8,10},{10,8},{9,1... | collective-permute-start | bytes 2949128 | tf_op jit(solution)/shard_map/ppermute | solution.py:554
  197.0 20.8 %collective-permute-start.32 = (bf16[512,768]{1,0:T(8,128)(2,1)S(1)}, bf16[512,768]{1,0:T(8,128)(2,1)S(1)}, u32[]{:S(2)}, u32[]{:S(2)}) collective-permute-start(bf16[512,768]{1,0:T(8,128)(2,1)S(1)} %slice.126), channel_id=1, source_target_pairs={{0,4},{4,8},{8,12},{12,0},{16,20},{20,24},{24,28},{28,16},{32,36},... | collective-permute-start | bytes 2359304 | tf_op jit(solution)/shard_map/ppermute | solution.py:51
  198.3 23.1 %collective-permute-start.33 = (bf16[512,768]{1,0:T(8,128)(2,1)S(1)}, bf16[512,768]{1,0:T(8,128)(2,1)S(1)}, u32[]{:S(2)}, u32[]{:S(2)}) collective-permute-start(bf16[512,768]{1,0:T(8,128)(2,1)S(1)} %slice.127), channel_id=1, source_target_pairs={{0,12},{4,0},{8,4},{12,8},{16,28},{20,16},{24,20},{28,24},{32,44},... | collective-permute-start | bytes 2359304 | tf_op jit(solution)/shard_map/ppermute | solution.py:51
  202.2 20.1 %collective-permute-start.34 = (bf16[512,768]{1,0:T(8,128)(2,1)S(1)}, bf16[512,768]{1,0:T(8,128)(2,1)S(1)}, u32[]{:S(2)}, u32[]{:S(2)}) collective-permute-start(bf16[512,768]{1,0:T(8,128)(2,1)S(1)} %slice.128), channel_id=1, source_target_pairs={{0,32},{4,36},{8,40},{12,44},{16,48},{20,52},{24,56},{28,60},{32,6... | collective-permute-start | bytes 2359304 | tf_op jit(solution)/shard_map/ppermute | solution.py:51
  203.5 22.4 %collective-permute-start.35 = (bf16[512,768]{1,0:T(8,128)(2,1)S(1)}, bf16[512,768]{1,0:T(8,128)(2,1)S(1)}, u32[]{:S(2)}, u32[]{:S(2)}) collective-permute-start(bf16[512,768]{1,0:T(8,128)(2,1)S(1)} %slice.129), channel_id=1, source_target_pairs={{0,96},{4,100},{8,104},{12,108},{16,112},{20,116},{24,120},{28,124... | collective-permute-start | bytes 2359304 | tf_op jit(solution)/shard_map/ppermute | solution.py:51
  217.8 34.9 %collective-permute-start.36 = (bf16[1024,640]{1,0:T(8,128)(2,1)}, bf16[1024,640]{1,0:T(8,128)(2,1)}, u32[]{:S(2)}, u32[]{:S(2)}) collective-permute-start(bf16[1024,640]{1,0:T(8,128)(2,1)} %get-tuple-element.121.refs_0_), channel_id=1, source_target_pairs={{0,4},{4,8},{8,12},{12,0},{16,20},{20,24},{24,28},{28,16},{32,36},... | collective-permute-start | bytes 3932168 | tf_op jit(solution)/shard_map/ppermute | solution.py:51
  218.8 34.0 %collective-permute-start.37 = (bf16[1024,640]{1,0:T(8,128)(2,1)}, bf16[1024,640]{1,0:T(8,128)(2,1)}, u32[]{:S(2)}, u32[]{:S(2)}) collective-permute-start(bf16[1024,640]{1,0:T(8,128)(2,1)} %get-tuple-element.121.refs_0_), channel_id=1, source_target_pairs={{0,12},{4,0},{8,4},{12,8},{16,28},{20,16},{24,20},{28,24},{32,44},... | collective-permute-start | bytes 3932168 | tf_op jit(solution)/shard_map/ppermute | solution.py:51
  222.3 30.5 %collective-permute-start.38 = (bf16[1024,640]{1,0:T(8,128)(2,1)}, bf16[1024,640]{1,0:T(8,128)(2,1)}, u32[]{:S(2)}, u32[]{:S(2)}) collective-permute-start(bf16[1024,640]{1,0:T(8,128)(2,1)} %get-tuple-element.128.refs_5_), channel_id=1, source_target_pairs={{0,32},{4,36},{8,40},{12,44},{16,48},{20,52},{24,56},{28,60},{32,6... | collective-permute-start | bytes 3932168 | tf_op jit(solution)/shard_map/ppermute | solution.py:51
  223.2 29.6 %collective-permute-start.39 = (bf16[1024,640]{1,0:T(8,128)(2,1)}, bf16[1024,640]{1,0:T(8,128)(2,1)}, u32[]{:S(2)}, u32[]{:S(2)}) collective-permute-start(bf16[1024,640]{1,0:T(8,128)(2,1)} %get-tuple-element.128.refs_5_), channel_id=1, source_target_pairs={{0,96},{4,100},{8,104},{12,108},{16,112},{20,116},{24,120},{28,124... | collective-permute-start | bytes 3932168 | tf_op jit(solution)/shard_map/ppermute | solution.py:51
  252.8 6.6 %collective-permute-start.40 = (bf16[2,2,192,1536]{3,2,1,0:T(8,128)(2,1)S(1)}, bf16[2,2,192,1536]{3,2,1,0:T(8,128)(2,1)S(1)}, u32[]{:S(2)}, u32[]{:S(2)}) collective-permute-start(bf16[2,2,192,1536]{3,2,1,0:T(8,128)(2,1)S(1)} %get-tuple-element.119), channel_id=1, source_target_pairs={{0,1},{1,0},{2,3},{3,2},{4,5},{5,4},{6,7},{7,6},{8,9},{9,8},{10,11... | collective-permute-start | bytes 7077896 | tf_op jit(solution)/shard_map/ppermute | solution.py:552
  262.1 28.8 %collective-permute-start.41 = (bf16[2,192,1536]{2,1,0:T(8,128)(2,1)S(1)}, bf16[2,192,1536]{2,1,0:T(8,128)(2,1)S(1)}, u32[]{:S(2)}, u32[]{:S(2)}) collective-permute-start(bf16[2,192,1536]{2,1,0:T(8,128)(2,1)S(1)} %slice_bitcast_fusion.1), channel_id=1, source_target_pairs={{0,2},{2,0},{1,3},{3,1},{4,6},{6,4},{5,7},{7,5},{8,10},{10,8},{9,1... | collective-permute-start | bytes 3538952 | tf_op jit(solution)/shard_map/ppermute | solution.py:554
  265.7 25.1 %collective-permute-start.42 = (bf16[512,640]{1,0:T(8,128)(2,1)S(1)}, bf16[512,640]{1,0:T(8,128)(2,1)S(1)}, u32[]{:S(2)}, u32[]{:S(2)}) collective-permute-start(bf16[512,640]{1,0:T(8,128)(2,1)S(1)} %slice.131), channel_id=1, source_target_pairs={{0,4},{4,8},{8,12},{12,0},{16,20},{20,24},{24,28},{28,16},{32,36},... | collective-permute-start | bytes 1966088 | tf_op jit(solution)/shard_map/ppermute | solution.py:51
  267.0 24.7 %collective-permute-start.43 = (bf16[512,640]{1,0:T(8,128)(2,1)S(1)}, bf16[512,640]{1,0:T(8,128)(2,1)S(1)}, u32[]{:S(2)}, u32[]{:S(2)}) collective-permute-start(bf16[512,640]{1,0:T(8,128)(2,1)S(1)} %slice.132), channel_id=1, source_target_pairs={{0,12},{4,0},{8,4},{12,8},{16,28},{20,16},{24,20},{28,24},{32,44},... | collective-permute-start | bytes 1966088 | tf_op jit(solution)/shard_map/ppermute | solution.py:51
  270.8 21.7 %collective-permute-start.44 = (bf16[512,640]{1,0:T(8,128)(2,1)S(1)}, bf16[512,640]{1,0:T(8,128)(2,1)S(1)}, u32[]{:S(2)}, u32[]{:S(2)}) collective-permute-start(bf16[512,640]{1,0:T(8,128)(2,1)S(1)} %slice.133), channel_id=1, source_target_pairs={{0,32},{4,36},{8,40},{12,44},{16,48},{20,52},{24,56},{28,60},{32,6... | collective-permute-start | bytes 1966088 | tf_op jit(solution)/shard_map/ppermute | solution.py:51
  272.1 21.4 %collective-permute-start.45 = (bf16[512,640]{1,0:T(8,128)(2,1)S(1)}, bf16[512,640]{1,0:T(8,128)(2,1)S(1)}, u32[]{:S(2)}, u32[]{:S(2)}) collective-permute-start(bf16[512,640]{1,0:T(8,128)(2,1)S(1)} %slice.134), channel_id=1, source_target_pairs={{0,96},{4,100},{8,104},{12,108},{16,112},{20,116},{24,120},{28,124... | collective-permute-start | bytes 1966088 | tf_op jit(solution)/shard_map/ppermute | solution.py:51
  328.1 40.9 %collective-permute-start.47 = (bf16[2,192,1280]{2,1,0:T(8,128)(2,1)}, bf16[2,192,1280]{2,1,0:T(8,128)(2,1)}, u32[]{:S(2)}, u32[]{:S(2)}) collective-permute-start(bf16[2,192,1280]{2,1,0:T(8,128)(2,1)} %slice_bitcast_fusion.2), channel_id=1, source_target_pairs={{0,2},{2,0},{1,3},{3,1},{4,6},{6,4},{5,7},{7,5},{8,10},{10,8},{9,1... | collective-permute-start | bytes 2949128 | tf_op jit(solution)/shard_map/ppermute | solution.py:554
  352.1 16.2 %all-to-all-start.1 = ((f32[32,2,128]{2,1,0:T(2,128)}), f32[32,2,128]{2,1,0:T(2,128)S(1)}, u32[]{:S(2)}, u32[]{:S(2)}) async-start(f32[32,2,128]{2,1,0:T(2,128)} %copy.28), calls=%async_computation.1 | async-start | bytes 65536 | tf_op jit(solution)/shard_map/all_to_all | solution.py:570
  (63 other events, 442.2 us)

commit v2 on v1

--- a/solution.py
+++ b/solution.py
@@ -17,10 +17,10 @@
 PICK = EXP * MOST
 WINDOW = 64
 SHARE = HID // 4
-STAGES = (1280, 1536, 1280)
-GROUPS = ((0,), (1, 2))
+STAGES = (2304, 1792)
 MIB = 1024 * 1024
 CROSSED_LAG = 1
+LIMIT_HALVE = 60
 
 NZ, NX, NY = 4, 2, 4
 
@@ -137,47 +137,102 @@
             jax.ShapeDtypeStruct((EXP, CAP, TOK), jnp.float32),
             jax.ShapeDtypeStruct((EXP, CAP, TOK), jnp.bfloat16),
         ],
-        compiler_params=pltpu.CompilerParams(vmem_limit_bytes=36 * MIB),
+        compiler_params=pltpu.CompilerParams(vmem_limit_bytes=60 * MIB),
         cost_estimate=pl.CostEstimate(flops=10**9, bytes_accessed=16 * 10**6, transcendentals=0),
         name="prepare",
     )(base, lead, count, place, rank, gate, saved)
 
 
-def join_kernel(spans, *refs):
-    pieces, outs, sems = refs[:10], refs[10:-1], refs[-1]
-    copies = []
+def join_kernel(spans, staged, *refs):
+    pieces, outs = refs[:16], refs[16 : 16 + 2 * len(spans)]
+    rest = refs[16 + 2 * len(spans) :]
+    sems = rest[-1]
+    targets = rest[: len(outs)] if staged else outs
+    groups = []
     for number, (low, high) in enumerate(spans):
         for side in range(2):
             first = 0
-            for part in range(5):
-                piece = pieces[side * 5 + part]
+            group = []
+            for part in range(8):
+                piece = pieces[side * 8 + part]
                 size = piece.shape[0]
                 copy = pltpu.make_async_copy(
                     piece.at[:, pl.ds(low, high - low)],
-                    outs[number * 2 + side].at[pl.ds(first, size), :],
-                    sems.at[len(copies)],
+                    targets[number * 2 + side].at[pl.ds(first, size), :],
+                    sems.at[len(groups) * 8 + part],
                 )
                 copy.start()
-                copies.append(copy)
+                group.append(copy)
                 first += size
-    for copy in copies:
+            groups.append(group)
+    leaving = []
+    for number, group in enumerate(groups):
+        for copy in group:
+            copy.wait()
+        if staged:
+            copy = pltpu.make_async_copy(
+                targets[number], outs[number], sems.at[8 * len(groups) + number]
+            )
+            copy.start()
+            leaving.append(copy)
+    for copy in leaving:
         copy.wait()
 
 
-def join(pieces, spans):
+def join(pieces, spans, staged):
     shapes = []
     for low, high in spans:
-        shapes += [jax.ShapeDtypeStruct((1024, high - low), jnp.bfloat16)] * 2
+        shapes += [(1024, high - low)] * 2
+    place = pl.BlockSpec(memory_space=pl.ANY if staged else pltpu.VMEM)
     return pl.pallas_call(
-        functools.partial(join_kernel, spans),
-        in_specs=[pl.BlockSpec(memory_space=pl.ANY)] * 10,
-        out_specs=[pl.BlockSpec(memory_space=pltpu.VMEM)] * len(shapes),
-        out_shape=shapes,
-        scratch_shapes=[pltpu.SemaphoreType.DMA((10 * len(spans),))],
+        functools.partial(join_kernel, spans, staged),
+        in_specs=[pl.BlockSpec(memory_space=pl.ANY)] * 16,
+        out_specs=[place] * len(shapes),
+        out_shape=[jax.ShapeDtypeStruct(shape, jnp.bfloat16) for shape in shapes],
+        scratch_shapes=[pltpu.VMEM(shape, jnp.bfloat16) for shape in shapes if staged]
+        + [pltpu.SemaphoreType.DMA((9 * len(shapes),))],
         compiler_params=pltpu.CompilerParams(vmem_limit_bytes=16 * MIB),
         cost_estimate=pl.CostEstimate(flops=0, bytes_accessed=2 * MIB, transcendentals=0),
         name="join",
     )(*pieces)
+
+
+def halve_kernel(*refs):
+    values, outs, held, sems = refs[:4], refs[4:8], refs[8], refs[9]
+    size = held.shape[1]
+    copies = []
+    for i in range(4):
+        copy = pltpu.make_async_copy(
+            values[i].at[pl.ds((i % 2) * size, size), :], held.at[i], sems.at[i]
+        )
+        copy.start()
+        copies.append(copy)
+    leaving = []
+    for i in range(4):
+        copies[i].wait()
+        copy = pltpu.make_async_copy(held.at[i], outs[i], sems.at[4 + i])
+        copy.start()
+        leaving.append(copy)
+    for copy in leaving:
+        copy.wait()
+
+
+def halve(values):
+    rows, width = values[0].shape
+    anywhere = pl.BlockSpec(memory_space=pl.ANY)
+    return pl.pallas_call(
+        halve_kernel,
+        in_specs=[anywhere] * 4,
+        out_specs=[anywhere] * 4,
+        out_shape=[jax.ShapeDtypeStruct((rows // 2, width), jnp.bfloat16)] * 4,
+        scratch_shapes=[
+            pltpu.VMEM((4, rows // 2, width), jnp.bfloat16),
+            pltpu.SemaphoreType.DMA((8,)),
+        ],
+        compiler_params=pltpu.CompilerParams(vmem_limit_bytes=LIMIT_HALVE * MIB),
+        cost_estimate=pl.CostEstimate(flops=0, bytes_accessed=2 * MIB, transcendentals=0),
+        name="halve",
+    )(*values)
 
 
 def select_kernel(width, order_ref, pick_ref, scaled_hbm, *refs):
@@ -276,7 +331,7 @@
             pltpu.SemaphoreType.DMA((11,)),
             pltpu.SemaphoreType.DMA((10,)),
         ],
-        compiler_params=pltpu.CompilerParams(vmem_limit_bytes=need + 8 * MIB),
+        compiler_params=pltpu.CompilerParams(vmem_limit_bytes=60 * MIB),
         cost_estimate=pl.CostEstimate(
             flops=2 * EXP * CAP * HID * width * 2,
             bytes_accessed=SOURCES * TOK * width * 2 + EXP * CAP * width * 2 + 8 * 10**6,
@@ -375,7 +430,7 @@
             pltpu.SemaphoreType.DMA((EXP,)),
         ],
         input_output_aliases=aliases,
-        compiler_params=pltpu.CompilerParams(vmem_limit_bytes=32 * MIB),
+        compiler_params=pltpu.CompilerParams(vmem_limit_bytes=60 * MIB),
         cost_estimate=pl.CostEstimate(
             flops=2 * EXP * CAP * HID * width // 64,
             bytes_accessed=EXP * CAP * HID,
@@ -416,7 +471,7 @@
             out_specs=pl.BlockSpec((1, 1, CAP, HID), lambda e, *_: (0, e, 0, 0)),
         ),
         out_shape=jax.ShapeDtypeStruct((1, EXP, CAP, HID), jnp.bfloat16),
-        compiler_params=pltpu.CompilerParams(vmem_limit_bytes=24 * MIB),
+        compiler_params=pltpu.CompilerParams(vmem_limit_bytes=60 * MIB),
         cost_estimate=pl.CostEstimate(flops=10**9, bytes_accessed=12 * 10**6, transcendentals=0),
         name="in_slot_order",
     )(base, lead, count, hidden)
@@ -426,12 +481,11 @@
     return send(block, up), send(block, down)
 
 
-def ring_second(from_up, from_down, up, down):
-    half = from_up.shape[0] // 2
-    return send(from_up[:half], up), send(from_down[half:], down)
-
-
-def gate_tables(gates, index):
+def ring_second(ends, up, down):
+    return send(ends[0], up), send(ends[1], down)
+
+
+def send_gates(gates, index):
     index_t = index[0].T
     gates_t = gates[0].T
     experts = jnp.arange(SOURCES * EXP, dtype=jnp.int32)[None, :, None]
@@ -439,7 +493,10 @@
         jnp.where(index_t[:, None, :] == experts, gates_t[:, None, :].astype(jnp.float32), 0.0), axis=0
     )
     dense = dense.astype(jnp.bfloat16).reshape(SOURCES, EXP, TOK)
-    gate = lax.all_to_all(dense, "expert", split_axis=0, concat_axis=0, tiled=True)
+    return lax.all_to_all(dense, "expert", split_axis=0, concat_axis=0, tiled=True)
+
+
+def gate_tables(gate):
     present = gate > 0
     ones = present.astype(jnp.float32)
     earlier_token = jnp.triu(jnp.ones((TOK, TOK), jnp.float32), 1)
@@ -471,41 +528,37 @@
     count = len(STAGES)
     starts = [sum(STAGES[:s]) for s in range(count)]
 
-    def first_swap(group, hold):
-        lefts, rights, spans = [], [], []
-        at = 0
-        for s in group:
-            half = STAGES[s] // 2
-            lefts.append(tokens[:, starts[s] : starts[s] + half])
-            rights.append(tokens[:, starts[s] + half : starts[s] + 2 * half])
-            spans.append((at, at + half))
-            at += half
-        mine = jnp.concatenate(lefts + rights, axis=1)
-        if hold is not None:
-            mine = after(mine, *hold)
-        met = send(mine, X_SWAP)
-        return jnp.concatenate([mine, met], axis=0), at, spans, group, met
-
-    def first_rings(swapped, ready):
-        both, at, spans, group, _ = swapped
-        if ready is not None:
-            both = after(both, ready)
-        a, b = both[:, :at], both[:, at:]
-        a_up, a_down = ring_first(a, Z_UP, Z_DOWN)
-        b_up, b_down = ring_first(b, Y_UP, Y_DOWN)
-        a_far = ring_second(a_up, a_down, Z_UP, Z_DOWN)
-        b_far = ring_second(b_up, b_down, Y_UP, Y_DOWN)
-        pieces = (a, a_up, a_down, *a_far, b, b_up, b_down, *b_far)
-        joined = join(pieces, tuple(spans))
-        return {s: joined[2 * i : 2 * i + 2] for i, s in enumerate(group)}
-
-    swapped = first_swap(GROUPS[0], None)
-    gate, rank, base, lead, counts = gate_tables(after(gates, swapped[4]), expert_index)
-    wide = first_rings(swapped, None)
-    swapped = first_swap(GROUPS[1], (wide[0][0],))
+    halves = [width // 2 for width in STAGES]
+    spans = [(sum(halves[:s]), sum(halves[: s + 1])) for s in range(count)]
+
+    def split(rows):
+        lefts = [rows[:, starts[s] : starts[s] + halves[s]] for s in range(count)]
+        rights = [rows[:, starts[s] + halves[s] : starts[s] + STAGES[s]] for s in range(count)]
+        return jnp.concatenate(lefts, axis=1), jnp.concatenate(rights, axis=1)
+
+    met = send(tokens, X_SWAP)
+    sides = []
+    mine = split(tokens)
+    links = ((Z_UP, Z_DOWN), (Y_UP, Y_DOWN))
+    own_near = [ring_first(block, *link) for block, link in zip(mine, links)]
+    own_far = [send(near[0], link[0]) for near, link in zip(own_near, links)]
+    other = split(met)
+    other_near = [ring_first(block, *link) for block, link in zip(other, links)]
+    other_far = [send(near[1], link[1]) for near, link in zip(other_near, links)]
+    for side in range(2):
+        sides += [mine[side], other[side]]
+        for way in range(2):
+            sides += [own_near[side][way], other_near[side][way]]
+        sides += [own_far[side], other_far[side]]
+    gate = send_gates(after(gates, own_near[0][0]), expert_index)
+    wide = {0: join([after(piece, gate) for piece in sides], spans[:1], False)}
+    joined = join([after(piece, wide[0][0]) for piece in sides], spans[1:], True)
+    wide.update({s: joined[2 * s - 2 : 2 * s] for s in range(1, count)})
+    gate, rank, base, lead, counts = gate_tables(after(gate, wide[0][0]))
     scaled, padded, row_gate, pick = prepare(
-        base, lead, counts, place, after(rank, wide[0][0]), gate, saved_hidden
+        base, lead, counts, place, after(rank, joined[0]), gate, saved_hidden
     )
+
     total = None
     shares = []
     near = pair = None
@@ -523,14 +576,11 @@
 
     def second_ring_second(near, hold):
         ends = [after(value, *hold) if hold else value for value in near]
-        return (
-            ring_second(ends[0], ends[1], Y_UP, Y_DOWN),
-            ring_second(ends[2], ends[3], Z_UP, Z_DOWN),
-        )
+        ends = halve(ends)
+        return ring_second(ends[:2], Y_UP, Y_DOWN), ring_second(ends[2:], Z_UP, Z_DOWN), ends
 
     (a, b), near = second_ring_first(0)
-    wide.update(first_rings(swapped, scaled))
-    far_a, far_b = second_ring_second(near, ())
+    far_a, far_b, _ = second_ring_second(near, (scaled,))
     for s in range(count):
         pieces = (a, near[0], near[1], *far_a, b, near[2], near[3], *far_b)
         last = s + 1 == count
@@ -550,23 +600,37 @@
         selected.append(go)
         leaving = after(go, *near) if not last else go
         met = lax.ppermute(leaving, "replica", CORE_SWAP)
-        pair = (met.astype(jnp.float32) + stay.astype(jnp.float32)).astype(jnp.bfloat16)
-        across = lax.ppermute(pair[1], "replica", XHI_SWAP)
-        shares.append(
-            (pair[0].astype(jnp.float32) + across.astype(jnp.float32)).astype(jnp.bfloat16)
-        )
         if not last:
-            far_a, far_b = second_ring_second(near, (go,))
+            next_far_a, next_far_b, ends = second_ring_second(near, (go,))
+        cuts = (0, STAGES[s]) if last else (0, STAGES[s] // 2, STAGES[s])
+        parts = []
+        for low, high in zip(cuts, cuts[1:]):
+            pair = (
+                met[1, :, :, low:high].astype(jnp.float32)
+                + stay[1, :, :, low:high].astype(jnp.float32)
+            ).astype(jnp.bfloat16)
+            across = lax.ppermute(after(pair, *parts), "replica", XHI_SWAP)
+            if not parts:
+                crossed.append(across)
+            parts.append(across)
+        shares.append((met[0], stay[0], parts))
+        if not last:
+            far_a, far_b = next_far_a, next_far_b
         if last:
             rows = after(rows, pair)
-        crossed.append(across)
         result = upstream(rows, down_weight, starts[s], total, (padded, row_gate, pick), last)
         if last:
             hidden, sums = result
         else:
             total = result
 
-    weight_grad = jnp.concatenate(shares, axis=2)
+    finished = []
+    for s, (met, stay, parts) in enumerate(shares):
+        parts = [after(part, sums) for part in parts] if s + 1 < count else parts
+        across = jnp.concatenate(parts, axis=2).astype(jnp.float32)
+        pair = met.astype(jnp.float32) + stay.astype(jnp.float32)
+        finished.append((pair + across).astype(jnp.bfloat16))
+    weight_grad = jnp.concatenate(finished, axis=2)
     back = lax.all_to_all(
         jnp.swapaxes(sums, 0, 1), "expert", split_axis=0, concat_axis=0, tiled=True
     ).reshape(SOURCES * EXP, TOK)

time: 374 us -> 308 us (0.82)
  local copies, waits for them, and re-layouts: 64.9 us -> 21.5 us
  starting transfers between devices: 99.1 us -> 62.8 us
  blocking collectives: 0 us -> 10.8 us
  Pallas kernels: 118 us -> 125 us
  waiting for transfers between devices: 75.5 us -> 68.8 us
    unnamed x122 -> x60, local copies, waits for them, and re-layouts: 48.1 us -> 14.6 us
    ppermute x42 -> x29, starting transfers between devices: 54.6 us -> 38.1 us  [send(): return lax.ppermute(value, 'expert', pairs)]
    ppermute x3 -> x2, starting transfers between devices: 26 us -> 11.1 us  [body(): met = lax.ppermute(leaving, 'replica', CORE_SWAP)]
    all_to_all x0 -> x1, blocking collectives: none -> 10.8 us  [send_gates(): lax.all_to_all(dense, 'expert', split_axis=0, concat_axis=0, tiled=True)]
    slice x23 -> x4, local copies, waits for them, and re-layouts: 12.8 us -> 2.27 us  [split(): rows[:, starts[s] + halves[s]:starts[s] + STAGES[s]]]
    ppermute x42 -> x29, waiting for transfers between devices: 50.2 us -> 60.1 us  [send(): return lax.ppermute(value, 'expert', pairs)]
    ppermute x3 -> x2, waiting for transfers between devices: 11.4 us -> 2.17 us  [body(): met = lax.ppermute(leaving, 'replica', CORE_SWAP)]
    pallas_call x3 -> x2, Pallas kernels: 59.5 us -> 51.1 us  [select(): pl.pallas_call(functools.partial(select_kernel, width), in_specs=[smem, v...]
  transfers between devices with their start and end apart: 50 -> 35, of which waited for: 13 -> 14; matrix products, arithmetic and copies ran while one was open for 6% -> 6% of each run, Pallas kernels for 26% -> 31%
where the time goes in v2:
time: 308 us; the launch traced here: 307 us
  Pallas kernels  125 us (41%)
  waiting for transfers between devices  68.8 us (22%)
  starting transfers between devices  62.8 us (20%)
  local copies, waits for them, and re-layouts  21.5 us (7%)
  other arithmetic  16.4 us (5%)
  blocking collectives  10.8 us (4%)
    ppermute x29, waiting for transfers between devices, send(): return lax.ppermute(value, 'expert', pairs)  60.1 us
    pallas_call x2, Pallas kernels, select(): pl.pallas_call(functools.partial(select_kernel, width), in_specs=[smem, v...  51.1 us
    ppermute x29, starting transfers between devices, send(): return lax.ppermute(value, 'expert', pairs)  38.1 us
    pallas_call x2, Pallas kernels, upstream(): pl.pallas_call(functools.partial(upstream_kernel, total is not None, last...  35.9 us
    pallas_call x1, Pallas kernels, prepare(): pl.pallas_call(prepare_kernel, grid_spec=pltpu.PrefetchScalarGridSpec(num...  16.9 us
    unnamed x60, local copies, waits for them, and re-layouts  14.6 us
    ppermute x2, starting transfers between devices, body(): met = lax.ppermute(leaving, 'replica', CORE_SWAP)  11.1 us
    all_to_all x1, blocking collectives, send_gates(): lax.all_to_all(dense, 'expert', split_axis=0, concat_axis=0, tiled=True)  10.8 us
  transfers between devices with their start and end apart: 35, of which 14 were waited for; matrix products, arithmetic and copies ran while one was open for 6% of the time, Pallas kernels for 31%

profile of v2, /device:TPU:1, one launch (start us, length us, event | category | flops | bytes accessed | tf_op | source)
XLA Modules:
  0.0 306.7 jit_solution(15019690454629927731)
XLA Ops:
  0.6 2.1 collective-permute-start.1
  5.0 1.7 collective-permute-start
  6.7 2.2 collective-permute-start.3
  9.0 1.4 collective-permute-start.7
  10.4 1.5 collective-permute-start.9
  11.9 8.3 %collective-permute-done.refs_2_ = bf16[128,2048]{1,0:T(8,128)(2,1)S(1)} collective-permute-done((bf16[128,2048]{1,0:T(8,128)(2,1)S(1)}, bf16[128,2048]{1,0:T(8,128)(2,1)S(1)}, u32[]{:S(2)}, u32[]{:S(2)}) %collective-permute-start) | collective-permute-done | bytes 524320 | tf_op jit(solution)/shard_map/ppermute | solution.py:51
  20.2 5.2 %collective-permute-done.1 = bf16[128,4096]{1,0:T(8,128)(2,1)S(1)} collective-permute-done((bf16[128,4096]{1,0:T(8,128)(2,1)}, bf16[128,4096]{1,0:T(8,128)(2,1)S(1)}, u32[]{:S(2)}, u32[]{:S(2)}) %collective-permute-start.1) | collective-permute-done | bytes 1048608 | tf_op jit(solution)/shard_map/ppermute | solution.py:51
  25.5 4.3 %collective-permute-start.4 = (bf16[128,2048]{1,0:T(8,128)(2,1)S(1)}, bf16[128,2048]{1,0:T(8,128)(2,1)S(1)}, u32[]{:S(2)}, u32[]{:S(2)}) collective-permute-start(bf16[128,2048]{1,0:T(8,128)(2,1)S(1)} %pad_maximum_fusion.2.refs_1_), channel_id=1, source_target_pairs={{0,96},{4,100},{8,104},{12,108},{16,112},{20,116},{24,120},{28,124... | collective-permute-start | bytes 1572872 | tf_op jit(solution)/shard_map/ppermute | solution.py:51
  29.8 2.8 collective-permute-start.10
  33.3 6.2 %collective-permute-done.4.refs_5_ = bf16[128,2048]{1,0:T(8,128)(2,1)S(1)} collective-permute-done((bf16[128,2048]{1,0:T(8,128)(2,1)S(1)}, bf16[128,2048]{1,0:T(8,128)(2,1)S(1)}, u32[]{:S(2)}, u32[]{:S(2)}) %collective-permute-start.4) | collective-permute-done | bytes 524320 | tf_op jit(solution)/shard_map/ppermute | solution.py:51
  39.4 3.4 %collective-permute-start.6 = (bf16[128,2048]{1,0:T(8,128)(2,1)S(1)}, bf16[128,2048]{1,0:T(8,128)(2,1)S(1)}, u32[]{:S(2)}, u32[]{:S(2)}) collective-permute-start(bf16[128,2048]{1,0:T(8,128)(2,1)S(1)} %collective-permute-done.4.refs_5_), channel_id=1, source_target_pairs={{0,96},{4,100},{8,104},{12,108},{16,112},{20,116},{24,120},{28,124... | collective-permute-start | bytes 1572872 | tf_op jit(solution)/shard_map/ppermute | solution.py:51
  42.8 2.7 collective-permute-start.12
  45.6 10.8 %all_to_all.10 = bf16[32,2,128]{2,1,0:T(2,128)(2,1)S(1)} all-to-all(bf16[32,2,128]{2,1,0:T(2,128)(2,1)S(1)} %bitcast.41), channel_id=1, replica_groups=mesh['expert'=32,'replica'=4] {'expert'}, dimensions={0} | all-to-all | bytes 32768 | tf_op jit(solution)/shard_map/all_to_all | solution.py:496
  56.5 3.1 %join.2 = (bf16[1024,1152]{1,0:T(8,128)(2,1)}, bf16[1024,1152]{1,0:T(8,128)(2,1)}) custom-call(bf16[128,2048]{1,0:T(8,128)(2,1)S(1)} %pad_maximum_fusion.1.refs_0_, bf16[128,2048]{1,0:T(8,128)(2,1)S(1)} %pad_maximum_fusion.2.refs_1_, bf16[128,2048]{1,0:T(8,128)(2,1)S(1)} %collective-permute-done.refs_2_, ...), custom_call_target="tpu_custom_call" | custom-call | bytes 2097152 | tf_op jit(solution)/shard_map/join/pallas_call | solution.py:187
  59.8 2.2 collective-permute-start.16
  81.8 16.9 %prepare.1 = (bf16[2,768,1536]{2,1,0:T(8,128)(2,1)}, bf16[2,1536,768]{2,1,0:T(8,128)(2,1)}, f32[2,1536,128]{2,1,0:T(8,128)}, bf16[2,1536,128]{2,1,0:T(8,128)(2,1)}) custom-call(s32[64]{0:T(128)} %reshape.42.base_ref, s32[64]{0:T(128)} %reshape.43.lead_ref, s32[64]{0:T(128)} %convert_element_type.114.count_ref, s32[2]{0:T(128)} %pad_add_fusion.place_ref, ...), custom_call_target="tpu_custom_call" | custom-call | flops 1000000000 | bytes 16000000 | tf_op jit(solution)/shard_map/prepare/pallas_call | solution.py:120
  98.7 10.7 %collective-permute-done.16.refs_3_.refs_7_ = bf16[1024,1152]{1,0:T(8,128)(2,1)} collective-permute-done((bf16[1024,1152]{1,0:T(8,128)(2,1)}, bf16[1024,1152]{1,0:T(8,128)(2,1)}, u32[]{:S(2)}, u32[]{:S(2)}) %collective-permute-start.16) | collective-permute-done | bytes 2359328 | tf_op jit(solution)/shard_map/ppermute | solution.py:51
  109.4 3.1 %collective-permute-done.15.refs_2_.refs_6_ = bf16[1024,1152]{1,0:T(8,128)(2,1)} collective-permute-done((bf16[1024,1152]{1,0:T(8,128)(2,1)}, bf16[1024,1152]{1,0:T(8,128)(2,1)}, u32[]{:S(2)}, u32[]{:S(2)}) %collective-permute-start.15) | collective-permute-done | bytes 2359328 | tf_op jit(solution)/shard_map/ppermute | solution.py:51
  112.7 3.8 %halve.2 = (bf16[512,1152]{1,0:T(8,128)(2,1)}, bf16[512,1152]{1,0:T(8,128)(2,1)}, bf16[512,1152]{1,0:T(8,128)(2,1)}, bf16[512,1152]{1,0:T(8,128)(2,1)}) custom-call(bf16[1024,1152]{1,0:T(8,128)(2,1)} %collective-permute-done.13.refs_0_.refs_1_, bf16[1024,1152]{1,0:T(8,128)(2,1)} %collective-permute-done.14.refs_1_.refs_2_, ...), custom_call_target="tpu_custom_call" | custom-call | bytes 2097152 | tf_op jit(solution)/shard_map/halve/pallas_call | solution.py:223
  116.5 2.5 collective-permute-start.20
  121.7 2.7 collective-permute-start.24
  124.4 14.5 %collective-permute-done.20.refs_9_ = bf16[512,1152]{1,0:T(8,128)(2,1)S(1)} collective-permute-done((bf16[512,1152]{1,0:T(8,128)(2,1)}, bf16[512,1152]{1,0:T(8,128)(2,1)S(1)}, u32[]{:S(2)}, u32[]{:S(2)}) %collective-permute-start.20) | collective-permute-done | bytes 1179680 | tf_op jit(solution)/shard_map/ppermute | solution.py:51
  138.9 3.0 collective-permute-done.19.refs_8_
  143.4 27.7 %select.12 = (bf16[2,1536,2304]{2,1,0:T(8,128)(2,1)}, bf16[2,2,192,2304]{3,2,1,0:T(8,128)(2,1)}, bf16[2,2,192,2304]{3,2,1,0:T(8,128)(2,1)}) custom-call(s32[64]{0:T(128)} %dynamic-slice_bitcast_fusion.order_ref, bf16[2,1536,128]{2,1,0:T(8,128)(2,1)} %get-tuple-element.134.pick_ref.refs_5_, bf16[2,768,1536]{2,1,0:T(8,128)(2,1)} %get-tuple-element.135.scaled_hbm, ...), custom_call_target="tpu_custom_call" | custom-call | flops 21743271936 | bytes 41030144 | tf_op jit(solution)/shard_map/select/pallas_call | solution.py:316
  171.1 7.1 %collective-permute-done.24.refs_3_.refs_7_ = bf16[1024,896]{1,0:T(8,128)(2,1)} collective-permute-done((bf16[1024,896]{1,0:T(8,128)(2,1)}, bf16[1024,896]{1,0:T(8,128)(2,1)}, u32[]{:S(2)}, u32[]{:S(2)}) %collective-permute-start.24) | collective-permute-done | bytes 1835040 | tf_op jit(solution)/shard_map/ppermute | solution.py:51
  179.4 9.1 %collective-permute-start.25 = (bf16[2,2,192,2304]{3,2,1,0:T(8,128)(2,1)}, bf16[2,2,192,2304]{3,2,1,0:T(8,128)(2,1)}, u32[]{:S(2)}, u32[]{:S(2)}) collective-permute-start(bf16[2,2,192,2304]{3,2,1,0:T(8,128)(2,1)} %get-tuple-element.160), channel_id=1, source_target_pairs={{0,1},{1,0},{2,3},{3,2},{4,5},{5,4},{6,7},{7,6},{8,9},{9,8},{10,11... | collective-permute-start | bytes 10616840 | tf_op jit(solution)/shard_map/ppermute | solution.py:602
  188.5 3.1 %halve.3 = (bf16[512,896]{1,0:T(8,128)(2,1)}, bf16[512,896]{1,0:T(8,128)(2,1)}, bf16[512,896]{1,0:T(8,128)(2,1)}, bf16[512,896]{1,0:T(8,128)(2,1)}) custom-call(bf16[1024,896]{1,0:T(8,128)(2,1)} %collective-permute-done.21.refs_0_.refs_1_, bf16[1024,896]{1,0:T(8,128)(2,1)} %collective-permute-done.22.refs_1_.refs_2_, ...), custom_call_target="tpu_custom_call" | custom-call | bytes 2097152 | tf_op jit(solution)/shard_map/halve/pallas_call | solution.py:223
  191.6 2.7 collective-permute-start.30
  194.4 1.5 collective-permute-start.27
  195.8 3.1 %fusion.4 = (bf16[2,192,1152]{2,1,0:T(8,128)(2,1)}, bf16[2,192,1152]{2,1,0:T(8,128)(2,1)}) fusion(bf16[2,2,192,2304]{3,2,1,0:T(8,128)(2,1)} %collective-permute-done.25, bf16[2,2,192,2304]{3,2,1,0:T(8,128)(2,1)S(1)} %copy-done.23), kind=kLoop, calls=%fused_computation.11 | loop fusion | flops 3538944 | bytes 5308416 | tf_op jit(solution)/shard_map/convert_element_type | solution.py:611
  198.9 2.7 collective-permute-start.26
  201.7 17.7 %upstream.1.refs_2_ = f32[2,1536,768]{2,1,0:T(8,128)} custom-call(bf16[2,1536,2304]{2,1,0:T(8,128)(2,1)} %get-tuple-element.158.refs_0_, bf16[2,768,4096]{2,1,0:T(8,128)(2,1)} %refs_1_.3), custom_call_target="tpu_custom_call" | custom-call | flops 169869312 | bytes 2359296 | tf_op jit(solution)/shard_map/upstream/pallas_call | solution.py:422
  219.4 1.3 collective-permute-done.26
  220.8 23.5 %select.13 = (bf16[2,1536,1792]{2,1,0:T(8,128)(2,1)}, bf16[2,2,192,1792]{3,2,1,0:T(8,128)(2,1)}, bf16[2,2,192,1792]{3,2,1,0:T(8,128)(2,1)}) custom-call(s32[64]{0:T(128)} %dynamic-slice_bitcast_fusion.order_ref, bf16[2,1536,128]{2,1,0:T(8,128)(2,1)} %get-tuple-element.134.pick_ref.refs_5_, bf16[2,768,1536]{2,1,0:T(8,128)(2,1)} %get-tuple-element.135.scaled_hbm, ...), custom_call_target="tpu_custom_call" | custom-call | flops 16911433728 | bytes 33690112 | tf_op jit(solution)/shard_map/select/pallas_call | solution.py:316
  244.2 2.0 collective-permute-start.31
  246.3 2.8 collective-permute-start.32
  249.0 2.2 collective-permute-done.31
  251.2 1.5 copy-done.24
  252.7 2.9 fusion.2
  255.6 2.7 collective-permute-start.33
  258.4 18.2 %finish.1 = (bf16[2,1536,768]{2,1,0:T(8,128)(2,1)}, f32[2,32,128]{2,1,0:T(8,128)}) custom-call(bf16[2,1536,1792]{2,1,0:T(8,128)(2,1)} %get-tuple-element.183.refs_0_, bf16[2,768,4096]{2,1,0:T(8,128)(2,1)} %refs_1_.3, f32[2,1536,768]{2,1,0:T(8,128)} %upstream.1.refs_2_, bf16[2,1536,768]{2,1,0:T(8,128)(2,1)} %get-tuple-element.184.refs_3_, ...), custom_call_target="tpu_custom_call" | custom-call | flops 132120576 | bytes 2359296 | tf_op jit(solution)/shard_map/finish/pallas_call | solution.py:422
  276.6 1.4 copy.27
  278.0 5.3 %all-to-all-start.1 = ((f32[32,2,128]{2,1,0:T(2,128)}), f32[32,2,128]{2,1,0:T(2,128)S(1)}, u32[]{:S(2)}, u32[]{:S(2)}) async-start(f32[32,2,128]{2,1,0:T(2,128)} %copy.27), calls=%async_computation.1 | async-start | bytes 65536 | tf_op jit(solution)/shard_map/all_to_all | solution.py:634
  283.4 3.2 %fusion = bf16[2,192,2304]{2,1,0:T(8,128)(2,1)S(1)} fusion(bf16[2,2,192,2304]{3,2,1,0:T(8,128)(2,1)} %collective-permute-done.25, bf16[2,192,1152]{2,1,0:T(8,128)(2,1)} %collective-permute-done.32, bf16[2,192,1152]{2,1,0:T(8,128)(2,1)} %copy-done.25, bf16[2,2,192,2304]{3,2,1,0:T(8,128)(2,1)} %get-tuple-element.161), kind=kLoop, calls=%fused_computation.1 | loop fusion | flops 7962624 | bytes 7077888 | tf_op jit(solution)/shard_map/convert_element_type | solution.py:632
  286.5 10.1 %in_slot_order.1 = bf16[1,2,1536,768]{3,2,1,0:T(8,128)(2,1)} custom-call(s32[64]{0:T(128)} %reshape.42.base_ref, s32[64]{0:T(128)} %reshape.43.lead_ref, s32[64]{0:T(128)} %convert_element_type.114.count_ref, bf16[2,1536,768]{2,1,0:T(8,128)(2,1)} %get-tuple-element.186.hidden_ref), custom_call_target="tpu_custom_call" | custom-call | flops 1000000000 | bytes 12000000 | tf_op jit(solution)/shard_map/in_slot_order/pallas_call | solution.py:465
  296.6 5.1 %all-to-all-done.1 = f32[32,2,128]{2,1,0:T(2,128)S(1)} async-done(((f32[32,2,128]{2,1,0:T(2,128)}), f32[32,2,128]{2,1,0:T(2,128)S(1)}, u32[]{:S(2)}, u32[]{:S(2)}) %all-to-all-start.1) | async-done | bytes 32800 | tf_op jit(solution)/shard_map/all_to_all | solution.py:634
  302.4 2.2 fusion.1
  304.6 2.1 pad_maximum_fusion
  (125 shorter events, 29.3 us)
Async XLA Ops:
  0.6 24.7 %collective-permute-start.1 = (bf16[128,4096]{1,0:T(8,128)(2,1)}, bf16[128,4096]{1,0:T(8,128)(2,1)S(1)}, u32[]{:S(2)}, u32[]{:S(2)}) collective-permute-start(bf16[128,4096]{1,0:T(8,128)(2,1)} %bitcast.37), channel_id=1, source_target_pairs={{0,16},{4,20},{8,24},{12,28},{16,0},{20,4},{24,8},{28,12},{32,48},... | collective-permute-start | bytes 3145736 | tf_op jit(solution)/shard_map/ppermute | solution.py:51
  5.0 40.6 %copy-start.28 = (bf16[1,128,8]{1,2,0:T(8,128)(2,1)S(1)}, bf16[1,128,8]{1,2,0:T(8,128)(2,1)}, u32[]{:S(2)}) copy-start(bf16[1,128,8]{1,2,0:T(8,128)(2,1)} %param.7) | copy-start | bytes 6148
  5.0 40.6 %copy-start.27 = (s32[1,128,8]{1,2,0:T(8,128)S(1)}, s32[1,128,8]{1,2,0:T(8,128)}, u32[]{:S(2)}) copy-start(s32[1,128,8]{1,2,0:T(8,128)} %param.8) | copy-start | bytes 12292
  5.0 15.2 %collective-permute-start = (bf16[128,2048]{1,0:T(8,128)(2,1)S(1)}, bf16[128,2048]{1,0:T(8,128)(2,1)S(1)}, u32[]{:S(2)}, u32[]{:S(2)}) collective-permute-start(bf16[128,2048]{1,0:T(8,128)(2,1)S(1)} %pad_maximum_fusion.1.refs_0_), channel_id=1, source_target_pairs={{0,32},{4,36},{8,40},{12,44},{16,48},{20,52},{24,56},{28,60},{32,6... | collective-permute-start | bytes 1572872 | tf_op jit(solution)/shard_map/ppermute | solution.py:51
  6.7 25.9 %collective-permute-start.3 = (bf16[128,2048]{1,0:T(8,128)(2,1)S(1)}, bf16[128,2048]{1,0:T(8,128)(2,1)S(1)}, u32[]{:S(2)}, u32[]{:S(2)}) collective-permute-start(bf16[128,2048]{1,0:T(8,128)(2,1)S(1)} %pad_maximum_fusion.1.refs_0_), channel_id=1, source_target_pairs={{0,96},{4,100},{8,104},{12,108},{16,112},{20,116},{24,120},{28,124... | collective-permute-start | bytes 1572872 | tf_op jit(solution)/shard_map/ppermute | solution.py:51
  9.0 20.8 %collective-permute-start.7 = (bf16[128,2048]{1,0:T(8,128)(2,1)S(1)}, bf16[128,2048]{1,0:T(8,128)(2,1)S(1)}, u32[]{:S(2)}, u32[]{:S(2)}) collective-permute-start(bf16[128,2048]{1,0:T(8,128)(2,1)S(1)} %pad_maximum_fusion.3.refs_8_), channel_id=1, source_target_pairs={{0,4},{4,8},{8,12},{12,0},{16,20},{20,24},{24,28},{28,16},{32,36},... | collective-permute-start | bytes 1572872 | tf_op jit(solution)/shard_map/ppermute | solution.py:51
  10.4 22.3 %collective-permute-start.9 = (bf16[128,2048]{1,0:T(8,128)(2,1)S(1)}, bf16[128,2048]{1,0:T(8,128)(2,1)S(1)}, u32[]{:S(2)}, u32[]{:S(2)}) collective-permute-start(bf16[128,2048]{1,0:T(8,128)(2,1)S(1)} %pad_maximum_fusion.3.refs_8_), channel_id=1, source_target_pairs={{0,12},{4,0},{8,4},{12,8},{16,28},{20,16},{24,20},{28,24},{32,44},... | collective-permute-start | bytes 1572872 | tf_op jit(solution)/shard_map/ppermute | solution.py:51
  20.2 13.1 %collective-permute-start.5 = (bf16[128,2048]{1,0:T(8,128)(2,1)S(1)}, bf16[128,2048]{1,0:T(8,128)(2,1)S(1)}, u32[]{:S(2)}, u32[]{:S(2)}) collective-permute-start(bf16[128,2048]{1,0:T(8,128)(2,1)S(1)} %collective-permute-done.refs_2_), channel_id=1, source_target_pairs={{0,32},{4,36},{8,40},{12,44},{16,48},{20,52},{24,56},{28,60},{32,6... | collective-permute-start | bytes 1572872 | tf_op jit(solution)/shard_map/ppermute | solution.py:51
  25.5 13.9 %collective-permute-start.4 = (bf16[128,2048]{1,0:T(8,128)(2,1)S(1)}, bf16[128,2048]{1,0:T(8,128)(2,1)S(1)}, u32[]{:S(2)}, u32[]{:S(2)}) collective-permute-start(bf16[128,2048]{1,0:T(8,128)(2,1)S(1)} %pad_maximum_fusion.2.refs_1_), channel_id=1, source_target_pairs={{0,96},{4,100},{8,104},{12,108},{16,112},{20,116},{24,120},{28,124... | collective-permute-start | bytes 1572872 | tf_op jit(solution)/shard_map/ppermute | solution.py:51
  29.8 29.8 %copy-start = (bf16[128,2048]{1,0:T(8,128)(2,1)}, bf16[128,2048]{1,0:T(8,128)(2,1)S(1)}, u32[]{:S(2)}) copy-start(bf16[128,2048]{1,0:T(8,128)(2,1)S(1)} %collective-permute-done.7.refs_10_) | copy-start | bytes 1572868
  29.8 13.0 %collective-permute-start.10 = (bf16[128,2048]{1,0:T(8,128)(2,1)S(1)}, bf16[128,2048]{1,0:T(8,128)(2,1)S(1)}, u32[]{:S(2)}, u32[]{:S(2)}) collective-permute-start(bf16[128,2048]{1,0:T(8,128)(2,1)S(1)} %pad_maximum_fusion.4.refs_9_), channel_id=1, source_target_pairs={{0,12},{4,0},{8,4},{12,8},{16,28},{20,16},{24,20},{28,24},{32,44},... | collective-permute-start | bytes 1572872 | tf_op jit(solution)/shard_map/ppermute | solution.py:51
  32.6 23.8 %collective-permute-start.11 = (bf16[128,2048]{1,0:T(8,128)(2,1)S(1)}, bf16[128,2048]{1,0:T(8,128)(2,1)S(1)}, u32[]{:S(2)}, u32[]{:S(2)}) collective-permute-start(bf16[128,2048]{1,0:T(8,128)(2,1)S(1)} %collective-permute-done.7.refs_10_), channel_id=1, source_target_pairs={{0,4},{4,8},{8,12},{12,0},{16,20},{20,24},{24,28},{28,16},{32,36},... | collective-permute-start | bytes 1572872 | tf_op jit(solution)/shard_map/ppermute | solution.py:51
  32.6 27.0 %copy-start.2 = (bf16[128,2048]{1,0:T(8,128)(2,1)}, bf16[128,2048]{1,0:T(8,128)(2,1)S(1)}, u32[]{:S(2)}) copy-start(bf16[128,2048]{1,0:T(8,128)(2,1)S(1)} %collective-permute-done.9.refs_12_) | copy-start | bytes 1572868
  32.7 23.8 %collective-permute-start.8 = (bf16[128,2048]{1,0:T(8,128)(2,1)S(1)}, bf16[128,2048]{1,0:T(8,128)(2,1)S(1)}, u32[]{:S(2)}, u32[]{:S(2)}) collective-permute-start(bf16[128,2048]{1,0:T(8,128)(2,1)S(1)} %pad_maximum_fusion.4.refs_9_), channel_id=1, source_target_pairs={{0,4},{4,8},{8,12},{12,0},{16,20},{20,24},{24,28},{28,16},{32,36},... | collective-permute-start | bytes 1572872 | tf_op jit(solution)/shard_map/ppermute | solution.py:51
  33.3 26.4 %copy-start.4 = (bf16[128,2048]{1,0:T(8,128)(2,1)}, bf16[128,2048]{1,0:T(8,128)(2,1)S(1)}, u32[]{:S(2)}) copy-start(bf16[128,2048]{1,0:T(8,128)(2,1)S(1)} %collective-permute-done.5.refs_6_) | copy-start | bytes 1572868
  33.3 23.2 %collective-permute-start.2 = (bf16[128,2048]{1,0:T(8,128)(2,1)S(1)}, bf16[128,2048]{1,0:T(8,128)(2,1)S(1)}, u32[]{:S(2)}, u32[]{:S(2)}) collective-permute-start(bf16[128,2048]{1,0:T(8,128)(2,1)S(1)} %pad_maximum_fusion.2.refs_1_), channel_id=1, source_target_pairs={{0,32},{4,36},{8,40},{12,44},{16,48},{20,52},{24,56},{28,60},{32,6... | collective-permute-start | bytes 1572872 | tf_op jit(solution)/shard_map/ppermute | solution.py:51
  39.4 20.3 %copy-start.6 = (bf16[128,2048]{1,0:T(8,128)(2,1)}, bf16[128,2048]{1,0:T(8,128)(2,1)S(1)}, u32[]{:S(2)}) copy-start(bf16[128,2048]{1,0:T(8,128)(2,1)S(1)} %collective-permute-done.4.refs_5_) | copy-start | bytes 1572868
  39.4 17.1 %collective-permute-start.6 = (bf16[128,2048]{1,0:T(8,128)(2,1)S(1)}, bf16[128,2048]{1,0:T(8,128)(2,1)S(1)}, u32[]{:S(2)}, u32[]{:S(2)}) collective-permute-start(bf16[128,2048]{1,0:T(8,128)(2,1)S(1)} %collective-permute-done.4.refs_5_), channel_id=1, source_target_pairs={{0,96},{4,100},{8,104},{12,108},{16,112},{20,116},{24,120},{28,124... | collective-permute-start | bytes 1572872 | tf_op jit(solution)/shard_map/ppermute | solution.py:51
  42.8 16.9 %copy-start.8 = (bf16[128,2048]{1,0:T(8,128)(2,1)}, bf16[128,2048]{1,0:T(8,128)(2,1)S(1)}, u32[]{:S(2)}) copy-start(bf16[128,2048]{1,0:T(8,128)(2,1)S(1)} %collective-permute-done.10.refs_13_) | copy-start | bytes 1572868
  42.8 13.7 %collective-permute-start.12 = (bf16[128,2048]{1,0:T(8,128)(2,1)S(1)}, bf16[128,2048]{1,0:T(8,128)(2,1)S(1)}, u32[]{:S(2)}, u32[]{:S(2)}) collective-permute-start(bf16[128,2048]{1,0:T(8,128)(2,1)S(1)} %collective-permute-done.10.refs_13_), channel_id=1, source_target_pairs={{0,12},{4,0},{8,4},{12,8},{16,28},{20,16},{24,20},{28,24},{32,44},... | collective-permute-start | bytes 1572872 | tf_op jit(solution)/shard_map/ppermute | solution.py:51
  56.5 3.2 %copy-start.12 = (bf16[128,2048]{1,0:T(8,128)(2,1)}, bf16[128,2048]{1,0:T(8,128)(2,1)S(1)}, u32[]{:S(2)}) copy-start(bf16[128,2048]{1,0:T(8,128)(2,1)S(1)} %collective-permute-done.8.refs_11_) | copy-start | bytes 1572868
  59.8 49.6 %collective-permute-start.16 = (bf16[1024,1152]{1,0:T(8,128)(2,1)}, bf16[1024,1152]{1,0:T(8,128)(2,1)}, u32[]{:S(2)}, u32[]{:S(2)}) collective-permute-start(bf16[1024,1152]{1,0:T(8,128)(2,1)} %get-tuple-element.151.refs_5_), channel_id=1, source_target_pairs={{0,96},{4,100},{8,104},{12,108},{16,112},{20,116},{24,120},{28,124... | collective-permute-start | bytes 7077896 | tf_op jit(solution)/shard_map/ppermute | solution.py:51
  61.9 50.6 %collective-permute-start.15 = (bf16[1024,1152]{1,0:T(8,128)(2,1)}, bf16[1024,1152]{1,0:T(8,128)(2,1)}, u32[]{:S(2)}, u32[]{:S(2)}) collective-permute-start(bf16[1024,1152]{1,0:T(8,128)(2,1)} %get-tuple-element.151.refs_5_), channel_id=1, source_target_pairs={{0,32},{4,36},{8,40},{12,44},{16,48},{20,52},{24,56},{28,60},{32,6... | collective-permute-start | bytes 7077896 | tf_op jit(solution)/shard_map/ppermute | solution.py:51
  61.9 50.6 %collective-permute-start.14 = (bf16[1024,1152]{1,0:T(8,128)(2,1)}, bf16[1024,1152]{1,0:T(8,128)(2,1)}, u32[]{:S(2)}, u32[]{:S(2)}) collective-permute-start(bf16[1024,1152]{1,0:T(8,128)(2,1)} %get-tuple-element.140.refs_0_), channel_id=1, source_target_pairs={{0,12},{4,0},{8,4},{12,8},{16,28},{20,16},{24,20},{28,24},{32,44},... | collective-permute-start | bytes 7077896 | tf_op jit(solution)/shard_map/ppermute | solution.py:51
  63.0 49.7 %collective-permute-start.13 = (bf16[1024,1152]{1,0:T(8,128)(2,1)}, bf16[1024,1152]{1,0:T(8,128)(2,1)}, u32[]{:S(2)}, u32[]{:S(2)}) collective-permute-start(bf16[1024,1152]{1,0:T(8,128)(2,1)} %get-tuple-element.140.refs_0_), channel_id=1, source_target_pairs={{0,4},{4,8},{8,12},{12,0},{16,20},{20,24},{24,28},{28,16},{32,36},... | collective-permute-start | bytes 7077896 | tf_op jit(solution)/shard_map/ppermute | solution.py:51
  109.4 32.5 %copy-start.21 = (bf16[1024,896]{1,0:T(8,128)(2,1)S(1)}, bf16[1024,896]{1,0:T(8,128)(2,1)}, u32[]{:S(2)}) copy-start(bf16[1024,896]{1,0:T(8,128)(2,1)} %copy-done.20) | copy-start | bytes 5505028
  116.5 22.4 %collective-permute-start.20 = (bf16[512,1152]{1,0:T(8,128)(2,1)}, bf16[512,1152]{1,0:T(8,128)(2,1)S(1)}, u32[]{:S(2)}, u32[]{:S(2)}) collective-permute-start(bf16[512,1152]{1,0:T(8,128)(2,1)} %get-tuple-element.156), channel_id=1, source_target_pairs={{0,96},{4,100},{8,104},{12,108},{16,112},{20,116},{24,120},{28,124... | collective-permute-start | bytes 3538952 | tf_op jit(solution)/shard_map/ppermute | solution.py:51
  119.0 22.9 %collective-permute-start.19 = (bf16[512,1152]{1,0:T(8,128)(2,1)}, bf16[512,1152]{1,0:T(8,128)(2,1)}, u32[]{:S(2)}, u32[]{:S(2)}) collective-permute-start(bf16[512,1152]{1,0:T(8,128)(2,1)} %get-tuple-element.154), channel_id=1, source_target_pairs={{0,32},{4,36},{8,40},{12,44},{16,48},{20,52},{24,56},{28,60},{32,6... | collective-permute-start | bytes 3538952 | tf_op jit(solution)/shard_map/ppermute | solution.py:51
  119.0 23.5 %collective-permute-start.18 = (bf16[512,1152]{1,0:T(8,128)(2,1)}, bf16[512,1152]{1,0:T(8,128)(2,1)}, u32[]{:S(2)}, u32[]{:S(2)}) collective-permute-start(bf16[512,1152]{1,0:T(8,128)(2,1)} %get-tuple-element.149), channel_id=1, source_target_pairs={{0,12},{4,0},{8,4},{12,8},{16,28},{20,16},{24,20},{28,24},{32,44},... | collective-permute-start | bytes 3538952 | tf_op jit(solution)/shard_map/ppermute | solution.py:51
  119.3 24.1 %collective-permute-start.17 = (bf16[512,1152]{1,0:T(8,128)(2,1)}, bf16[512,1152]{1,0:T(8,128)(2,1)}, u32[]{:S(2)}, u32[]{:S(2)}) collective-permute-start(bf16[512,1152]{1,0:T(8,128)(2,1)} %get-tuple-element.147), channel_id=1, source_target_pairs={{0,4},{4,8},{8,12},{12,0},{16,20},{20,24},{24,28},{28,16},{32,36},... | collective-permute-start | bytes 3538952 | tf_op jit(solution)/shard_map/ppermute | solution.py:51
  121.7 56.5 %collective-permute-start.24 = (bf16[1024,896]{1,0:T(8,128)(2,1)}, bf16[1024,896]{1,0:T(8,128)(2,1)}, u32[]{:S(2)}, u32[]{:S(2)}) collective-permute-start(bf16[1024,896]{1,0:T(8,128)(2,1)} %copy-done.22), channel_id=1, source_target_pairs={{0,96},{4,100},{8,104},{12,108},{16,112},{20,116},{24,120},{28,124... | collective-permute-start | bytes 5505032 | tf_op jit(solution)/shard_map/ppermute | solution.py:51
  138.9 4.5 %copy-start.29 = (bf16[512,1152]{1,0:T(8,128)(2,1)}, bf16[512,1152]{1,0:T(8,128)(2,1)S(1)}, u32[]{:S(2)}) copy-start(bf16[512,1152]{1,0:T(8,128)(2,1)S(1)} %collective-permute-done.20.refs_9_) | copy-start | bytes 3538948
  138.9 40.5 %collective-permute-start.23 = (bf16[1024,896]{1,0:T(8,128)(2,1)}, bf16[1024,896]{1,0:T(8,128)(2,1)}, u32[]{:S(2)}, u32[]{:S(2)}) collective-permute-start(bf16[1024,896]{1,0:T(8,128)(2,1)} %copy-done.22), channel_id=1, source_target_pairs={{0,32},{4,36},{8,40},{12,44},{16,48},{20,52},{24,56},{28,60},{32,6... | collective-permute-start | bytes 5505032 | tf_op jit(solution)/shard_map/ppermute | solution.py:51
  141.9 37.5 %collective-permute-start.22 = (bf16[1024,896]{1,0:T(8,128)(2,1)S(1)}, bf16[1024,896]{1,0:T(8,128)(2,1)}, u32[]{:S(2)}, u32[]{:S(2)}) collective-permute-start(bf16[1024,896]{1,0:T(8,128)(2,1)S(1)} %copy-done.21), channel_id=1, source_target_pairs={{0,12},{4,0},{8,4},{12,8},{16,28},{20,16},{24,20},{28,24},{32,44},... | collective-permute-start | bytes 5505032 | tf_op jit(solution)/shard_map/ppermute | solution.py:51
  142.5 36.9 %collective-permute-start.21 = (bf16[1024,896]{1,0:T(8,128)(2,1)S(1)}, bf16[1024,896]{1,0:T(8,128)(2,1)}, u32[]{:S(2)}, u32[]{:S(2)}) collective-permute-start(bf16[1024,896]{1,0:T(8,128)(2,1)S(1)} %copy-done.21), channel_id=1, source_target_pairs={{0,4},{4,8},{8,12},{12,0},{16,20},{20,24},{24,28},{28,16},{32,36},... | collective-permute-start | bytes 5505032 | tf_op jit(solution)/shard_map/ppermute | solution.py:51
  179.4 16.4 %copy-start.23 = (bf16[2,2,192,2304]{3,2,1,0:T(8,128)(2,1)S(1)}, bf16[2,2,192,2304]{3,2,1,0:T(8,128)(2,1)}, u32[]{:S(2)}) copy-start(bf16[2,2,192,2304]{3,2,1,0:T(8,128)(2,1)} %get-tuple-element.161) | copy-start | bytes 10616836
  179.4 16.4 %collective-permute-start.25 = (bf16[2,2,192,2304]{3,2,1,0:T(8,128)(2,1)}, bf16[2,2,192,2304]{3,2,1,0:T(8,128)(2,1)}, u32[]{:S(2)}, u32[]{:S(2)}) collective-permute-start(bf16[2,2,192,2304]{3,2,1,0:T(8,128)(2,1)} %get-tuple-element.160), channel_id=1, source_target_pairs={{0,1},{1,0},{2,3},{3,2},{4,5},{5,4},{6,7},{7,6},{8,9},{9,8},{10,11... | collective-permute-start | bytes 10616840 | tf_op jit(solution)/shard_map/ppermute | solution.py:602
  191.6 27.8 %collective-permute-start.30 = (bf16[512,896]{1,0:T(8,128)(2,1)}, bf16[512,896]{1,0:T(8,128)(2,1)}, u32[]{:S(2)}, u32[]{:S(2)}) collective-permute-start(bf16[512,896]{1,0:T(8,128)(2,1)} %get-tuple-element.178), channel_id=1, source_target_pairs={{0,96},{4,100},{8,104},{12,108},{16,112},{20,116},{24,120},{28,124... | collective-permute-start | bytes 2752520 | tf_op jit(solution)/shard_map/ppermute | solution.py:51
  194.4 26.4 %collective-permute-start.29 = (bf16[512,896]{1,0:T(8,128)(2,1)}, bf16[512,896]{1,0:T(8,128)(2,1)}, u32[]{:S(2)}, u32[]{:S(2)}) collective-permute-start(bf16[512,896]{1,0:T(8,128)(2,1)} %get-tuple-element.176), channel_id=1, source_target_pairs={{0,32},{4,36},{8,40},{12,44},{16,48},{20,52},{24,56},{28,60},{32,6... | collective-permute-start | bytes 2752520 | tf_op jit(solution)/shard_map/ppermute | solution.py:51
  194.4 26.4 %collective-permute-start.28 = (bf16[512,896]{1,0:T(8,128)(2,1)}, bf16[512,896]{1,0:T(8,128)(2,1)}, u32[]{:S(2)}, u32[]{:S(2)}) collective-permute-start(bf16[512,896]{1,0:T(8,128)(2,1)} %get-tuple-element.171), channel_id=1, source_target_pairs={{0,12},{4,0},{8,4},{12,8},{16,28},{20,16},{24,20},{28,24},{32,44},... | collective-permute-start | bytes 2752520 | tf_op jit(solution)/shard_map/ppermute | solution.py:51
  194.4 26.4 %collective-permute-start.27 = (bf16[512,896]{1,0:T(8,128)(2,1)}, bf16[512,896]{1,0:T(8,128)(2,1)}, u32[]{:S(2)}, u32[]{:S(2)}) collective-permute-start(bf16[512,896]{1,0:T(8,128)(2,1)} %get-tuple-element.169), channel_id=1, source_target_pairs={{0,4},{4,8},{8,12},{12,0},{16,20},{20,24},{24,28},{28,16},{32,36},... | collective-permute-start | bytes 2752520 | tf_op jit(solution)/shard_map/ppermute | solution.py:51
  198.9 21.8 %collective-permute-start.26 = (bf16[2,192,1152]{2,1,0:T(8,128)(2,1)}, bf16[2,192,1152]{2,1,0:T(8,128)(2,1)S(1)}, u32[]{:S(2)}, u32[]{:S(2)}) collective-permute-start(bf16[2,192,1152]{2,1,0:T(8,128)(2,1)} %get-tuple-element.193), channel_id=1, source_target_pairs={{0,2},{2,0},{1,3},{3,1},{4,6},{6,4},{5,7},{7,5},{8,10},{10,8},{9,1... | collective-permute-start | bytes 2654216 | tf_op jit(solution)/shard_map/ppermute | solution.py:612
  220.7 23.5 %copy-start.25 = (bf16[2,192,1152]{2,1,0:T(8,128)(2,1)}, bf16[2,192,1152]{2,1,0:T(8,128)(2,1)S(1)}, u32[]{:S(2)}) copy-start(bf16[2,192,1152]{2,1,0:T(8,128)(2,1)S(1)} %collective-permute-done.26) | copy-start | bytes 2654212
  220.7 25.5 %copy-start.26 = (bf16[2,192,1152]{2,1,0:T(8,128)(2,1)S(1)}, bf16[2,192,1152]{2,1,0:T(8,128)(2,1)}, u32[]{:S(2)}) copy-start(bf16[2,192,1152]{2,1,0:T(8,128)(2,1)} %get-tuple-element.189) | copy-start | bytes 2654212
  244.2 7.0 %collective-permute-start.31 = (bf16[2,2,192,1792]{3,2,1,0:T(8,128)(2,1)}, bf16[2,2,192,1792]{3,2,1,0:T(8,128)(2,1)S(1)}, u32[]{:S(2)}, u32[]{:S(2)}) collective-permute-start(bf16[2,2,192,1792]{3,2,1,0:T(8,128)(2,1)} %get-tuple-element.181), channel_id=1, source_target_pairs={{0,1},{1,0},{2,3},{3,2},{4,5},{5,4},{6,7},{7,6},{8,9},{9,8},{10,11... | collective-permute-start | bytes 8257544 | tf_op jit(solution)/shard_map/ppermute | solution.py:602
  246.3 30.3 %collective-permute-start.32 = (bf16[2,192,1152]{2,1,0:T(8,128)(2,1)S(1)}, bf16[2,192,1152]{2,1,0:T(8,128)(2,1)}, u32[]{:S(2)}, u32[]{:S(2)}) collective-permute-start(bf16[2,192,1152]{2,1,0:T(8,128)(2,1)S(1)} %copy-done.26), channel_id=1, source_target_pairs={{0,2},{2,0},{1,3},{3,1},{4,6},{6,4},{5,7},{7,5},{8,10},{10,8},{9,1... | collective-permute-start | bytes 2654216 | tf_op jit(solution)/shard_map/ppermute | solution.py:612
  255.6 46.7 %collective-permute-start.33 = (bf16[2,192,1792]{2,1,0:T(8,128)(2,1)}, bf16[2,192,1792]{2,1,0:T(8,128)(2,1)S(1)}, u32[]{:S(2)}, u32[]{:S(2)}) collective-permute-start(bf16[2,192,1792]{2,1,0:T(8,128)(2,1)} %fusion.2), channel_id=1, source_target_pairs={{0,2},{2,0},{1,3},{3,1},{4,6},{6,4},{5,7},{7,5},{8,10},{10,8},{9,1... | collective-permute-start | bytes 4128776 | tf_op jit(solution)/shard_map/ppermute | solution.py:612
  278.0 23.7 %all-to-all-start.1 = ((f32[32,2,128]{2,1,0:T(2,128)}), f32[32,2,128]{2,1,0:T(2,128)S(1)}, u32[]{:S(2)}, u32[]{:S(2)}) async-start(f32[32,2,128]{2,1,0:T(2,128)} %copy.27), calls=%async_computation.1 | async-start | bytes 65536 | tf_op jit(solution)/shard_map/all_to_all | solution.py:634
  (17 other events, 27.4 us)

commit v3 on v2

--- a/solution.py
+++ b/solution.py
@@ -273,14 +273,14 @@
                     rows[e, to, side * half : (side + 1) * half] = found[e * MOST : (e + 1) * MOST]
                 return carry
 
-            lax.fori_loop(0, size // TOK, place, 0, unroll=2)
+            lax.fori_loop(0, size // TOK, place, 0, unroll=4)
     outs = []
     for e in range(EXP):
         copy = pltpu.make_async_copy(rows.at[e], rows_out.at[e], out_sems.at[e])
         copy.start()
         outs.append(copy)
     load.wait()
-    tile = 256
+    tile = width // 3 if width % 768 == 0 else width // 2
     for e in range(EXP):
 
         def multiply(number, carry, e=e):
@@ -386,7 +386,7 @@
     sum_ref[0] = jnp.sum(spread.reshape(ROW_TILE_LAST // MOST, MOST, TOK), axis=1)
 
 
-ROW_TILE_LAST = 384
+ROW_TILE_LAST = 768
 
 
 def upstream(rows, weight, first_column, total, extra, last):
@@ -635,6 +635,7 @@
         jnp.swapaxes(sums, 0, 1), "expert", split_axis=0, concat_axis=0, tiled=True
     ).reshape(SOURCES * EXP, TOK)
     hidden_grad = in_slot_order(base, lead, counts, hidden)
+    back = after(back, weight_grad, hidden_grad)
     index_t = expert_index[0].T
     experts = jnp.arange(SOURCES * EXP, dtype=jnp.int32)[None, :, None]
     picked = jnp.sum(jnp.where(index_t[:, None, :] == experts, back[None], 0.0), axis=1)

time: 308 us -> 302 us (0.981)
  Pallas kernels: 125 us -> 117 us
    pallas_call x2, Pallas kernels: 51.1 us -> 43.1 us  [select(): pl.pallas_call(functools.partial(select_kernel, width), in_specs=[smem, v...]
    all_to_all x1, waiting for transfers between devices: 5.13 us -> 0.01 us  [body(): lax.all_to_all(jnp.swapaxes(sums, 0, 1), 'expert', split_axis=0, concat_a...]
    ppermute x29, waiting for transfers between devices: 60.1 us -> 64.8 us  [send(): return lax.ppermute(value, 'expert', pairs)]
  transfers between devices with their start and end apart: 35 -> 35, of which waited for: 14 -> 14; matrix products, arithmetic and copies ran while one was open for 6% -> 7% of each run, Pallas kernels for 31% -> 30%
where the time goes in v3:
time: 302 us; the launch traced here: 301 us
  Pallas kernels  117 us (39%)
  waiting for transfers between devices  71.3 us (24%)
  starting transfers between devices  62.9 us (21%)
  local copies, waits for them, and re-layouts  21.6 us (7%)
  other arithmetic  16.3 us (5%)
  blocking collectives  10.8 us (4%)
    ppermute x29, waiting for transfers between devices, send(): return lax.ppermute(value, 'expert', pairs)  64.8 us
    pallas_call x2, Pallas kernels, select(): pl.pallas_call(functools.partial(select_kernel, width), in_specs=[smem, v...  43.1 us
    ppermute x29, starting transfers between devices, send(): return lax.ppermute(value, 'expert', pairs)  38.1 us
    pallas_call x2, Pallas kernels, upstream(): pl.pallas_call(functools.partial(upstream_kernel, total is not None, last...  35.6 us
    pallas_call x1, Pallas kernels, prepare(): pl.pallas_call(prepare_kernel, grid_spec=pltpu.PrefetchScalarGridSpec(num...  16.9 us
    unnamed x60, local copies, waits for them, and re-layouts  14.6 us
    ppermute x2, starting transfers between devices, body(): met = lax.ppermute(leaving, 'replica', CORE_SWAP)  11.1 us
    all_to_all x1, blocking collectives, send_gates(): lax.all_to_all(dense, 'expert', split_axis=0, concat_axis=0, tiled=True)  10.8 us
  transfers between devices with their start and end apart: 35, of which 14 were waited for; matrix products, arithmetic and copies ran while one was open for 7% of the time, Pallas kernels for 30%

profile of v3, /device:TPU:1, one launch (start us, length us, event | category | flops | bytes accessed | tf_op | source)
XLA Modules:
  0.0 301.1 jit_solution(15761600799059518880)
XLA Ops:
  0.6 2.1 collective-permute-start.1
  5.0 1.7 collective-permute-start
  6.7 2.2 collective-permute-start.3
  10.4 1.5 collective-permute-start.9
  11.9 8.3 %collective-permute-done.refs_2_ = bf16[128,2048]{1,0:T(8,128)(2,1)S(1)} collective-permute-done((bf16[128,2048]{1,0:T(8,128)(2,1)S(1)}, bf16[128,2048]{1,0:T(8,128)(2,1)S(1)}, u32[]{:S(2)}, u32[]{:S(2)}) %collective-permute-start) | collective-permute-done | bytes 524320 | tf_op jit(solution)/shard_map/ppermute | solution.py:51
  20.2 5.2 %collective-permute-done.1 = bf16[128,4096]{1,0:T(8,128)(2,1)S(1)} collective-permute-done((bf16[128,4096]{1,0:T(8,128)(2,1)}, bf16[128,4096]{1,0:T(8,128)(2,1)S(1)}, u32[]{:S(2)}, u32[]{:S(2)}) %collective-permute-start.1) | collective-permute-done | bytes 1048608 | tf_op jit(solution)/shard_map/ppermute | solution.py:51
  25.5 4.3 %collective-permute-start.4 = (bf16[128,2048]{1,0:T(8,128)(2,1)S(1)}, bf16[128,2048]{1,0:T(8,128)(2,1)S(1)}, u32[]{:S(2)}, u32[]{:S(2)}) collective-permute-start(bf16[128,2048]{1,0:T(8,128)(2,1)S(1)} %pad_maximum_fusion.2.refs_1_), channel_id=1, source_target_pairs={{0,96},{4,100},{8,104},{12,108},{16,112},{20,116},{24,120},{28,124... | collective-permute-start | bytes 1572872 | tf_op jit(solution)/shard_map/ppermute | solution.py:51
  29.8 2.8 collective-permute-start.10
  33.3 6.2 %collective-permute-done.4.refs_5_ = bf16[128,2048]{1,0:T(8,128)(2,1)S(1)} collective-permute-done((bf16[128,2048]{1,0:T(8,128)(2,1)S(1)}, bf16[128,2048]{1,0:T(8,128)(2,1)S(1)}, u32[]{:S(2)}, u32[]{:S(2)}) %collective-permute-start.4) | collective-permute-done | bytes 524320 | tf_op jit(solution)/shard_map/ppermute | solution.py:51
  39.4 3.4 %collective-permute-start.6 = (bf16[128,2048]{1,0:T(8,128)(2,1)S(1)}, bf16[128,2048]{1,0:T(8,128)(2,1)S(1)}, u32[]{:S(2)}, u32[]{:S(2)}) collective-permute-start(bf16[128,2048]{1,0:T(8,128)(2,1)S(1)} %collective-permute-done.4.refs_5_), channel_id=1, source_target_pairs={{0,96},{4,100},{8,104},{12,108},{16,112},{20,116},{24,120},{28,124... | collective-permute-start | bytes 1572872 | tf_op jit(solution)/shard_map/ppermute | solution.py:51
  42.8 2.7 collective-permute-start.12
  45.6 10.8 %all_to_all.10 = bf16[32,2,128]{2,1,0:T(2,128)(2,1)S(1)} all-to-all(bf16[32,2,128]{2,1,0:T(2,128)(2,1)S(1)} %bitcast.40), channel_id=1, replica_groups=mesh['expert'=32,'replica'=4] {'expert'}, dimensions={0} | all-to-all | bytes 32768 | tf_op jit(solution)/shard_map/all_to_all | solution.py:496
  56.5 3.2 %join.2 = (bf16[1024,1152]{1,0:T(8,128)(2,1)}, bf16[1024,1152]{1,0:T(8,128)(2,1)}) custom-call(bf16[128,2048]{1,0:T(8,128)(2,1)S(1)} %pad_maximum_fusion.1.refs_0_, bf16[128,2048]{1,0:T(8,128)(2,1)S(1)} %pad_maximum_fusion.2.refs_1_, bf16[128,2048]{1,0:T(8,128)(2,1)S(1)} %collective-permute-done.refs_2_, ...), custom_call_target="tpu_custom_call" | custom-call | bytes 2097152 | tf_op jit(solution)/shard_map/join/pallas_call | solution.py:187
  59.8 2.2 collective-permute-start.16
  81.9 16.9 %prepare.1 = (bf16[2,768,1536]{2,1,0:T(8,128)(2,1)}, bf16[2,1536,768]{2,1,0:T(8,128)(2,1)}, f32[2,1536,128]{2,1,0:T(8,128)}, bf16[2,1536,128]{2,1,0:T(8,128)(2,1)}) custom-call(s32[64]{0:T(128)} %reshape.45.base_ref, s32[64]{0:T(128)} %reshape.46.lead_ref, s32[64]{0:T(128)} %convert_element_type.114.count_ref, s32[2]{0:T(128)} %pad_add_fusion.place_ref, ...), custom_call_target="tpu_custom_call" | custom-call | flops 1000000000 | bytes 16000000 | tf_op jit(solution)/shard_map/prepare/pallas_call | solution.py:120
  98.8 10.7 %collective-permute-done.16.refs_3_.refs_7_ = bf16[1024,1152]{1,0:T(8,128)(2,1)} collective-permute-done((bf16[1024,1152]{1,0:T(8,128)(2,1)}, bf16[1024,1152]{1,0:T(8,128)(2,1)}, u32[]{:S(2)}, u32[]{:S(2)}) %collective-permute-start.16) | collective-permute-done | bytes 2359328 | tf_op jit(solution)/shard_map/ppermute | solution.py:51
  109.5 3.1 %collective-permute-done.15.refs_2_.refs_6_ = bf16[1024,1152]{1,0:T(8,128)(2,1)} collective-permute-done((bf16[1024,1152]{1,0:T(8,128)(2,1)}, bf16[1024,1152]{1,0:T(8,128)(2,1)}, u32[]{:S(2)}, u32[]{:S(2)}) %collective-permute-start.15) | collective-permute-done | bytes 2359328 | tf_op jit(solution)/shard_map/ppermute | solution.py:51
  112.8 3.8 %halve.2 = (bf16[512,1152]{1,0:T(8,128)(2,1)}, bf16[512,1152]{1,0:T(8,128)(2,1)}, bf16[512,1152]{1,0:T(8,128)(2,1)}, bf16[512,1152]{1,0:T(8,128)(2,1)}) custom-call(bf16[1024,1152]{1,0:T(8,128)(2,1)} %collective-permute-done.13.refs_0_.refs_1_, bf16[1024,1152]{1,0:T(8,128)(2,1)} %collective-permute-done.14.refs_1_.refs_2_, ...), custom_call_target="tpu_custom_call" | custom-call | bytes 2097152 | tf_op jit(solution)/shard_map/halve/pallas_call | solution.py:223
  116.7 2.5 collective-permute-start.20
  121.9 2.7 collective-permute-start.24
  124.5 14.5 %collective-permute-done.20.refs_9_ = bf16[512,1152]{1,0:T(8,128)(2,1)S(1)} collective-permute-done((bf16[512,1152]{1,0:T(8,128)(2,1)}, bf16[512,1152]{1,0:T(8,128)(2,1)S(1)}, u32[]{:S(2)}, u32[]{:S(2)}) %collective-permute-start.20) | collective-permute-done | bytes 1179680 | tf_op jit(solution)/shard_map/ppermute | solution.py:51
  139.0 3.0 %collective-permute-done.19.refs_8_ = bf16[512,1152]{1,0:T(8,128)(2,1)} collective-permute-done((bf16[512,1152]{1,0:T(8,128)(2,1)}, bf16[512,1152]{1,0:T(8,128)(2,1)}, u32[]{:S(2)}, u32[]{:S(2)}) %collective-permute-start.19) | collective-permute-done | bytes 1179680 | tf_op jit(solution)/shard_map/ppermute | solution.py:51
  143.5 23.0 %select.12 = (bf16[2,1536,2304]{2,1,0:T(8,128)(2,1)}, bf16[2,2,192,2304]{3,2,1,0:T(8,128)(2,1)}, bf16[2,2,192,2304]{3,2,1,0:T(8,128)(2,1)}) custom-call(s32[64]{0:T(128)} %dynamic-slice_bitcast_fusion.order_ref, bf16[2,1536,128]{2,1,0:T(8,128)(2,1)} %get-tuple-element.135.pick_ref.refs_5_, bf16[2,768,1536]{2,1,0:T(8,128)(2,1)} %get-tuple-element.136.scaled_hbm, ...), custom_call_target="tpu_custom_call" | custom-call | flops 21743271936 | bytes 41030144 | tf_op jit(solution)/shard_map/select/pallas_call | solution.py:316
  166.5 11.8 %collective-permute-done.24.refs_3_.refs_7_ = bf16[1024,896]{1,0:T(8,128)(2,1)} collective-permute-done((bf16[1024,896]{1,0:T(8,128)(2,1)}, bf16[1024,896]{1,0:T(8,128)(2,1)}, u32[]{:S(2)}, u32[]{:S(2)}) %collective-permute-start.24) | collective-permute-done | bytes 1835040 | tf_op jit(solution)/shard_map/ppermute | solution.py:51
  179.6 9.1 %collective-permute-start.25 = (bf16[2,2,192,2304]{3,2,1,0:T(8,128)(2,1)}, bf16[2,2,192,2304]{3,2,1,0:T(8,128)(2,1)}, u32[]{:S(2)}, u32[]{:S(2)}) collective-permute-start(bf16[2,2,192,2304]{3,2,1,0:T(8,128)(2,1)} %get-tuple-element.161), channel_id=1, source_target_pairs={{0,1},{1,0},{2,3},{3,2},{4,5},{5,4},{6,7},{7,6},{8,9},{9,8},{10,11... | collective-permute-start | bytes 10616840 | tf_op jit(solution)/shard_map/ppermute | solution.py:602
  188.6 3.1 %halve.3 = (bf16[512,896]{1,0:T(8,128)(2,1)}, bf16[512,896]{1,0:T(8,128)(2,1)}, bf16[512,896]{1,0:T(8,128)(2,1)}, bf16[512,896]{1,0:T(8,128)(2,1)}) custom-call(bf16[1024,896]{1,0:T(8,128)(2,1)} %collective-permute-done.21.refs_0_.refs_1_, bf16[1024,896]{1,0:T(8,128)(2,1)} %collective-permute-done.22.refs_1_.refs_2_, ...), custom_call_target="tpu_custom_call" | custom-call | bytes 2097152 | tf_op jit(solution)/shard_map/halve/pallas_call | solution.py:223
  191.7 2.7 collective-permute-start.30
  194.5 1.5 collective-permute-start.27
  196.0 3.1 %fusion.4 = (bf16[2,192,1152]{2,1,0:T(8,128)(2,1)}, bf16[2,192,1152]{2,1,0:T(8,128)(2,1)}) fusion(bf16[2,2,192,2304]{3,2,1,0:T(8,128)(2,1)} %collective-permute-done.25, bf16[2,2,192,2304]{3,2,1,0:T(8,128)(2,1)S(1)} %copy-done.23), kind=kLoop, calls=%fused_computation.11 | loop fusion | flops 3538944 | bytes 5308416 | tf_op jit(solution)/shard_map/convert_element_type | solution.py:611
  199.0 2.7 collective-permute-start.26
  201.8 17.7 %upstream.1.refs_2_ = f32[2,1536,768]{2,1,0:T(8,128)} custom-call(bf16[2,1536,2304]{2,1,0:T(8,128)(2,1)} %get-tuple-element.159.refs_0_, bf16[2,768,4096]{2,1,0:T(8,128)(2,1)} %refs_1_.3), custom_call_target="tpu_custom_call" | custom-call | flops 169869312 | bytes 2359296 | tf_op jit(solution)/shard_map/upstream/pallas_call | solution.py:422
  219.5 1.5 collective-permute-done.26
  221.0 20.2 %select.13 = (bf16[2,1536,1792]{2,1,0:T(8,128)(2,1)}, bf16[2,2,192,1792]{3,2,1,0:T(8,128)(2,1)}, bf16[2,2,192,1792]{3,2,1,0:T(8,128)(2,1)}) custom-call(s32[64]{0:T(128)} %dynamic-slice_bitcast_fusion.order_ref, bf16[2,1536,128]{2,1,0:T(8,128)(2,1)} %get-tuple-element.135.pick_ref.refs_5_, bf16[2,768,1536]{2,1,0:T(8,128)(2,1)} %get-tuple-element.136.scaled_hbm, ...), custom_call_target="tpu_custom_call" | custom-call | flops 16911433728 | bytes 33690112 | tf_op jit(solution)/shard_map/select/pallas_call | solution.py:316
  241.2 2.0 collective-permute-start.31
  243.2 2.8 collective-permute-start.32
  246.0 2.2 collective-permute-done.31
  248.1 1.5 copy-done.25
  249.7 2.8 fusion.2
  252.5 2.7 collective-permute-start.33
  255.2 17.9 %finish.1 = (bf16[2,1536,768]{2,1,0:T(8,128)(2,1)}, f32[2,32,128]{2,1,0:T(8,128)}) custom-call(bf16[2,1536,1792]{2,1,0:T(8,128)(2,1)} %get-tuple-element.184.refs_0_, bf16[2,768,4096]{2,1,0:T(8,128)(2,1)} %refs_1_.3, f32[2,1536,768]{2,1,0:T(8,128)} %upstream.1.refs_2_, bf16[2,1536,768]{2,1,0:T(8,128)(2,1)} %get-tuple-element.185.refs_3_, ...), custom_call_target="tpu_custom_call" | custom-call | flops 132120576 | bytes 2359296 | tf_op jit(solution)/shard_map/finish/pallas_call | solution.py:422
  273.1 1.4 copy.27
  274.5 5.5 %all-to-all-start.1 = ((f32[32,2,128]{2,1,0:T(2,128)}), f32[32,2,128]{2,1,0:T(2,128)}, u32[]{:S(2)}, u32[]{:S(2)}) async-start(f32[32,2,128]{2,1,0:T(2,128)} %copy.27), calls=%async_computation.1 | async-start | bytes 65536 | tf_op jit(solution)/shard_map/all_to_all | solution.py:634
  280.0 10.1 %in_slot_order.1 = bf16[1,2,1536,768]{3,2,1,0:T(8,128)(2,1)} custom-call(s32[64]{0:T(128)} %reshape.45.base_ref, s32[64]{0:T(128)} %reshape.46.lead_ref, s32[64]{0:T(128)} %convert_element_type.114.count_ref, bf16[2,1536,768]{2,1,0:T(8,128)(2,1)} %get-tuple-element.187.hidden_ref), custom_call_target="tpu_custom_call" | custom-call | flops 1000000000 | bytes 12000000 | tf_op jit(solution)/shard_map/in_slot_order/pallas_call | solution.py:465
  290.1 2.7 fusion
  292.8 2.9 collective-permute-done.33
  295.7 1.9 fusion.1
  297.6 2.1 pad_maximum_fusion
  299.7 1.4 select_reduce_fusion
  (125 shorter events, 30.1 us)
Async XLA Ops:
  0.6 24.7 %collective-permute-start.1 = (bf16[128,4096]{1,0:T(8,128)(2,1)}, bf16[128,4096]{1,0:T(8,128)(2,1)S(1)}, u32[]{:S(2)}, u32[]{:S(2)}) collective-permute-start(bf16[128,4096]{1,0:T(8,128)(2,1)} %bitcast.37), channel_id=1, source_target_pairs={{0,16},{4,20},{8,24},{12,28},{16,0},{20,4},{24,8},{28,12},{32,48},... | collective-permute-start | bytes 3145736 | tf_op jit(solution)/shard_map/ppermute | solution.py:51
  5.0 40.6 %copy-start.28 = (bf16[1,128,8]{1,2,0:T(8,128)(2,1)S(1)}, bf16[1,128,8]{1,2,0:T(8,128)(2,1)}, u32[]{:S(2)}) copy-start(bf16[1,128,8]{1,2,0:T(8,128)(2,1)} %param.7) | copy-start | bytes 6148
  5.0 40.6 %copy-start.27 = (s32[1,128,8]{1,2,0:T(8,128)S(1)}, s32[1,128,8]{1,2,0:T(8,128)}, u32[]{:S(2)}) copy-start(s32[1,128,8]{1,2,0:T(8,128)} %param.8) | copy-start | bytes 12292
  5.0 15.2 %collective-permute-start = (bf16[128,2048]{1,0:T(8,128)(2,1)S(1)}, bf16[128,2048]{1,0:T(8,128)(2,1)S(1)}, u32[]{:S(2)}, u32[]{:S(2)}) collective-permute-start(bf16[128,2048]{1,0:T(8,128)(2,1)S(1)} %pad_maximum_fusion.1.refs_0_), channel_id=1, source_target_pairs={{0,32},{4,36},{8,40},{12,44},{16,48},{20,52},{24,56},{28,60},{32,6... | collective-permute-start | bytes 1572872 | tf_op jit(solution)/shard_map/ppermute | solution.py:51
  6.7 25.9 %collective-permute-start.3 = (bf16[128,2048]{1,0:T(8,128)(2,1)S(1)}, bf16[128,2048]{1,0:T(8,128)(2,1)S(1)}, u32[]{:S(2)}, u32[]{:S(2)}) collective-permute-start(bf16[128,2048]{1,0:T(8,128)(2,1)S(1)} %pad_maximum_fusion.1.refs_0_), channel_id=1, source_target_pairs={{0,96},{4,100},{8,104},{12,108},{16,112},{20,116},{24,120},{28,124... | collective-permute-start | bytes 1572872 | tf_op jit(solution)/shard_map/ppermute | solution.py:51
  9.0 20.8 %collective-permute-start.7 = (bf16[128,2048]{1,0:T(8,128)(2,1)S(1)}, bf16[128,2048]{1,0:T(8,128)(2,1)S(1)}, u32[]{:S(2)}, u32[]{:S(2)}) collective-permute-start(bf16[128,2048]{1,0:T(8,128)(2,1)S(1)} %pad_maximum_fusion.3.refs_8_), channel_id=1, source_target_pairs={{0,4},{4,8},{8,12},{12,0},{16,20},{20,24},{24,28},{28,16},{32,36},... | collective-permute-start | bytes 1572872 | tf_op jit(solution)/shard_map/ppermute | solution.py:51
  10.4 22.3 %collective-permute-start.9 = (bf16[128,2048]{1,0:T(8,128)(2,1)S(1)}, bf16[128,2048]{1,0:T(8,128)(2,1)S(1)}, u32[]{:S(2)}, u32[]{:S(2)}) collective-permute-start(bf16[128,2048]{1,0:T(8,128)(2,1)S(1)} %pad_maximum_fusion.3.refs_8_), channel_id=1, source_target_pairs={{0,12},{4,0},{8,4},{12,8},{16,28},{20,16},{24,20},{28,24},{32,44},... | collective-permute-start | bytes 1572872 | tf_op jit(solution)/shard_map/ppermute | solution.py:51
  20.2 13.1 %collective-permute-start.5 = (bf16[128,2048]{1,0:T(8,128)(2,1)S(1)}, bf16[128,2048]{1,0:T(8,128)(2,1)S(1)}, u32[]{:S(2)}, u32[]{:S(2)}) collective-permute-start(bf16[128,2048]{1,0:T(8,128)(2,1)S(1)} %collective-permute-done.refs_2_), channel_id=1, source_target_pairs={{0,32},{4,36},{8,40},{12,44},{16,48},{20,52},{24,56},{28,60},{32,6... | collective-permute-start | bytes 1572872 | tf_op jit(solution)/shard_map/ppermute | solution.py:51
  25.5 13.9 %collective-permute-start.4 = (bf16[128,2048]{1,0:T(8,128)(2,1)S(1)}, bf16[128,2048]{1,0:T(8,128)(2,1)S(1)}, u32[]{:S(2)}, u32[]{:S(2)}) collective-permute-start(bf16[128,2048]{1,0:T(8,128)(2,1)S(1)} %pad_maximum_fusion.2.refs_1_), channel_id=1, source_target_pairs={{0,96},{4,100},{8,104},{12,108},{16,112},{20,116},{24,120},{28,124... | collective-permute-start | bytes 1572872 | tf_op jit(solution)/shard_map/ppermute | solution.py:51
  29.8 29.9 %copy-start = (bf16[128,2048]{1,0:T(8,128)(2,1)}, bf16[128,2048]{1,0:T(8,128)(2,1)S(1)}, u32[]{:S(2)}) copy-start(bf16[128,2048]{1,0:T(8,128)(2,1)S(1)} %collective-permute-done.7.refs_10_) | copy-start | bytes 1572868
  29.8 13.0 %collective-permute-start.10 = (bf16[128,2048]{1,0:T(8,128)(2,1)S(1)}, bf16[128,2048]{1,0:T(8,128)(2,1)S(1)}, u32[]{:S(2)}, u32[]{:S(2)}) collective-permute-start(bf16[128,2048]{1,0:T(8,128)(2,1)S(1)} %pad_maximum_fusion.4.refs_9_), channel_id=1, source_target_pairs={{0,12},{4,0},{8,4},{12,8},{16,28},{20,16},{24,20},{28,24},{32,44},... | collective-permute-start | bytes 1572872 | tf_op jit(solution)/shard_map/ppermute | solution.py:51
  32.6 23.8 %collective-permute-start.11 = (bf16[128,2048]{1,0:T(8,128)(2,1)S(1)}, bf16[128,2048]{1,0:T(8,128)(2,1)S(1)}, u32[]{:S(2)}, u32[]{:S(2)}) collective-permute-start(bf16[128,2048]{1,0:T(8,128)(2,1)S(1)} %collective-permute-done.7.refs_10_), channel_id=1, source_target_pairs={{0,4},{4,8},{8,12},{12,0},{16,20},{20,24},{24,28},{28,16},{32,36},... | collective-permute-start | bytes 1572872 | tf_op jit(solution)/shard_map/ppermute | solution.py:51
  32.6 27.1 %copy-start.2 = (bf16[128,2048]{1,0:T(8,128)(2,1)}, bf16[128,2048]{1,0:T(8,128)(2,1)S(1)}, u32[]{:S(2)}) copy-start(bf16[128,2048]{1,0:T(8,128)(2,1)S(1)} %collective-permute-done.9.refs_12_) | copy-start | bytes 1572868
  32.7 23.8 %collective-permute-start.8 = (bf16[128,2048]{1,0:T(8,128)(2,1)S(1)}, bf16[128,2048]{1,0:T(8,128)(2,1)S(1)}, u32[]{:S(2)}, u32[]{:S(2)}) collective-permute-start(bf16[128,2048]{1,0:T(8,128)(2,1)S(1)} %pad_maximum_fusion.4.refs_9_), channel_id=1, source_target_pairs={{0,4},{4,8},{8,12},{12,0},{16,20},{20,24},{24,28},{28,16},{32,36},... | collective-permute-start | bytes 1572872 | tf_op jit(solution)/shard_map/ppermute | solution.py:51
  33.3 26.5 %copy-start.4 = (bf16[128,2048]{1,0:T(8,128)(2,1)}, bf16[128,2048]{1,0:T(8,128)(2,1)S(1)}, u32[]{:S(2)}) copy-start(bf16[128,2048]{1,0:T(8,128)(2,1)S(1)} %collective-permute-done.5.refs_6_) | copy-start | bytes 1572868
  33.3 23.2 %collective-permute-start.2 = (bf16[128,2048]{1,0:T(8,128)(2,1)S(1)}, bf16[128,2048]{1,0:T(8,128)(2,1)S(1)}, u32[]{:S(2)}, u32[]{:S(2)}) collective-permute-start(bf16[128,2048]{1,0:T(8,128)(2,1)S(1)} %pad_maximum_fusion.2.refs_1_), channel_id=1, source_target_pairs={{0,32},{4,36},{8,40},{12,44},{16,48},{20,52},{24,56},{28,60},{32,6... | collective-permute-start | bytes 1572872 | tf_op jit(solution)/shard_map/ppermute | solution.py:51
  39.4 20.4 %copy-start.6 = (bf16[128,2048]{1,0:T(8,128)(2,1)}, bf16[128,2048]{1,0:T(8,128)(2,1)S(1)}, u32[]{:S(2)}) copy-start(bf16[128,2048]{1,0:T(8,128)(2,1)S(1)} %collective-permute-done.4.refs_5_) | copy-start | bytes 1572868
  39.4 17.1 %collective-permute-start.6 = (bf16[128,2048]{1,0:T(8,128)(2,1)S(1)}, bf16[128,2048]{1,0:T(8,128)(2,1)S(1)}, u32[]{:S(2)}, u32[]{:S(2)}) collective-permute-start(bf16[128,2048]{1,0:T(8,128)(2,1)S(1)} %collective-permute-done.4.refs_5_), channel_id=1, source_target_pairs={{0,96},{4,100},{8,104},{12,108},{16,112},{20,116},{24,120},{28,124... | collective-permute-start | bytes 1572872 | tf_op jit(solution)/shard_map/ppermute | solution.py:51
  42.8 16.9 %copy-start.8 = (bf16[128,2048]{1,0:T(8,128)(2,1)}, bf16[128,2048]{1,0:T(8,128)(2,1)S(1)}, u32[]{:S(2)}) copy-start(bf16[128,2048]{1,0:T(8,128)(2,1)S(1)} %collective-permute-done.10.refs_13_) | copy-start | bytes 1572868
  42.8 13.7 %collective-permute-start.12 = (bf16[128,2048]{1,0:T(8,128)(2,1)S(1)}, bf16[128,2048]{1,0:T(8,128)(2,1)S(1)}, u32[]{:S(2)}, u32[]{:S(2)}) collective-permute-start(bf16[128,2048]{1,0:T(8,128)(2,1)S(1)} %collective-permute-done.10.refs_13_), channel_id=1, source_target_pairs={{0,12},{4,0},{8,4},{12,8},{16,28},{20,16},{24,20},{28,24},{32,44},... | collective-permute-start | bytes 1572872 | tf_op jit(solution)/shard_map/ppermute | solution.py:51
  56.5 3.3 %copy-start.12 = (bf16[128,2048]{1,0:T(8,128)(2,1)}, bf16[128,2048]{1,0:T(8,128)(2,1)S(1)}, u32[]{:S(2)}) copy-start(bf16[128,2048]{1,0:T(8,128)(2,1)S(1)} %collective-permute-done.8.refs_11_) | copy-start | bytes 1572868
  59.8 49.6 %collective-permute-start.16 = (bf16[1024,1152]{1,0:T(8,128)(2,1)}, bf16[1024,1152]{1,0:T(8,128)(2,1)}, u32[]{:S(2)}, u32[]{:S(2)}) collective-permute-start(bf16[1024,1152]{1,0:T(8,128)(2,1)} %get-tuple-element.152.refs_5_), channel_id=1, source_target_pairs={{0,96},{4,100},{8,104},{12,108},{16,112},{20,116},{24,120},{28,124... | collective-permute-start | bytes 7077896 | tf_op jit(solution)/shard_map/ppermute | solution.py:51
  62.0 50.6 %collective-permute-start.15 = (bf16[1024,1152]{1,0:T(8,128)(2,1)}, bf16[1024,1152]{1,0:T(8,128)(2,1)}, u32[]{:S(2)}, u32[]{:S(2)}) collective-permute-start(bf16[1024,1152]{1,0:T(8,128)(2,1)} %get-tuple-element.152.refs_5_), channel_id=1, source_target_pairs={{0,32},{4,36},{8,40},{12,44},{16,48},{20,52},{24,56},{28,60},{32,6... | collective-permute-start | bytes 7077896 | tf_op jit(solution)/shard_map/ppermute | solution.py:51
  62.0 50.6 %collective-permute-start.14 = (bf16[1024,1152]{1,0:T(8,128)(2,1)}, bf16[1024,1152]{1,0:T(8,128)(2,1)}, u32[]{:S(2)}, u32[]{:S(2)}) collective-permute-start(bf16[1024,1152]{1,0:T(8,128)(2,1)} %get-tuple-element.141.refs_0_), channel_id=1, source_target_pairs={{0,12},{4,0},{8,4},{12,8},{16,28},{20,16},{24,20},{28,24},{32,44},... | collective-permute-start | bytes 7077896 | tf_op jit(solution)/shard_map/ppermute | solution.py:51
  63.1 49.7 %collective-permute-start.13 = (bf16[1024,1152]{1,0:T(8,128)(2,1)}, bf16[1024,1152]{1,0:T(8,128)(2,1)}, u32[]{:S(2)}, u32[]{:S(2)}) collective-permute-start(bf16[1024,1152]{1,0:T(8,128)(2,1)} %get-tuple-element.141.refs_0_), channel_id=1, source_target_pairs={{0,4},{4,8},{8,12},{12,0},{16,20},{20,24},{24,28},{28,16},{32,36},... | collective-permute-start | bytes 7077896 | tf_op jit(solution)/shard_map/ppermute | solution.py:51
  109.5 32.6 %copy-start.21 = (bf16[1024,896]{1,0:T(8,128)(2,1)S(1)}, bf16[1024,896]{1,0:T(8,128)(2,1)}, u32[]{:S(2)}) copy-start(bf16[1024,896]{1,0:T(8,128)(2,1)} %copy-done.20) | copy-start | bytes 5505028
  116.7 22.4 %collective-permute-start.20 = (bf16[512,1152]{1,0:T(8,128)(2,1)}, bf16[512,1152]{1,0:T(8,128)(2,1)S(1)}, u32[]{:S(2)}, u32[]{:S(2)}) collective-permute-start(bf16[512,1152]{1,0:T(8,128)(2,1)} %get-tuple-element.157), channel_id=1, source_target_pairs={{0,96},{4,100},{8,104},{12,108},{16,112},{20,116},{24,120},{28,124... | collective-permute-start | bytes 3538952 | tf_op jit(solution)/shard_map/ppermute | solution.py:51
  119.1 22.9 %collective-permute-start.19 = (bf16[512,1152]{1,0:T(8,128)(2,1)}, bf16[512,1152]{1,0:T(8,128)(2,1)}, u32[]{:S(2)}, u32[]{:S(2)}) collective-permute-start(bf16[512,1152]{1,0:T(8,128)(2,1)} %get-tuple-element.155), channel_id=1, source_target_pairs={{0,32},{4,36},{8,40},{12,44},{16,48},{20,52},{24,56},{28,60},{32,6... | collective-permute-start | bytes 3538952 | tf_op jit(solution)/shard_map/ppermute | solution.py:51
  119.1 23.5 %collective-permute-start.18 = (bf16[512,1152]{1,0:T(8,128)(2,1)}, bf16[512,1152]{1,0:T(8,128)(2,1)}, u32[]{:S(2)}, u32[]{:S(2)}) collective-permute-start(bf16[512,1152]{1,0:T(8,128)(2,1)} %get-tuple-element.150), channel_id=1, source_target_pairs={{0,12},{4,0},{8,4},{12,8},{16,28},{20,16},{24,20},{28,24},{32,44},... | collective-permute-start | bytes 3538952 | tf_op jit(solution)/shard_map/ppermute | solution.py:51
  119.4 24.1 %collective-permute-start.17 = (bf16[512,1152]{1,0:T(8,128)(2,1)}, bf16[512,1152]{1,0:T(8,128)(2,1)}, u32[]{:S(2)}, u32[]{:S(2)}) collective-permute-start(bf16[512,1152]{1,0:T(8,128)(2,1)} %get-tuple-element.148), channel_id=1, source_target_pairs={{0,4},{4,8},{8,12},{12,0},{16,20},{20,24},{24,28},{28,16},{32,36},... | collective-permute-start | bytes 3538952 | tf_op jit(solution)/shard_map/ppermute | solution.py:51
  121.9 56.5 %collective-permute-start.24 = (bf16[1024,896]{1,0:T(8,128)(2,1)}, bf16[1024,896]{1,0:T(8,128)(2,1)}, u32[]{:S(2)}, u32[]{:S(2)}) collective-permute-start(bf16[1024,896]{1,0:T(8,128)(2,1)} %copy-done.22), channel_id=1, source_target_pairs={{0,96},{4,100},{8,104},{12,108},{16,112},{20,116},{24,120},{28,124... | collective-permute-start | bytes 5505032 | tf_op jit(solution)/shard_map/ppermute | solution.py:51
  139.0 4.5 %copy-start.29 = (bf16[512,1152]{1,0:T(8,128)(2,1)}, bf16[512,1152]{1,0:T(8,128)(2,1)S(1)}, u32[]{:S(2)}) copy-start(bf16[512,1152]{1,0:T(8,128)(2,1)S(1)} %collective-permute-done.20.refs_9_) | copy-start | bytes 3538948
  139.0 40.5 %collective-permute-start.23 = (bf16[1024,896]{1,0:T(8,128)(2,1)}, bf16[1024,896]{1,0:T(8,128)(2,1)}, u32[]{:S(2)}, u32[]{:S(2)}) collective-permute-start(bf16[1024,896]{1,0:T(8,128)(2,1)} %copy-done.22), channel_id=1, source_target_pairs={{0,32},{4,36},{8,40},{12,44},{16,48},{20,52},{24,56},{28,60},{32,6... | collective-permute-start | bytes 5505032 | tf_op jit(solution)/shard_map/ppermute | solution.py:51
  142.1 37.5 %collective-permute-start.22 = (bf16[1024,896]{1,0:T(8,128)(2,1)S(1)}, bf16[1024,896]{1,0:T(8,128)(2,1)}, u32[]{:S(2)}, u32[]{:S(2)}) collective-permute-start(bf16[1024,896]{1,0:T(8,128)(2,1)S(1)} %copy-done.21), channel_id=1, source_target_pairs={{0,12},{4,0},{8,4},{12,8},{16,28},{20,16},{24,20},{28,24},{32,44},... | collective-permute-start | bytes 5505032 | tf_op jit(solution)/shard_map/ppermute | solution.py:51
  142.6 36.9 %collective-permute-start.21 = (bf16[1024,896]{1,0:T(8,128)(2,1)S(1)}, bf16[1024,896]{1,0:T(8,128)(2,1)}, u32[]{:S(2)}, u32[]{:S(2)}) collective-permute-start(bf16[1024,896]{1,0:T(8,128)(2,1)S(1)} %copy-done.21), channel_id=1, source_target_pairs={{0,4},{4,8},{8,12},{12,0},{16,20},{20,24},{24,28},{28,16},{32,36},... | collective-permute-start | bytes 5505032 | tf_op jit(solution)/shard_map/ppermute | solution.py:51
  179.6 16.4 %copy-start.23 = (bf16[2,2,192,2304]{3,2,1,0:T(8,128)(2,1)S(1)}, bf16[2,2,192,2304]{3,2,1,0:T(8,128)(2,1)}, u32[]{:S(2)}) copy-start(bf16[2,2,192,2304]{3,2,1,0:T(8,128)(2,1)} %get-tuple-element.162) | copy-start | bytes 10616836
  179.6 16.4 %collective-permute-start.25 = (bf16[2,2,192,2304]{3,2,1,0:T(8,128)(2,1)}, bf16[2,2,192,2304]{3,2,1,0:T(8,128)(2,1)}, u32[]{:S(2)}, u32[]{:S(2)}) collective-permute-start(bf16[2,2,192,2304]{3,2,1,0:T(8,128)(2,1)} %get-tuple-element.161), channel_id=1, source_target_pairs={{0,1},{1,0},{2,3},{3,2},{4,5},{5,4},{6,7},{7,6},{8,9},{9,8},{10,11... | collective-permute-start | bytes 10616840 | tf_op jit(solution)/shard_map/ppermute | solution.py:602
  191.7 27.8 %collective-permute-start.30 = (bf16[512,896]{1,0:T(8,128)(2,1)}, bf16[512,896]{1,0:T(8,128)(2,1)}, u32[]{:S(2)}, u32[]{:S(2)}) collective-permute-start(bf16[512,896]{1,0:T(8,128)(2,1)} %get-tuple-element.179), channel_id=1, source_target_pairs={{0,96},{4,100},{8,104},{12,108},{16,112},{20,116},{24,120},{28,124... | collective-permute-start | bytes 2752520 | tf_op jit(solution)/shard_map/ppermute | solution.py:51
  194.5 26.5 %collective-permute-start.29 = (bf16[512,896]{1,0:T(8,128)(2,1)}, bf16[512,896]{1,0:T(8,128)(2,1)}, u32[]{:S(2)}, u32[]{:S(2)}) collective-permute-start(bf16[512,896]{1,0:T(8,128)(2,1)} %get-tuple-element.177), channel_id=1, source_target_pairs={{0,32},{4,36},{8,40},{12,44},{16,48},{20,52},{24,56},{28,60},{32,6... | collective-permute-start | bytes 2752520 | tf_op jit(solution)/shard_map/ppermute | solution.py:51
  194.5 26.5 %collective-permute-start.28 = (bf16[512,896]{1,0:T(8,128)(2,1)}, bf16[512,896]{1,0:T(8,128)(2,1)}, u32[]{:S(2)}, u32[]{:S(2)}) collective-permute-start(bf16[512,896]{1,0:T(8,128)(2,1)} %get-tuple-element.172), channel_id=1, source_target_pairs={{0,12},{4,0},{8,4},{12,8},{16,28},{20,16},{24,20},{28,24},{32,44},... | collective-permute-start | bytes 2752520 | tf_op jit(solution)/shard_map/ppermute | solution.py:51
  194.5 26.5 %collective-permute-start.27 = (bf16[512,896]{1,0:T(8,128)(2,1)}, bf16[512,896]{1,0:T(8,128)(2,1)}, u32[]{:S(2)}, u32[]{:S(2)}) collective-permute-start(bf16[512,896]{1,0:T(8,128)(2,1)} %get-tuple-element.170), channel_id=1, source_target_pairs={{0,4},{4,8},{8,12},{12,0},{16,20},{20,24},{24,28},{28,16},{32,36},... | collective-permute-start | bytes 2752520 | tf_op jit(solution)/shard_map/ppermute | solution.py:51
  199.0 21.9 %collective-permute-start.26 = (bf16[2,192,1152]{2,1,0:T(8,128)(2,1)}, bf16[2,192,1152]{2,1,0:T(8,128)(2,1)}, u32[]{:S(2)}, u32[]{:S(2)}) collective-permute-start(bf16[2,192,1152]{2,1,0:T(8,128)(2,1)} %get-tuple-element.195), channel_id=1, source_target_pairs={{0,2},{2,0},{1,3},{3,1},{4,6},{6,4},{5,7},{7,5},{8,10},{10,8},{9,1... | collective-permute-start | bytes 2654216 | tf_op jit(solution)/shard_map/ppermute | solution.py:612
  241.2 7.0 %collective-permute-start.31 = (bf16[2,2,192,1792]{3,2,1,0:T(8,128)(2,1)}, bf16[2,2,192,1792]{3,2,1,0:T(8,128)(2,1)S(1)}, u32[]{:S(2)}, u32[]{:S(2)}) collective-permute-start(bf16[2,2,192,1792]{3,2,1,0:T(8,128)(2,1)} %get-tuple-element.182), channel_id=1, source_target_pairs={{0,1},{1,0},{2,3},{3,2},{4,5},{5,4},{6,7},{7,6},{8,9},{9,8},{10,11... | collective-permute-start | bytes 8257544 | tf_op jit(solution)/shard_map/ppermute | solution.py:602
  243.2 29.9 %collective-permute-start.32 = (bf16[2,192,1152]{2,1,0:T(8,128)(2,1)}, bf16[2,192,1152]{2,1,0:T(8,128)(2,1)}, u32[]{:S(2)}, u32[]{:S(2)}) collective-permute-start(bf16[2,192,1152]{2,1,0:T(8,128)(2,1)} %get-tuple-element.190), channel_id=1, source_target_pairs={{0,2},{2,0},{1,3},{3,1},{4,6},{6,4},{5,7},{7,5},{8,10},{10,8},{9,1... | collective-permute-start | bytes 2654216 | tf_op jit(solution)/shard_map/ppermute | solution.py:612
  252.5 43.2 %collective-permute-start.33 = (bf16[2,192,1792]{2,1,0:T(8,128)(2,1)}, bf16[2,192,1792]{2,1,0:T(8,128)(2,1)}, u32[]{:S(2)}, u32[]{:S(2)}) collective-permute-start(bf16[2,192,1792]{2,1,0:T(8,128)(2,1)} %fusion.2), channel_id=1, source_target_pairs={{0,2},{2,0},{1,3},{3,1},{4,6},{6,4},{5,7},{7,5},{8,10},{10,8},{9,1... | collective-permute-start | bytes 4128776 | tf_op jit(solution)/shard_map/ppermute | solution.py:612
  274.5 25.2 %all-to-all-start.1 = ((f32[32,2,128]{2,1,0:T(2,128)}), f32[32,2,128]{2,1,0:T(2,128)}, u32[]{:S(2)}, u32[]{:S(2)}) async-start(f32[32,2,128]{2,1,0:T(2,128)} %copy.27), calls=%async_computation.1 | async-start | bytes 65536 | tf_op jit(solution)/shard_map/all_to_all | solution.py:634
  290.1 5.6 %copy-start.24 = (bf16[2,2,192,1792]{3,2,1,0:T(8,128)(2,1)S(1)}, bf16[2,2,192,1792]{3,2,1,0:T(8,128)(2,1)}, u32[]{:S(2)}) copy-start(bf16[2,2,192,1792]{3,2,1,0:T(8,128)(2,1)} %get-tuple-element.183) | copy-start | bytes 8257540
  290.1 5.6 %copy-start.26 = (bf16[2,2,192,1792]{3,2,1,0:T(8,128)(2,1)S(1)}, bf16[2,2,192,1792]{3,2,1,0:T(8,128)(2,1)}, u32[]{:S(2)}) copy-start(bf16[2,2,192,1792]{3,2,1,0:T(8,128)(2,1)} %copy-done.25) | copy-start | bytes 8257540
  (17 other events, 27.8 us)

commit v4 on v3

--- a/solution.py
+++ b/solution.py
@@ -630,7 +630,9 @@
         across = jnp.concatenate(parts, axis=2).astype(jnp.float32)
         pair = met.astype(jnp.float32) + stay.astype(jnp.float32)
         finished.append((pair + across).astype(jnp.bfloat16))
-    weight_grad = jnp.concatenate(finished, axis=2)
+    blank = jnp.zeros((EXP, SHARE, STAGES[-1]), jnp.bfloat16)
+    weight_grad = after(jnp.concatenate(finished[:-1] + [blank], axis=2), sums)
+    weight_grad = lax.dynamic_update_slice(weight_grad, finished[-1], (0, 0, starts[-1]))
     back = lax.all_to_all(
         jnp.swapaxes(sums, 0, 1), "expert", split_axis=0, concat_axis=0, tiled=True
     ).reshape(SOURCES * EXP, TOK)

time: 302 us -> 301 us (level)
  transfers between devices with their start and end apart: 35 -> 35, of which waited for: 14 -> 15; matrix products, arithmetic and copies ran while one was open for 7% -> 7% of each run, Pallas kernels for 30% -> 30%
where the time goes in v4:
time: 301 us; the launch traced here: 300 us
  Pallas kernels  117 us (39%)
  waiting for transfers between devices  72.1 us (24%)
  starting transfers between devices  62.8 us (21%)
  local copies, waits for them, and re-layouts  21.7 us (7%)
  other arithmetic  14.4 us (5%)
  blocking collectives  10.8 us (4%)
    ppermute x29, waiting for transfers between devices, send(): return lax.ppermute(value, 'expert', pairs)  64.8 us
    pallas_call x2, Pallas kernels, select(): pl.pallas_call(functools.partial(select_kernel, width), in_specs=[smem, v...  43.1 us
    ppermute x29, starting transfers between devices, send(): return lax.ppermute(value, 'expert', pairs)  38.1 us
    pallas_call x2, Pallas kernels, upstream(): pl.pallas_call(functools.partial(upstream_kernel, total is not None, last...  35.6 us
    pallas_call x1, Pallas kernels, prepare(): pl.pallas_call(prepare_kernel, grid_spec=pltpu.PrefetchScalarGridSpec(num...  16.9 us
    unnamed x60, local copies, waits for them, and re-layouts  15.1 us
    ppermute x2, starting transfers between devices, body(): met = lax.ppermute(leaving, 'replica', CORE_SWAP)  11.1 us
    all_to_all x1, blocking collectives, send_gates(): lax.all_to_all(dense, 'expert', split_axis=0, concat_axis=0, tiled=True)  10.8 us
  transfers between devices with their start and end apart: 35, of which 15 were waited for; matrix products, arithmetic and copies ran while one was open for 7% of the time, Pallas kernels for 30%

profile of v4, /device:TPU:1, one launch (start us, length us, event | category | flops | bytes accessed | tf_op | source)
XLA Modules:
  0.0 300.0 jit_solution(10510365301692686944)
XLA Ops:
  0.6 2.1 collective-permute-start.1
  5.0 1.7 collective-permute-start
  6.7 2.2 collective-permute-start.3
  9.0 1.4 collective-permute-start.7
  10.4 1.5 collective-permute-start.9
  11.9 8.3 %collective-permute-done.refs_2_ = bf16[128,2048]{1,0:T(8,128)(2,1)S(1)} collective-permute-done((bf16[128,2048]{1,0:T(8,128)(2,1)S(1)}, bf16[128,2048]{1,0:T(8,128)(2,1)S(1)}, u32[]{:S(2)}, u32[]{:S(2)}) %collective-permute-start) | collective-permute-done | bytes 524320 | tf_op jit(solution)/shard_map/ppermute | solution.py:51
  20.2 5.2 %collective-permute-done.1 = bf16[128,4096]{1,0:T(8,128)(2,1)S(1)} collective-permute-done((bf16[128,4096]{1,0:T(8,128)(2,1)}, bf16[128,4096]{1,0:T(8,128)(2,1)S(1)}, u32[]{:S(2)}, u32[]{:S(2)}) %collective-permute-start.1) | collective-permute-done | bytes 1048608 | tf_op jit(solution)/shard_map/ppermute | solution.py:51
  25.5 4.3 %collective-permute-start.4 = (bf16[128,2048]{1,0:T(8,128)(2,1)S(1)}, bf16[128,2048]{1,0:T(8,128)(2,1)S(1)}, u32[]{:S(2)}, u32[]{:S(2)}) collective-permute-start(bf16[128,2048]{1,0:T(8,128)(2,1)S(1)} %pad_maximum_fusion.1.refs_1_), channel_id=1, source_target_pairs={{0,96},{4,100},{8,104},{12,108},{16,112},{20,116},{24,120},{28,124... | collective-permute-start | bytes 1572872 | tf_op jit(solution)/shard_map/ppermute | solution.py:51
  29.8 2.8 collective-permute-start.10
  33.3 6.2 %collective-permute-done.4.refs_5_ = bf16[128,2048]{1,0:T(8,128)(2,1)S(1)} collective-permute-done((bf16[128,2048]{1,0:T(8,128)(2,1)S(1)}, bf16[128,2048]{1,0:T(8,128)(2,1)S(1)}, u32[]{:S(2)}, u32[]{:S(2)}) %collective-permute-start.4) | collective-permute-done | bytes 524320 | tf_op jit(solution)/shard_map/ppermute | solution.py:51
  39.4 3.4 %collective-permute-start.6 = (bf16[128,2048]{1,0:T(8,128)(2,1)S(1)}, bf16[128,2048]{1,0:T(8,128)(2,1)S(1)}, u32[]{:S(2)}, u32[]{:S(2)}) collective-permute-start(bf16[128,2048]{1,0:T(8,128)(2,1)S(1)} %collective-permute-done.4.refs_5_), channel_id=1, source_target_pairs={{0,96},{4,100},{8,104},{12,108},{16,112},{20,116},{24,120},{28,124... | collective-permute-start | bytes 1572872 | tf_op jit(solution)/shard_map/ppermute | solution.py:51
  42.8 2.7 collective-permute-start.12
  45.6 10.8 %all_to_all.10 = bf16[32,2,128]{2,1,0:T(2,128)(2,1)S(1)} all-to-all(bf16[32,2,128]{2,1,0:T(2,128)(2,1)S(1)} %bitcast.43), channel_id=1, replica_groups=mesh['expert'=32,'replica'=4] {'expert'}, dimensions={0} | all-to-all | bytes 32768 | tf_op jit(solution)/shard_map/all_to_all | solution.py:496
  56.5 3.2 %join.2 = (bf16[1024,1152]{1,0:T(8,128)(2,1)}, bf16[1024,1152]{1,0:T(8,128)(2,1)}) custom-call(bf16[128,2048]{1,0:T(8,128)(2,1)S(1)} %pad_maximum_fusion.refs_0_, bf16[128,2048]{1,0:T(8,128)(2,1)S(1)} %pad_maximum_fusion.1.refs_1_, bf16[128,2048]{1,0:T(8,128)(2,1)S(1)} %collective-permute-done.refs_2_, bf16[128,2048]{1,0:T(8,128)(2,1)S(1)} %collective-permute-done.2.refs_3_, ...), custom_call_target="tpu_custom_call" | custom-call | bytes 2097152 | tf_op jit(solution)/shard_map/join/pallas_call | solution.py:187
  59.8 2.2 collective-permute-start.16
  76.1 1.3 copy-done.20
  81.9 16.9 %prepare.1 = (bf16[2,768,1536]{2,1,0:T(8,128)(2,1)}, bf16[2,1536,768]{2,1,0:T(8,128)(2,1)}, f32[2,1536,128]{2,1,0:T(8,128)}, bf16[2,1536,128]{2,1,0:T(8,128)(2,1)}) custom-call(s32[64]{0:T(128)} %reshape.45.base_ref, s32[64]{0:T(128)} %reshape.46.lead_ref, s32[64]{0:T(128)} %convert_element_type.114.count_ref, s32[2]{0:T(128)} %pad_add_fusion.place_ref, ...), custom_call_target="tpu_custom_call" | custom-call | flops 1000000000 | bytes 16000000 | tf_op jit(solution)/shard_map/prepare/pallas_call | solution.py:120
  98.8 10.7 %collective-permute-done.16.refs_3_.refs_7_ = bf16[1024,1152]{1,0:T(8,128)(2,1)} collective-permute-done((bf16[1024,1152]{1,0:T(8,128)(2,1)}, bf16[1024,1152]{1,0:T(8,128)(2,1)}, u32[]{:S(2)}, u32[]{:S(2)}) %collective-permute-start.16) | collective-permute-done | bytes 2359328 | tf_op jit(solution)/shard_map/ppermute | solution.py:51
  109.5 3.1 %collective-permute-done.15.refs_2_.refs_6_ = bf16[1024,1152]{1,0:T(8,128)(2,1)} collective-permute-done((bf16[1024,1152]{1,0:T(8,128)(2,1)}, bf16[1024,1152]{1,0:T(8,128)(2,1)}, u32[]{:S(2)}, u32[]{:S(2)}) %collective-permute-start.15) | collective-permute-done | bytes 2359328 | tf_op jit(solution)/shard_map/ppermute | solution.py:51
  112.8 3.8 %halve.2 = (bf16[512,1152]{1,0:T(8,128)(2,1)}, bf16[512,1152]{1,0:T(8,128)(2,1)}, bf16[512,1152]{1,0:T(8,128)(2,1)}, bf16[512,1152]{1,0:T(8,128)(2,1)}) custom-call(bf16[1024,1152]{1,0:T(8,128)(2,1)} %collective-permute-done.13.refs_0_.refs_1_, bf16[1024,1152]{1,0:T(8,128)(2,1)} %collective-permute-done.14.refs_1_.refs_2_, ...), custom_call_target="tpu_custom_call" | custom-call | bytes 2097152 | tf_op jit(solution)/shard_map/halve/pallas_call | solution.py:223
  116.7 2.5 collective-permute-start.20
  120.6 1.3 dynamic-slice_bitcast_fusion.order_ref
  121.9 2.7 collective-permute-start.24
  124.5 14.5 %collective-permute-done.20.refs_9_ = bf16[512,1152]{1,0:T(8,128)(2,1)S(1)} collective-permute-done((bf16[512,1152]{1,0:T(8,128)(2,1)}, bf16[512,1152]{1,0:T(8,128)(2,1)S(1)}, u32[]{:S(2)}, u32[]{:S(2)}) %collective-permute-start.20) | collective-permute-done | bytes 1179680 | tf_op jit(solution)/shard_map/ppermute | solution.py:51
  139.0 3.0 %collective-permute-done.19.refs_8_ = bf16[512,1152]{1,0:T(8,128)(2,1)} collective-permute-done((bf16[512,1152]{1,0:T(8,128)(2,1)}, bf16[512,1152]{1,0:T(8,128)(2,1)}, u32[]{:S(2)}, u32[]{:S(2)}) %collective-permute-start.19) | collective-permute-done | bytes 1179680 | tf_op jit(solution)/shard_map/ppermute | solution.py:51
  143.5 23.0 %select.13 = (bf16[2,1536,2304]{2,1,0:T(8,128)(2,1)}, bf16[2,2,192,2304]{3,2,1,0:T(8,128)(2,1)}, bf16[2,2,192,2304]{3,2,1,0:T(8,128)(2,1)}) custom-call(s32[64]{0:T(128)} %dynamic-slice_bitcast_fusion.order_ref, bf16[2,1536,128]{2,1,0:T(8,128)(2,1)} %get-tuple-element.136.pick_ref.refs_5_, bf16[2,768,1536]{2,1,0:T(8,128)(2,1)} %get-tuple-element.137.scaled_hbm, ...), custom_call_target="tpu_custom_call" | custom-call | flops 21743271936 | bytes 41030144 | tf_op jit(solution)/shard_map/select/pallas_call | solution.py:316
  166.5 11.8 %collective-permute-done.24.refs_3_.refs_7_ = bf16[1024,896]{1,0:T(8,128)(2,1)} collective-permute-done((bf16[1024,896]{1,0:T(8,128)(2,1)}, bf16[1024,896]{1,0:T(8,128)(2,1)}, u32[]{:S(2)}, u32[]{:S(2)}) %collective-permute-start.24) | collective-permute-done | bytes 1835040 | tf_op jit(solution)/shard_map/ppermute | solution.py:51
  179.6 9.1 %collective-permute-start.25 = (bf16[2,2,192,2304]{3,2,1,0:T(8,128)(2,1)}, bf16[2,2,192,2304]{3,2,1,0:T(8,128)(2,1)}, u32[]{:S(2)}, u32[]{:S(2)}) collective-permute-start(bf16[2,2,192,2304]{3,2,1,0:T(8,128)(2,1)} %get-tuple-element.162), channel_id=1, source_target_pairs={{0,1},{1,0},{2,3},{3,2},{4,5},{5,4},{6,7},{7,6},{8,9},{9,8},{10,11... | collective-permute-start | bytes 10616840 | tf_op jit(solution)/shard_map/ppermute | solution.py:602
  188.6 3.1 %halve.3 = (bf16[512,896]{1,0:T(8,128)(2,1)}, bf16[512,896]{1,0:T(8,128)(2,1)}, bf16[512,896]{1,0:T(8,128)(2,1)}, bf16[512,896]{1,0:T(8,128)(2,1)}) custom-call(bf16[1024,896]{1,0:T(8,128)(2,1)} %collective-permute-done.21.refs_0_.refs_1_, bf16[1024,896]{1,0:T(8,128)(2,1)} %collective-permute-done.22.refs_1_.refs_2_, ...), custom_call_target="tpu_custom_call" | custom-call | bytes 2097152 | tf_op jit(solution)/shard_map/halve/pallas_call | solution.py:223
  191.7 2.7 collective-permute-start.30
  194.5 1.5 collective-permute-start.27
  196.0 3.1 %fusion.5 = (bf16[2,192,1152]{2,1,0:T(8,128)(2,1)}, bf16[2,192,1152]{2,1,0:T(8,128)(2,1)}) fusion(bf16[2,2,192,2304]{3,2,1,0:T(8,128)(2,1)} %collective-permute-done.25, bf16[2,2,192,2304]{3,2,1,0:T(8,128)(2,1)S(1)} %copy-done.23), kind=kLoop, calls=%fused_computation.11 | loop fusion | flops 3538944 | bytes 5308416 | tf_op jit(solution)/shard_map/convert_element_type | solution.py:611
  199.0 2.7 collective-permute-start.26
  201.8 17.7 %upstream.1.refs_2_ = f32[2,1536,768]{2,1,0:T(8,128)} custom-call(bf16[2,1536,2304]{2,1,0:T(8,128)(2,1)} %get-tuple-element.160.refs_0_, bf16[2,768,4096]{2,1,0:T(8,128)(2,1)} %refs_1_.3), custom_call_target="tpu_custom_call" | custom-call | flops 169869312 | bytes 2359296 | tf_op jit(solution)/shard_map/upstream/pallas_call | solution.py:422
  219.5 1.5 collective-permute-done.26
  221.0 20.2 %select.14 = (bf16[2,1536,1792]{2,1,0:T(8,128)(2,1)}, bf16[2,2,192,1792]{3,2,1,0:T(8,128)(2,1)}, bf16[2,2,192,1792]{3,2,1,0:T(8,128)(2,1)}) custom-call(s32[64]{0:T(128)} %dynamic-slice_bitcast_fusion.order_ref, bf16[2,1536,128]{2,1,0:T(8,128)(2,1)} %get-tuple-element.136.pick_ref.refs_5_, bf16[2,768,1536]{2,1,0:T(8,128)(2,1)} %get-tuple-element.137.scaled_hbm, ...), custom_call_target="tpu_custom_call" | custom-call | flops 16911433728 | bytes 33690112 | tf_op jit(solution)/shard_map/select/pallas_call | solution.py:316
  241.2 2.0 collective-permute-start.31
  243.2 2.8 collective-permute-start.32
  246.0 2.2 collective-permute-done.31
  248.1 1.5 copy-done.25
  249.7 2.8 fusion.2
  252.5 2.7 collective-permute-start.33
  255.2 17.9 %finish.1 = (bf16[2,1536,768]{2,1,0:T(8,128)(2,1)}, f32[2,32,128]{2,1,0:T(8,128)}) custom-call(bf16[2,1536,1792]{2,1,0:T(8,128)(2,1)} %get-tuple-element.185.refs_0_, bf16[2,768,4096]{2,1,0:T(8,128)(2,1)} %refs_1_.3, f32[2,1536,768]{2,1,0:T(8,128)} %upstream.1.refs_2_, bf16[2,1536,768]{2,1,0:T(8,128)(2,1)} %get-tuple-element.186.refs_3_, ...), custom_call_target="tpu_custom_call" | custom-call | flops 132120576 | bytes 2359296 | tf_op jit(solution)/shard_map/finish/pallas_call | solution.py:422
  273.1 2.6 fusion
  277.1 5.3 %all-to-all-start.1 = ((f32[32,2,128]{2,1,0:T(2,128)}), f32[32,2,128]{2,1,0:T(2,128)S(1)}, u32[]{:S(2)}, u32[]{:S(2)}) async-start(f32[32,2,128]{2,1,0:T(2,128)} %copy.27), calls=%async_computation.1 | async-start | bytes 65536 | tf_op jit(solution)/shard_map/all_to_all | solution.py:636
  282.5 10.0 %in_slot_order.1 = bf16[1,2,1536,768]{3,2,1,0:T(8,128)(2,1)} custom-call(s32[64]{0:T(128)} %reshape.45.base_ref, s32[64]{0:T(128)} %reshape.46.lead_ref, s32[64]{0:T(128)} %convert_element_type.114.count_ref, bf16[2,1536,768]{2,1,0:T(8,128)(2,1)} %get-tuple-element.188.hidden_ref), custom_call_target="tpu_custom_call" | custom-call | flops 1000000000 | bytes 12000000 | tf_op jit(solution)/shard_map/in_slot_order/pallas_call | solution.py:465
  292.5 3.2 %collective-permute-done.33 = bf16[2,192,1792]{2,1,0:T(8,128)(2,1)} collective-permute-done((bf16[2,192,1792]{2,1,0:T(8,128)(2,1)}, bf16[2,192,1792]{2,1,0:T(8,128)(2,1)}, u32[]{:S(2)}, u32[]{:S(2)}) %collective-permute-start.33) | collective-permute-done | bytes 1376288 | tf_op jit(solution)/shard_map/ppermute | solution.py:612
  295.7 2.7 fusion.3
  (125 shorter events, 29.1 us)
Async XLA Ops:
  0.6 24.7 %collective-permute-start.1 = (bf16[128,4096]{1,0:T(8,128)(2,1)}, bf16[128,4096]{1,0:T(8,128)(2,1)S(1)}, u32[]{:S(2)}, u32[]{:S(2)}) collective-permute-start(bf16[128,4096]{1,0:T(8,128)(2,1)} %bitcast.39), channel_id=1, source_target_pairs={{0,16},{4,20},{8,24},{12,28},{16,0},{20,4},{24,8},{28,12},{32,48},... | collective-permute-start | bytes 3145736 | tf_op jit(solution)/shard_map/ppermute | solution.py:51
  5.0 40.6 %copy-start.28 = (bf16[1,128,8]{1,2,0:T(8,128)(2,1)S(1)}, bf16[1,128,8]{1,2,0:T(8,128)(2,1)}, u32[]{:S(2)}) copy-start(bf16[1,128,8]{1,2,0:T(8,128)(2,1)} %param.7) | copy-start | bytes 6148
  5.0 40.6 %copy-start.27 = (s32[1,128,8]{1,2,0:T(8,128)S(1)}, s32[1,128,8]{1,2,0:T(8,128)}, u32[]{:S(2)}) copy-start(s32[1,128,8]{1,2,0:T(8,128)} %param.8) | copy-start | bytes 12292
  5.0 15.2 %collective-permute-start = (bf16[128,2048]{1,0:T(8,128)(2,1)S(1)}, bf16[128,2048]{1,0:T(8,128)(2,1)S(1)}, u32[]{:S(2)}, u32[]{:S(2)}) collective-permute-start(bf16[128,2048]{1,0:T(8,128)(2,1)S(1)} %pad_maximum_fusion.refs_0_), channel_id=1, source_target_pairs={{0,32},{4,36},{8,40},{12,44},{16,48},{20,52},{24,56},{28,60},{32,6... | collective-permute-start | bytes 1572872 | tf_op jit(solution)/shard_map/ppermute | solution.py:51
  6.7 25.9 %collective-permute-start.3 = (bf16[128,2048]{1,0:T(8,128)(2,1)S(1)}, bf16[128,2048]{1,0:T(8,128)(2,1)S(1)}, u32[]{:S(2)}, u32[]{:S(2)}) collective-permute-start(bf16[128,2048]{1,0:T(8,128)(2,1)S(1)} %pad_maximum_fusion.refs_0_), channel_id=1, source_target_pairs={{0,96},{4,100},{8,104},{12,108},{16,112},{20,116},{24,120},{28,124... | collective-permute-start | bytes 1572872 | tf_op jit(solution)/shard_map/ppermute | solution.py:51
  9.0 20.8 %collective-permute-start.7 = (bf16[128,2048]{1,0:T(8,128)(2,1)S(1)}, bf16[128,2048]{1,0:T(8,128)(2,1)S(1)}, u32[]{:S(2)}, u32[]{:S(2)}) collective-permute-start(bf16[128,2048]{1,0:T(8,128)(2,1)S(1)} %pad_maximum_fusion.2.refs_8_), channel_id=1, source_target_pairs={{0,4},{4,8},{8,12},{12,0},{16,20},{20,24},{24,28},{28,16},{32,36},... | collective-permute-start | bytes 1572872 | tf_op jit(solution)/shard_map/ppermute | solution.py:51
  10.4 22.3 %collective-permute-start.9 = (bf16[128,2048]{1,0:T(8,128)(2,1)S(1)}, bf16[128,2048]{1,0:T(8,128)(2,1)S(1)}, u32[]{:S(2)}, u32[]{:S(2)}) collective-permute-start(bf16[128,2048]{1,0:T(8,128)(2,1)S(1)} %pad_maximum_fusion.2.refs_8_), channel_id=1, source_target_pairs={{0,12},{4,0},{8,4},{12,8},{16,28},{20,16},{24,20},{28,24},{32,44},... | collective-permute-start | bytes 1572872 | tf_op jit(solution)/shard_map/ppermute | solution.py:51
  20.2 13.1 %collective-permute-start.5 = (bf16[128,2048]{1,0:T(8,128)(2,1)S(1)}, bf16[128,2048]{1,0:T(8,128)(2,1)S(1)}, u32[]{:S(2)}, u32[]{:S(2)}) collective-permute-start(bf16[128,2048]{1,0:T(8,128)(2,1)S(1)} %collective-permute-done.refs_2_), channel_id=1, source_target_pairs={{0,32},{4,36},{8,40},{12,44},{16,48},{20,52},{24,56},{28,60},{32,6... | collective-permute-start | bytes 1572872 | tf_op jit(solution)/shard_map/ppermute | solution.py:51
  25.5 13.9 %collective-permute-start.4 = (bf16[128,2048]{1,0:T(8,128)(2,1)S(1)}, bf16[128,2048]{1,0:T(8,128)(2,1)S(1)}, u32[]{:S(2)}, u32[]{:S(2)}) collective-permute-start(bf16[128,2048]{1,0:T(8,128)(2,1)S(1)} %pad_maximum_fusion.1.refs_1_), channel_id=1, source_target_pairs={{0,96},{4,100},{8,104},{12,108},{16,112},{20,116},{24,120},{28,124... | collective-permute-start | bytes 1572872 | tf_op jit(solution)/shard_map/ppermute | solution.py:51
  29.8 29.9 %copy-start = (bf16[128,2048]{1,0:T(8,128)(2,1)}, bf16[128,2048]{1,0:T(8,128)(2,1)S(1)}, u32[]{:S(2)}) copy-start(bf16[128,2048]{1,0:T(8,128)(2,1)S(1)} %collective-permute-done.7.refs_10_) | copy-start | bytes 1572868
  29.8 13.0 %collective-permute-start.10 = (bf16[128,2048]{1,0:T(8,128)(2,1)S(1)}, bf16[128,2048]{1,0:T(8,128)(2,1)S(1)}, u32[]{:S(2)}, u32[]{:S(2)}) collective-permute-start(bf16[128,2048]{1,0:T(8,128)(2,1)S(1)} %pad_maximum_fusion.3.refs_9_), channel_id=1, source_target_pairs={{0,12},{4,0},{8,4},{12,8},{16,28},{20,16},{24,20},{28,24},{32,44},... | collective-permute-start | bytes 1572872 | tf_op jit(solution)/shard_map/ppermute | solution.py:51
  32.6 23.8 %collective-permute-start.11 = (bf16[128,2048]{1,0:T(8,128)(2,1)S(1)}, bf16[128,2048]{1,0:T(8,128)(2,1)S(1)}, u32[]{:S(2)}, u32[]{:S(2)}) collective-permute-start(bf16[128,2048]{1,0:T(8,128)(2,1)S(1)} %collective-permute-done.7.refs_10_), channel_id=1, source_target_pairs={{0,4},{4,8},{8,12},{12,0},{16,20},{20,24},{24,28},{28,16},{32,36},... | collective-permute-start | bytes 1572872 | tf_op jit(solution)/shard_map/ppermute | solution.py:51
  32.6 27.1 %copy-start.2 = (bf16[128,2048]{1,0:T(8,128)(2,1)}, bf16[128,2048]{1,0:T(8,128)(2,1)S(1)}, u32[]{:S(2)}) copy-start(bf16[128,2048]{1,0:T(8,128)(2,1)S(1)} %collective-permute-done.9.refs_12_) | copy-start | bytes 1572868
  32.7 23.8 %collective-permute-start.8 = (bf16[128,2048]{1,0:T(8,128)(2,1)S(1)}, bf16[128,2048]{1,0:T(8,128)(2,1)S(1)}, u32[]{:S(2)}, u32[]{:S(2)}) collective-permute-start(bf16[128,2048]{1,0:T(8,128)(2,1)S(1)} %pad_maximum_fusion.3.refs_9_), channel_id=1, source_target_pairs={{0,4},{4,8},{8,12},{12,0},{16,20},{20,24},{24,28},{28,16},{32,36},... | collective-permute-start | bytes 1572872 | tf_op jit(solution)/shard_map/ppermute | solution.py:51
  33.3 26.5 %copy-start.4 = (bf16[128,2048]{1,0:T(8,128)(2,1)}, bf16[128,2048]{1,0:T(8,128)(2,1)S(1)}, u32[]{:S(2)}) copy-start(bf16[128,2048]{1,0:T(8,128)(2,1)S(1)} %collective-permute-done.5.refs_6_) | copy-start | bytes 1572868
  33.3 23.2 %collective-permute-start.2 = (bf16[128,2048]{1,0:T(8,128)(2,1)S(1)}, bf16[128,2048]{1,0:T(8,128)(2,1)S(1)}, u32[]{:S(2)}, u32[]{:S(2)}) collective-permute-start(bf16[128,2048]{1,0:T(8,128)(2,1)S(1)} %pad_maximum_fusion.1.refs_1_), channel_id=1, source_target_pairs={{0,32},{4,36},{8,40},{12,44},{16,48},{20,52},{24,56},{28,60},{32,6... | collective-permute-start | bytes 1572872 | tf_op jit(solution)/shard_map/ppermute | solution.py:51
  39.4 20.4 %copy-start.6 = (bf16[128,2048]{1,0:T(8,128)(2,1)}, bf16[128,2048]{1,0:T(8,128)(2,1)S(1)}, u32[]{:S(2)}) copy-start(bf16[128,2048]{1,0:T(8,128)(2,1)S(1)} %collective-permute-done.4.refs_5_) | copy-start | bytes 1572868
  39.4 17.1 %collective-permute-start.6 = (bf16[128,2048]{1,0:T(8,128)(2,1)S(1)}, bf16[128,2048]{1,0:T(8,128)(2,1)S(1)}, u32[]{:S(2)}, u32[]{:S(2)}) collective-permute-start(bf16[128,2048]{1,0:T(8,128)(2,1)S(1)} %collective-permute-done.4.refs_5_), channel_id=1, source_target_pairs={{0,96},{4,100},{8,104},{12,108},{16,112},{20,116},{24,120},{28,124... | collective-permute-start | bytes 1572872 | tf_op jit(solution)/shard_map/ppermute | solution.py:51
  42.8 16.9 %copy-start.8 = (bf16[128,2048]{1,0:T(8,128)(2,1)}, bf16[128,2048]{1,0:T(8,128)(2,1)S(1)}, u32[]{:S(2)}) copy-start(bf16[128,2048]{1,0:T(8,128)(2,1)S(1)} %collective-permute-done.10.refs_13_) | copy-start | bytes 1572868
  42.8 13.7 %collective-permute-start.12 = (bf16[128,2048]{1,0:T(8,128)(2,1)S(1)}, bf16[128,2048]{1,0:T(8,128)(2,1)S(1)}, u32[]{:S(2)}, u32[]{:S(2)}) collective-permute-start(bf16[128,2048]{1,0:T(8,128)(2,1)S(1)} %collective-permute-done.10.refs_13_), channel_id=1, source_target_pairs={{0,12},{4,0},{8,4},{12,8},{16,28},{20,16},{24,20},{28,24},{32,44},... | collective-permute-start | bytes 1572872 | tf_op jit(solution)/shard_map/ppermute | solution.py:51
  56.5 3.3 %copy-start.10 = (bf16[128,2048]{1,0:T(8,128)(2,1)}, bf16[128,2048]{1,0:T(8,128)(2,1)S(1)}, u32[]{:S(2)}) copy-start(bf16[128,2048]{1,0:T(8,128)(2,1)S(1)} %collective-permute-done.11.refs_14_) | copy-start | bytes 1572868
  56.5 3.3 %copy-start.12 = (bf16[128,2048]{1,0:T(8,128)(2,1)}, bf16[128,2048]{1,0:T(8,128)(2,1)S(1)}, u32[]{:S(2)}) copy-start(bf16[128,2048]{1,0:T(8,128)(2,1)S(1)} %collective-permute-done.8.refs_11_) | copy-start | bytes 1572868
  56.5 3.3 %copy-start.14 = (bf16[128,2048]{1,0:T(8,128)(2,1)}, bf16[128,2048]{1,0:T(8,128)(2,1)S(1)}, u32[]{:S(2)}) copy-start(bf16[128,2048]{1,0:T(8,128)(2,1)S(1)} %collective-permute-done.2.refs_3_) | copy-start | bytes 1572868
  59.8 49.6 %collective-permute-start.16 = (bf16[1024,1152]{1,0:T(8,128)(2,1)}, bf16[1024,1152]{1,0:T(8,128)(2,1)}, u32[]{:S(2)}, u32[]{:S(2)}) collective-permute-start(bf16[1024,1152]{1,0:T(8,128)(2,1)} %get-tuple-element.153.refs_5_), channel_id=1, source_target_pairs={{0,96},{4,100},{8,104},{12,108},{16,112},{20,116},{24,120},{28,124... | collective-permute-start | bytes 7077896 | tf_op jit(solution)/shard_map/ppermute | solution.py:51
  62.0 50.6 %collective-permute-start.15 = (bf16[1024,1152]{1,0:T(8,128)(2,1)}, bf16[1024,1152]{1,0:T(8,128)(2,1)}, u32[]{:S(2)}, u32[]{:S(2)}) collective-permute-start(bf16[1024,1152]{1,0:T(8,128)(2,1)} %get-tuple-element.153.refs_5_), channel_id=1, source_target_pairs={{0,32},{4,36},{8,40},{12,44},{16,48},{20,52},{24,56},{28,60},{32,6... | collective-permute-start | bytes 7077896 | tf_op jit(solution)/shard_map/ppermute | solution.py:51
  62.0 50.6 %collective-permute-start.14 = (bf16[1024,1152]{1,0:T(8,128)(2,1)}, bf16[1024,1152]{1,0:T(8,128)(2,1)}, u32[]{:S(2)}, u32[]{:S(2)}) collective-permute-start(bf16[1024,1152]{1,0:T(8,128)(2,1)} %get-tuple-element.142.refs_0_), channel_id=1, source_target_pairs={{0,12},{4,0},{8,4},{12,8},{16,28},{20,16},{24,20},{28,24},{32,44},... | collective-permute-start | bytes 7077896 | tf_op jit(solution)/shard_map/ppermute | solution.py:51
  63.1 49.7 %collective-permute-start.13 = (bf16[1024,1152]{1,0:T(8,128)(2,1)}, bf16[1024,1152]{1,0:T(8,128)(2,1)}, u32[]{:S(2)}, u32[]{:S(2)}) collective-permute-start(bf16[1024,1152]{1,0:T(8,128)(2,1)} %get-tuple-element.142.refs_0_), channel_id=1, source_target_pairs={{0,4},{4,8},{8,12},{12,0},{16,20},{20,24},{24,28},{28,16},{32,36},... | collective-permute-start | bytes 7077896 | tf_op jit(solution)/shard_map/ppermute | solution.py:51
  109.5 32.6 %copy-start.21 = (bf16[1024,896]{1,0:T(8,128)(2,1)S(1)}, bf16[1024,896]{1,0:T(8,128)(2,1)}, u32[]{:S(2)}) copy-start(bf16[1024,896]{1,0:T(8,128)(2,1)} %copy-done.20) | copy-start | bytes 5505028
  116.7 22.4 %collective-permute-start.20 = (bf16[512,1152]{1,0:T(8,128)(2,1)}, bf16[512,1152]{1,0:T(8,128)(2,1)S(1)}, u32[]{:S(2)}, u32[]{:S(2)}) collective-permute-start(bf16[512,1152]{1,0:T(8,128)(2,1)} %get-tuple-element.158), channel_id=1, source_target_pairs={{0,96},{4,100},{8,104},{12,108},{16,112},{20,116},{24,120},{28,124... | collective-permute-start | bytes 3538952 | tf_op jit(solution)/shard_map/ppermute | solution.py:51
  119.1 22.9 %collective-permute-start.19 = (bf16[512,1152]{1,0:T(8,128)(2,1)}, bf16[512,1152]{1,0:T(8,128)(2,1)}, u32[]{:S(2)}, u32[]{:S(2)}) collective-permute-start(bf16[512,1152]{1,0:T(8,128)(2,1)} %get-tuple-element.156), channel_id=1, source_target_pairs={{0,32},{4,36},{8,40},{12,44},{16,48},{20,52},{24,56},{28,60},{32,6... | collective-permute-start | bytes 3538952 | tf_op jit(solution)/shard_map/ppermute | solution.py:51
  119.1 23.5 %collective-permute-start.18 = (bf16[512,1152]{1,0:T(8,128)(2,1)}, bf16[512,1152]{1,0:T(8,128)(2,1)}, u32[]{:S(2)}, u32[]{:S(2)}) collective-permute-start(bf16[512,1152]{1,0:T(8,128)(2,1)} %get-tuple-element.151), channel_id=1, source_target_pairs={{0,12},{4,0},{8,4},{12,8},{16,28},{20,16},{24,20},{28,24},{32,44},... | collective-permute-start | bytes 3538952 | tf_op jit(solution)/shard_map/ppermute | solution.py:51
  119.4 24.1 %collective-permute-start.17 = (bf16[512,1152]{1,0:T(8,128)(2,1)}, bf16[512,1152]{1,0:T(8,128)(2,1)}, u32[]{:S(2)}, u32[]{:S(2)}) collective-permute-start(bf16[512,1152]{1,0:T(8,128)(2,1)} %get-tuple-element.149), channel_id=1, source_target_pairs={{0,4},{4,8},{8,12},{12,0},{16,20},{20,24},{24,28},{28,16},{32,36},... | collective-permute-start | bytes 3538952 | tf_op jit(solution)/shard_map/ppermute | solution.py:51
  121.9 56.5 %collective-permute-start.24 = (bf16[1024,896]{1,0:T(8,128)(2,1)}, bf16[1024,896]{1,0:T(8,128)(2,1)}, u32[]{:S(2)}, u32[]{:S(2)}) collective-permute-start(bf16[1024,896]{1,0:T(8,128)(2,1)} %copy-done.22), channel_id=1, source_target_pairs={{0,96},{4,100},{8,104},{12,108},{16,112},{20,116},{24,120},{28,124... | collective-permute-start | bytes 5505032 | tf_op jit(solution)/shard_map/ppermute | solution.py:51
  139.0 4.5 %copy-start.29 = (bf16[512,1152]{1,0:T(8,128)(2,1)}, bf16[512,1152]{1,0:T(8,128)(2,1)S(1)}, u32[]{:S(2)}) copy-start(bf16[512,1152]{1,0:T(8,128)(2,1)S(1)} %collective-permute-done.20.refs_9_) | copy-start | bytes 3538948
  139.0 40.5 %collective-permute-start.23 = (bf16[1024,896]{1,0:T(8,128)(2,1)}, bf16[1024,896]{1,0:T(8,128)(2,1)}, u32[]{:S(2)}, u32[]{:S(2)}) collective-permute-start(bf16[1024,896]{1,0:T(8,128)(2,1)} %copy-done.22), channel_id=1, source_target_pairs={{0,32},{4,36},{8,40},{12,44},{16,48},{20,52},{24,56},{28,60},{32,6... | collective-permute-start | bytes 5505032 | tf_op jit(solution)/shard_map/ppermute | solution.py:51
  142.1 37.5 %collective-permute-start.22 = (bf16[1024,896]{1,0:T(8,128)(2,1)S(1)}, bf16[1024,896]{1,0:T(8,128)(2,1)}, u32[]{:S(2)}, u32[]{:S(2)}) collective-permute-start(bf16[1024,896]{1,0:T(8,128)(2,1)S(1)} %copy-done.21), channel_id=1, source_target_pairs={{0,12},{4,0},{8,4},{12,8},{16,28},{20,16},{24,20},{28,24},{32,44},... | collective-permute-start | bytes 5505032 | tf_op jit(solution)/shard_map/ppermute | solution.py:51
  142.6 36.9 %collective-permute-start.21 = (bf16[1024,896]{1,0:T(8,128)(2,1)S(1)}, bf16[1024,896]{1,0:T(8,128)(2,1)}, u32[]{:S(2)}, u32[]{:S(2)}) collective-permute-start(bf16[1024,896]{1,0:T(8,128)(2,1)S(1)} %copy-done.21), channel_id=1, source_target_pairs={{0,4},{4,8},{8,12},{12,0},{16,20},{20,24},{24,28},{28,16},{32,36},... | collective-permute-start | bytes 5505032 | tf_op jit(solution)/shard_map/ppermute | solution.py:51
  179.6 16.4 %copy-start.23 = (bf16[2,2,192,2304]{3,2,1,0:T(8,128)(2,1)S(1)}, bf16[2,2,192,2304]{3,2,1,0:T(8,128)(2,1)}, u32[]{:S(2)}) copy-start(bf16[2,2,192,2304]{3,2,1,0:T(8,128)(2,1)} %get-tuple-element.163) | copy-start | bytes 10616836
  179.6 16.4 %collective-permute-start.25 = (bf16[2,2,192,2304]{3,2,1,0:T(8,128)(2,1)}, bf16[2,2,192,2304]{3,2,1,0:T(8,128)(2,1)}, u32[]{:S(2)}, u32[]{:S(2)}) collective-permute-start(bf16[2,2,192,2304]{3,2,1,0:T(8,128)(2,1)} %get-tuple-element.162), channel_id=1, source_target_pairs={{0,1},{1,0},{2,3},{3,2},{4,5},{5,4},{6,7},{7,6},{8,9},{9,8},{10,11... | collective-permute-start | bytes 10616840 | tf_op jit(solution)/shard_map/ppermute | solution.py:602
  191.7 27.8 %collective-permute-start.30 = (bf16[512,896]{1,0:T(8,128)(2,1)}, bf16[512,896]{1,0:T(8,128)(2,1)}, u32[]{:S(2)}, u32[]{:S(2)}) collective-permute-start(bf16[512,896]{1,0:T(8,128)(2,1)} %get-tuple-element.180), channel_id=1, source_target_pairs={{0,96},{4,100},{8,104},{12,108},{16,112},{20,116},{24,120},{28,124... | collective-permute-start | bytes 2752520 | tf_op jit(solution)/shard_map/ppermute | solution.py:51
  194.5 26.5 %collective-permute-start.29 = (bf16[512,896]{1,0:T(8,128)(2,1)}, bf16[512,896]{1,0:T(8,128)(2,1)}, u32[]{:S(2)}, u32[]{:S(2)}) collective-permute-start(bf16[512,896]{1,0:T(8,128)(2,1)} %get-tuple-element.178), channel_id=1, source_target_pairs={{0,32},{4,36},{8,40},{12,44},{16,48},{20,52},{24,56},{28,60},{32,6... | collective-permute-start | bytes 2752520 | tf_op jit(solution)/shard_map/ppermute | solution.py:51
  194.5 26.5 %collective-permute-start.28 = (bf16[512,896]{1,0:T(8,128)(2,1)}, bf16[512,896]{1,0:T(8,128)(2,1)}, u32[]{:S(2)}, u32[]{:S(2)}) collective-permute-start(bf16[512,896]{1,0:T(8,128)(2,1)} %get-tuple-element.173), channel_id=1, source_target_pairs={{0,12},{4,0},{8,4},{12,8},{16,28},{20,16},{24,20},{28,24},{32,44},... | collective-permute-start | bytes 2752520 | tf_op jit(solution)/shard_map/ppermute | solution.py:51
  194.5 26.5 %collective-permute-start.27 = (bf16[512,896]{1,0:T(8,128)(2,1)}, bf16[512,896]{1,0:T(8,128)(2,1)}, u32[]{:S(2)}, u32[]{:S(2)}) collective-permute-start(bf16[512,896]{1,0:T(8,128)(2,1)} %get-tuple-element.171), channel_id=1, source_target_pairs={{0,4},{4,8},{8,12},{12,0},{16,20},{20,24},{24,28},{28,16},{32,36},... | collective-permute-start | bytes 2752520 | tf_op jit(solution)/shard_map/ppermute | solution.py:51
  199.0 21.9 %collective-permute-start.26 = (bf16[2,192,1152]{2,1,0:T(8,128)(2,1)}, bf16[2,192,1152]{2,1,0:T(8,128)(2,1)}, u32[]{:S(2)}, u32[]{:S(2)}) collective-permute-start(bf16[2,192,1152]{2,1,0:T(8,128)(2,1)} %get-tuple-element.197), channel_id=1, source_target_pairs={{0,2},{2,0},{1,3},{3,1},{4,6},{6,4},{5,7},{7,5},{8,10},{10,8},{9,1... | collective-permute-start | bytes 2654216 | tf_op jit(solution)/shard_map/ppermute | solution.py:612
  241.2 7.0 %collective-permute-start.31 = (bf16[2,2,192,1792]{3,2,1,0:T(8,128)(2,1)}, bf16[2,2,192,1792]{3,2,1,0:T(8,128)(2,1)S(1)}, u32[]{:S(2)}, u32[]{:S(2)}) collective-permute-start(bf16[2,2,192,1792]{3,2,1,0:T(8,128)(2,1)} %get-tuple-element.183), channel_id=1, source_target_pairs={{0,1},{1,0},{2,3},{3,2},{4,5},{5,4},{6,7},{7,6},{8,9},{9,8},{10,11... | collective-permute-start | bytes 8257544 | tf_op jit(solution)/shard_map/ppermute | solution.py:602
  243.2 29.9 %collective-permute-start.32 = (bf16[2,192,1152]{2,1,0:T(8,128)(2,1)}, bf16[2,192,1152]{2,1,0:T(8,128)(2,1)}, u32[]{:S(2)}, u32[]{:S(2)}) collective-permute-start(bf16[2,192,1152]{2,1,0:T(8,128)(2,1)} %get-tuple-element.191), channel_id=1, source_target_pairs={{0,2},{2,0},{1,3},{3,1},{4,6},{6,4},{5,7},{7,5},{8,10},{10,8},{9,1... | collective-permute-start | bytes 2654216 | tf_op jit(solution)/shard_map/ppermute | solution.py:612
  252.5 43.2 %collective-permute-start.33 = (bf16[2,192,1792]{2,1,0:T(8,128)(2,1)}, bf16[2,192,1792]{2,1,0:T(8,128)(2,1)}, u32[]{:S(2)}, u32[]{:S(2)}) collective-permute-start(bf16[2,192,1792]{2,1,0:T(8,128)(2,1)} %fusion.2), channel_id=1, source_target_pairs={{0,2},{2,0},{1,3},{3,1},{4,6},{6,4},{5,7},{7,5},{8,10},{10,8},{9,1... | collective-permute-start | bytes 4128776 | tf_op jit(solution)/shard_map/ppermute | solution.py:612
  277.1 21.8 %all-to-all-start.1 = ((f32[32,2,128]{2,1,0:T(2,128)}), f32[32,2,128]{2,1,0:T(2,128)S(1)}, u32[]{:S(2)}, u32[]{:S(2)}) async-start(f32[32,2,128]{2,1,0:T(2,128)} %copy.27), calls=%async_computation.1 | async-start | bytes 65536 | tf_op jit(solution)/shard_map/all_to_all | solution.py:636
  (17 other events, 23.5 us)
